TPU v7x, 32 devices: a whole 2x2x4 slice. The times are simulated.
32 devices in a mesh: seq: 32 (over z, y, x, core).
Axes of the slice: x: 2, y: 2, z: 4, core: 2. Of those that a mesh axis runs over, the one named last changes fastest.
Arguments:
- tokens: bfloat16 [8192, 1024], P('seq'), may hold values from -6 to 6
- w_in: bfloat16 [1024, 4096], replicated, may hold values from -0.1875 to 0.1875
- w_out: bfloat16 [1024, 1024], replicated, may hold values from -0.1875 to 0.1875
- block_counts: int32 [16], replicated, may hold values from 1 to 16, 64 in all
- tails: int32 [16], replicated, may hold values from 1 to 128
- grad_out: bfloat16 [8192, 1024], P('seq'), may hold values from -6 to 6
Outputs:
- layer_out: bfloat16 [8192, 1024], P('seq')
- grad_tokens: bfloat16 [8192, 1024], P('seq')
- grad_w_in: float32 [4096, 1024], P('seq')
Inputs may be any that keep to these rules, and one draw needn't show every extreme that they name: `block_counts`: the block counts sum to 64; one user has exactly 16 blocks.
All inputs are finite; a program needn't handle non-finite values.
Results may differ from a plain program's by a relative error of at most 0.013.
Values may be sent and summed in bfloat16 or wider, within the bound.
No kernel may reach another device: no remote copies, remote signals or barrier semaphores. Data moves between devices by JAX's collectives and lax.ppermute only.
A program may use at most 192 MiB of HBM per device.

v0:
```python
import jax
import jax.numpy as jnp
from jax import lax
from jax.sharding import PartitionSpec as P

HEADS = 8
HD = 128
BLK = 128
MAXB = 16


eps = 1e-05


def from_behind(value, axis, steps):
    count = lax.axis_size(axis)
    first, last = (max(0, -steps), min(count, count - steps))
    return lax.ppermute(value, axis, [(source, source + steps) for source in range(first, last)])


def row_info(rows, counts, tails, block_rows):
    ends = jnp.cumsum(counts) * block_rows
    starts = ends - counts * block_rows
    lengths = (counts - 1) * block_rows + tails
    user = jnp.sum((rows[:, None] >= ends[None, :]).astype(jnp.int32), axis=1)
    pick = user[:, None] == jnp.arange(counts.shape[0], dtype=jnp.int32)[None, :]
    start = jnp.sum(jnp.where(pick, starts[None, :], 0), axis=1)
    length = jnp.sum(jnp.where(pick, lengths[None, :], 0), axis=1)
    valid = (rows >= 0) & (rows - start < length)
    return (user, rows, valid)


def attend(query, keys, values, qinfo, kinfo):
    q_user, q_rows, q_ok = qinfo
    k_user, k_rows, k_ok = kinfo
    qh = query.reshape(query.shape[0], HEADS, HD)
    kh = keys.reshape(keys.shape[0], HEADS, HD)
    vh = values.reshape(values.shape[0], HEADS, HD)
    scores = jnp.einsum("qhd,khd->hqk", qh, kh, preferred_element_type=jnp.float32)
    weights = jax.nn.silu(scores * HD ** (-0.5)) / (MAXB * BLK)
    visible = (q_user[:, None] == k_user[None, :]) & (k_rows[None, :] <= q_rows[:, None])
    visible = visible & q_ok[:, None] & k_ok[None, :]
    weights = jnp.where(visible[None], weights, 0.0).astype(jnp.bfloat16)
    out = jnp.einsum("hqk,khd->qhd", weights, vh, preferred_element_type=jnp.float32)
    return out.reshape(query.shape[0], HEADS * HD)


def stem_norm(xf):
    return xf * lax.rsqrt(jnp.mean(xf * xf, axis=-1, keepdims=True) + eps)


def split_parts(pre):
    width = pre.shape[1] // 4
    hidden = jax.nn.silu(pre)
    return tuple((hidden[:, i * width : (i + 1) * width].astype(jnp.bfloat16) for i in range(4)))


def per_device(tokens, w_in, w_out, block_counts, tails, grad_out):
    count = tokens.shape[0]
    reach = MAXB * BLK // count
    me = lax.axis_index("seq")
    local = jnp.arange(count, dtype=jnp.int32)

    def info_at(offset):
        return row_info((me + offset) * count + local, block_counts, tails, BLK)

    own = info_at(0)
    xf = tokens.astype(jnp.float32)
    normed_f, norm_back = jax.vjp(stem_norm, xf)
    normed = normed_f.astype(jnp.bfloat16)
    pre = jnp.dot(normed, w_in, preferred_element_type=jnp.float32)
    parts, split_back = jax.vjp(split_parts, pre)
    u, v, q, k = parts
    own_kv = jnp.stack([k, v])
    attn = attend(q, k, v, own, own)
    kept = []
    moving = own_kv
    for step in range(1, reach + 1):
        moving = from_behind(moving, "seq", 1)
        kept.append(moving)
        attn = attn + attend(q, moving[0], moving[1], own, info_at(-step))

    def tail_fn(attn, u, xf):
        normed_attn = attn * lax.rsqrt(jnp.mean(attn * attn, axis=-1, keepdims=True) + eps)
        gated = (normed_attn * u).astype(jnp.bfloat16)
        return xf + jnp.dot(gated, w_out, preferred_element_type=jnp.float32)

    out_f, tail_back = jax.vjp(tail_fn, attn, u, xf)
    layer_out = out_f.astype(jnp.bfloat16)
    d_attn, d_u, d_xf = tail_back(grad_out.astype(jnp.float32))
    _, local_back = jax.vjp(lambda qq, kk, vv: attend(qq, kk, vv, own, own), q, k, v)
    dq0, dk0, dv0 = local_back(d_attn)
    d_q = dq0.astype(jnp.float32)
    d_k = dk0.astype(jnp.float32)
    d_v = dv0.astype(jnp.float32)
    far_q = q
    far_grad = d_attn
    for step in range(1, reach + 1):
        earlier = kept[step - 1]
        kinfo = info_at(-step)
        _, q_back = jax.vjp(lambda qq: attend(qq, earlier[0], earlier[1], own, kinfo), q)
        d_q = d_q + q_back(d_attn)[0].astype(jnp.float32)
        far_q = from_behind(far_q, "seq", -1)
        far_grad = from_behind(far_grad.astype(jnp.bfloat16), "seq", -1).astype(far_grad.dtype)
        qinfo = info_at(step)
        _, kv_back = jax.vjp(lambda kk, vv: attend(far_q, kk, vv, qinfo, own), k, v)
        dk_far, dv_far = kv_back(far_grad)
        d_k = d_k + dk_far.astype(jnp.float32)
        d_v = d_v + dv_far.astype(jnp.float32)
    d_pre = split_back(
        (d_u, d_v.astype(jnp.bfloat16), d_q.astype(jnp.bfloat16), d_k.astype(jnp.bfloat16))
    )[0]
    d_pre_b = d_pre.astype(jnp.bfloat16)
    grad_w_in = lax.psum_scatter(
        lax.dot_general(
            d_pre_b, normed, (((0,), (0,)), ((), ())), preferred_element_type=jnp.float32
        ),
        "seq",
        scatter_dimension=0,
        tiled=True,
    )
    d_normed = lax.dot_general(
        d_pre_b, w_in, (((1,), (1,)), ((), ())), preferred_element_type=jnp.float32
    )
    grad_tokens = (d_xf + norm_back(d_normed)[0]).astype(jnp.bfloat16)
    return (layer_out, grad_tokens, grad_w_in)


def solution(mesh):
    in_specs = (P("seq", None), P(), P(), P(), P(), P("seq", None))
    out_specs = (P("seq", None), P("seq", None), P("seq", None))
    return jax.shard_map(
        per_device, mesh=mesh, in_specs=in_specs, out_specs=out_specs, check_vma=False
    )
```

profile of v0, /device:TPU:0, one launch (start us, length us, event | category | flops | bytes accessed | tf_op | source)
XLA Modules:
  0.0 618.7 jit_solution(18290374983823933766)
XLA Ops:
  8.6 8.0 %multiply_convert_fusion = (bf16[256,4096]{1,0:T(8,128)(2,1)S(1)}, f32[256,4096]{1,0:T(8,128)}) fusion(bf16[1024,4096]{1,0:T(8,128)(2,1)} %param.7, bf16[256,1024]{1,0:T(8,128)(2,1)} %param.6, f32[256]{0:T(256)S(1)} %fusion.579), kind=kOutput, calls=%fused_computation.4 | convolution fusion | flops 2153512960 | bytes 15205376 | tf_op jit(solution)/shard_map/dot_general | solution.py:71
  45.8 9.2 %collective-permute-start.1 = (bf16[2,256,1024]{2,1,0:T(8,128)(2,1)}, bf16[2,256,1024]{2,1,0:T(8,128)(2,1)}, u32[]{:S(2)}, u32[]{:S(2)}) collective-permute-start(bf16[2,256,1024]{2,1,0:T(8,128)(2,1)} %collective-permute-done), channel_id=1, source_target_pairs={{0,1},{1,2},{2,3},{3,4},{4,5},{5,6},{6,7},{7,8},{8,9},{9,10},{10,1... | collective-permute-start | bytes 3145736 | tf_op jit(solution)/shard_map/ppermute | solution.py:18
  77.0 13.9 %collective-permute-start.2 = (bf16[2,256,1024]{2,1,0:T(8,128)(2,1)}, bf16[2,256,1024]{2,1,0:T(8,128)(2,1)}, u32[]{:S(2)}, u32[]{:S(2)}) collective-permute-start(bf16[2,256,1024]{2,1,0:T(8,128)(2,1)} %collective-permute-done.1), channel_id=1, source_target_pairs={{0,1},{1,2},{2,3},{3,4},{4,5},{5,6},{6,7},{7,8},{8,9},{9,10},{10,1... | collective-permute-start | bytes 3145736 | tf_op jit(solution)/shard_map/ppermute | solution.py:18
  114.2 10.4 %collective-permute-start.3 = (bf16[2,256,1024]{2,1,0:T(8,128)(2,1)}, bf16[2,256,1024]{2,1,0:T(8,128)(2,1)}, u32[]{:S(2)}, u32[]{:S(2)}) collective-permute-start(bf16[2,256,1024]{2,1,0:T(8,128)(2,1)} %collective-permute-done.2), channel_id=1, source_target_pairs={{0,1},{1,2},{2,3},{3,4},{4,5},{5,6},{6,7},{7,8},{8,9},{9,10},{10,1... | collective-permute-start | bytes 3145736 | tf_op jit(solution)/shard_map/ppermute | solution.py:18
  146.7 12.1 %collective-permute-start.4 = (bf16[2,256,1024]{2,1,0:T(8,128)(2,1)}, bf16[2,256,1024]{2,1,0:T(8,128)(2,1)}, u32[]{:S(2)}, u32[]{:S(2)}) collective-permute-start(bf16[2,256,1024]{2,1,0:T(8,128)(2,1)} %collective-permute-done.3), channel_id=1, source_target_pairs={{0,1},{1,2},{2,3},{3,4},{4,5},{5,6},{6,7},{7,8},{8,9},{9,10},{10,1... | collective-permute-start | bytes 3145736 | tf_op jit(solution)/shard_map/ppermute | solution.py:18
  166.9 7.6 %collective-permute-start.5 = (bf16[2,256,1024]{2,1,0:T(8,128)(2,1)}, bf16[2,256,1024]{2,1,0:T(8,128)(2,1)}, u32[]{:S(2)}, u32[]{:S(2)}) collective-permute-start(bf16[2,256,1024]{2,1,0:T(8,128)(2,1)} %collective-permute-done.4), channel_id=1, source_target_pairs={{0,1},{1,2},{2,3},{3,4},{4,5},{5,6},{6,7},{7,8},{8,9},{9,10},{10,1... | collective-permute-start | bytes 3145736 | tf_op jit(solution)/shard_map/ppermute | solution.py:18
  183.6 7.3 %collective-permute-start.6 = (bf16[2,256,1024]{2,1,0:T(8,128)(2,1)}, bf16[2,256,1024]{2,1,0:T(8,128)(2,1)}, u32[]{:S(2)}, u32[]{:S(2)}) collective-permute-start(bf16[2,256,1024]{2,1,0:T(8,128)(2,1)} %collective-permute-done.5), channel_id=1, source_target_pairs={{0,1},{1,2},{2,3},{3,4},{4,5},{5,6},{6,7},{7,8},{8,9},{9,10},{10,1... | collective-permute-start | bytes 3145736 | tf_op jit(solution)/shard_map/ppermute | solution.py:18
  200.1 7.2 %collective-permute-start.7 = (bf16[2,256,1024]{2,1,0:T(8,128)(2,1)}, bf16[2,256,1024]{2,1,0:T(8,128)(2,1)}, u32[]{:S(2)}, u32[]{:S(2)}) collective-permute-start(bf16[2,256,1024]{2,1,0:T(8,128)(2,1)} %collective-permute-done.6), channel_id=1, source_target_pairs={{0,1},{1,2},{2,3},{3,4},{4,5},{5,6},{6,7},{7,8},{8,9},{9,10},{10,1... | collective-permute-start | bytes 3145736 | tf_op jit(solution)/shard_map/ppermute | solution.py:18
  234.7 10.0 %collective-permute-start.8 = (bf16[256,1024]{1,0:T(8,128)(2,1)}, bf16[256,1024]{1,0:T(8,128)(2,1)}, u32[]{:S(2)}, u32[]{:S(2)}) collective-permute-start(bf16[256,1024]{1,0:T(8,128)(2,1)} %add_add_fusion.1), channel_id=1, source_target_pairs={{1,0},{2,1},{3,2},{4,3},{5,4},{6,5},{7,6},{8,7},{9,8},{10,9},{11,1... | collective-permute-start | bytes 1572872 | tf_op jit(solution)/shard_map/ppermute | solution.py:18
  250.5 5.0 fusion.255
  255.5 4.8 fusion.246
  260.3 4.8 fusion.237
  265.1 4.8 fusion.228
  269.8 4.8 fusion.219
  274.6 4.8 fusion.210
  279.3 5.0 fusion.201
  284.4 4.6 fusion.192
  296.2 4.6 fusion.330
  302.0 3.8 fusion.349
  307.2 4.5 fusion.321
  312.8 3.8 fusion.347
  317.9 4.4 fusion.312
  329.1 4.5 fusion.303
  334.7 3.8 fusion.343
  339.8 4.5 fusion.294
  345.4 3.8 fusion.341
  351.2 4.4 fusion.285
  362.7 4.5 fusion.276
  372.6 4.3 fusion.267
  390.5 8.2 %fusion.575 = f32[4096,1024]{1,0:T(8,128)} fusion(bf16[256,4096]{1,0:T(8,128)(2,1)S(1)} %fusion.2, bf16[256,1024]{1,0:T(8,128)(2,1)S(1)} %copy-done.3, f32[256]{0:T(256)S(1)} %copy-done.59), kind=kOutput, calls=%fused_computation.573 | convolution fusion | flops 2148270080 | bytes 19399680 | tf_op jit(solution)/shard_map/dot_general | solution.py:115
  402.9 5.9 fusion.359
  409.9 201.8 %reduce-scatter.2.cloned.1.call-done = f32[128,1024]{1,0:T(8,128)} async-done(((f32[4096,1024]{1,0:T(8,128)}), f32[128,1024]{1,0:T(8,128)}) %reduce-scatter.2.cloned.1.call-update) | async-done | bytes 524304 | tf_op jit(solution)/shard_map/reduce_scatter | solution.py:114
  (313 shorter events, 212.3 us)
Async XLA Ops:
  7.2 220.0 %copy-start = (bf16[1024,1024]{1,0:T(8,128)(2,1)S(1)}, bf16[1024,1024]{1,0:T(8,128)(2,1)}, u32[]{:S(2)}) copy-start(bf16[1024,1024]{1,0:T(8,128)(2,1)} %param.8) | copy-start | bytes 6291460
  7.2 604.5 %reduce-scatter.2.cloned.1.call-start = ((), (), s32[]{:S(2)}) async-start(), calls=%async_computation.1 | async-start | bytes 17301504 | tf_op jit(solution)/shard_map/reduce_scatter | solution.py:114
  8.6 8.0 %copy-start.60 = (f32[256]{0:T(256)}, f32[256]{0:T(256)S(1)}, u32[]{:S(2)}) copy-start(f32[256]{0:T(256)S(1)} %fusion.357) | copy-start | bytes 3076
  8.6 8.0 %copy-start.58 = (f32[256]{0:T(256)}, f32[256]{0:T(256)S(1)}, u32[]{:S(2)}) copy-start(f32[256]{0:T(256)S(1)} %fusion.579) | copy-start | bytes 3076
  18.5 8.6 %copy-start.63 = (s32[16]{0:T(128)S(1)}, s32[16]{0:T(128)}, u32[]{:S(2)}) copy-start(s32[16]{0:T(128)} %param.10) | copy-start | bytes 196
  19.5 22.0 %collective-permute-start = (bf16[2,256,1024]{2,1,0:T(8,128)(2,1)}, bf16[2,256,1024]{2,1,0:T(8,128)(2,1)}, u32[]{:S(2)}, u32[]{:S(2)}) collective-permute-start(bf16[2,256,1024]{2,1,0:T(8,128)(2,1)} %pad_maximum_fusion), channel_id=1, source_target_pairs={{0,1},{1,2},{2,3},{3,4},{4,5},{5,6},{6,7},{7,8},{8,9},{9,10},{10,1... | collective-permute-start | bytes 3145736 | tf_op jit(solution)/shard_map/ppermute | solution.py:18
  22.9 12.5 %collective-permute-start.9 = (bf16[256,1024]{1,0:T(8,128)(2,1)}, bf16[256,1024]{1,0:T(8,128)(2,1)}, u32[]{:S(2)}, u32[]{:S(2)}) collective-permute-start(bf16[256,1024]{1,0:T(8,128)(2,1)} %get-tuple-element.329), channel_id=1, source_target_pairs={{1,0},{2,1},{3,2},{4,3},{5,4},{6,5},{7,6},{8,7},{9,8},{10,9},{11,1... | collective-permute-start | bytes 1572872 | tf_op jit(solution)/shard_map/ppermute | solution.py:18
  37.4 20.6 %collective-permute-start.11 = (bf16[256,1024]{1,0:T(8,128)(2,1)}, bf16[256,1024]{1,0:T(8,128)(2,1)}, u32[]{:S(2)}, u32[]{:S(2)}) collective-permute-start(bf16[256,1024]{1,0:T(8,128)(2,1)} %collective-permute-done.9), channel_id=1, source_target_pairs={{1,0},{2,1},{3,2},{4,3},{5,4},{6,5},{7,6},{8,7},{9,8},{10,9},{11,1... | collective-permute-start | bytes 1572872 | tf_op jit(solution)/shard_map/ppermute | solution.py:18
  45.8 26.9 %collective-permute-start.1 = (bf16[2,256,1024]{2,1,0:T(8,128)(2,1)}, bf16[2,256,1024]{2,1,0:T(8,128)(2,1)}, u32[]{:S(2)}, u32[]{:S(2)}) collective-permute-start(bf16[2,256,1024]{2,1,0:T(8,128)(2,1)} %collective-permute-done), channel_id=1, source_target_pairs={{0,1},{1,2},{2,3},{3,4},{4,5},{5,6},{6,7},{7,8},{8,9},{9,10},{10,1... | collective-permute-start | bytes 3145736 | tf_op jit(solution)/shard_map/ppermute | solution.py:18
  60.0 6.5 %collective-permute-start.13 = (bf16[256,1024]{1,0:T(8,128)(2,1)}, bf16[256,1024]{1,0:T(8,128)(2,1)}, u32[]{:S(2)}, u32[]{:S(2)}) collective-permute-start(bf16[256,1024]{1,0:T(8,128)(2,1)} %collective-permute-done.11), channel_id=1, source_target_pairs={{1,0},{2,1},{3,2},{4,3},{5,4},{6,5},{7,6},{8,7},{9,8},{10,9},{11,1... | collective-permute-start | bytes 1572872 | tf_op jit(solution)/shard_map/ppermute | solution.py:18
  68.6 25.1 %collective-permute-start.15 = (bf16[256,1024]{1,0:T(8,128)(2,1)}, bf16[256,1024]{1,0:T(8,128)(2,1)}, u32[]{:S(2)}, u32[]{:S(2)}) collective-permute-start(bf16[256,1024]{1,0:T(8,128)(2,1)} %collective-permute-done.13), channel_id=1, source_target_pairs={{1,0},{2,1},{3,2},{4,3},{5,4},{6,5},{7,6},{8,7},{9,8},{10,9},{11,1... | collective-permute-start | bytes 1572872 | tf_op jit(solution)/shard_map/ppermute | solution.py:18
  77.0 31.7 %collective-permute-start.2 = (bf16[2,256,1024]{2,1,0:T(8,128)(2,1)}, bf16[2,256,1024]{2,1,0:T(8,128)(2,1)}, u32[]{:S(2)}, u32[]{:S(2)}) collective-permute-start(bf16[2,256,1024]{2,1,0:T(8,128)(2,1)} %collective-permute-done.1), channel_id=1, source_target_pairs={{0,1},{1,2},{2,3},{3,4},{4,5},{5,6},{6,7},{7,8},{8,9},{9,10},{10,1... | collective-permute-start | bytes 3145736 | tf_op jit(solution)/shard_map/ppermute | solution.py:18
  95.7 6.7 %collective-permute-start.17 = (bf16[256,1024]{1,0:T(8,128)(2,1)}, bf16[256,1024]{1,0:T(8,128)(2,1)}, u32[]{:S(2)}, u32[]{:S(2)}) collective-permute-start(bf16[256,1024]{1,0:T(8,128)(2,1)} %collective-permute-done.15), channel_id=1, source_target_pairs={{1,0},{2,1},{3,2},{4,3},{5,4},{6,5},{7,6},{8,7},{9,8},{10,9},{11,1... | collective-permute-start | bytes 1572872 | tf_op jit(solution)/shard_map/ppermute | solution.py:18
  104.5 21.7 %collective-permute-start.19 = (bf16[256,1024]{1,0:T(8,128)(2,1)}, bf16[256,1024]{1,0:T(8,128)(2,1)}, u32[]{:S(2)}, u32[]{:S(2)}) collective-permute-start(bf16[256,1024]{1,0:T(8,128)(2,1)} %collective-permute-done.17), channel_id=1, source_target_pairs={{1,0},{2,1},{3,2},{4,3},{5,4},{6,5},{7,6},{8,7},{9,8},{10,9},{11,1... | collective-permute-start | bytes 1572872 | tf_op jit(solution)/shard_map/ppermute | solution.py:18
  112.9 14.5 %copy-start.55 = (pred[256,256]{1,0:T(8,128)(4,1)S(1)}, pred[256,256]{1,0:T(8,128)(4,1)}, u32[]{:S(2)}) copy-start(pred[256,256]{1,0:T(8,128)(4,1)} %get-tuple-element.364) | copy-start | bytes 196612
  112.9 14.5 %copy-start.66 = (f32[8,128,256]{2,1,0:T(8,128)S(1)}, f32[8,128,256]{2,1,0:T(8,128)}, u32[]{:S(2)}) copy-start(f32[8,128,256]{2,1,0:T(8,128)} %convolution_add_fusion.6) | copy-start | bytes 3145732
  114.2 13.3 %copy-start.39 = (bf16[32,8,8,128]{3,2,1,0:T(8,128)(2,1)}, bf16[32,8,8,128]{3,2,1,0:T(8,128)(2,1)S(1)}, u32[]{:S(2)}) copy-start(bf16[32,8,8,128]{3,2,1,0:T(8,128)(2,1)S(1)} %copy.403) | copy-start | bytes 1572868
  114.2 26.3 %collective-permute-start.3 = (bf16[2,256,1024]{2,1,0:T(8,128)(2,1)}, bf16[2,256,1024]{2,1,0:T(8,128)(2,1)}, u32[]{:S(2)}, u32[]{:S(2)}) collective-permute-start(bf16[2,256,1024]{2,1,0:T(8,128)(2,1)} %collective-permute-done.2), channel_id=1, source_target_pairs={{0,1},{1,2},{2,3},{3,4},{4,5},{5,6},{6,7},{7,8},{8,9},{9,10},{10,1... | collective-permute-start | bytes 3145736 | tf_op jit(solution)/shard_map/ppermute | solution.py:18
  126.1 8.2 %collective-permute-start.21 = (bf16[256,1024]{1,0:T(8,128)(2,1)}, bf16[256,1024]{1,0:T(8,128)(2,1)}, u32[]{:S(2)}, u32[]{:S(2)}) collective-permute-start(bf16[256,1024]{1,0:T(8,128)(2,1)} %collective-permute-done.19), channel_id=1, source_target_pairs={{1,0},{2,1},{3,2},{4,3},{5,4},{6,5},{7,6},{8,7},{9,8},{10,9},{11,1... | collective-permute-start | bytes 1572872 | tf_op jit(solution)/shard_map/ppermute | solution.py:18
  136.3 22.5 %collective-permute-start.23 = (bf16[256,1024]{1,0:T(8,128)(2,1)}, bf16[256,1024]{1,0:T(8,128)(2,1)}, u32[]{:S(2)}, u32[]{:S(2)}) collective-permute-start(bf16[256,1024]{1,0:T(8,128)(2,1)} %collective-permute-done.21), channel_id=1, source_target_pairs={{1,0},{2,1},{3,2},{4,3},{5,4},{6,5},{7,6},{8,7},{9,8},{10,9},{11,1... | collective-permute-start | bytes 1572872 | tf_op jit(solution)/shard_map/ppermute | solution.py:18
  146.7 20.2 %collective-permute-start.4 = (bf16[2,256,1024]{2,1,0:T(8,128)(2,1)}, bf16[2,256,1024]{2,1,0:T(8,128)(2,1)}, u32[]{:S(2)}, u32[]{:S(2)}) collective-permute-start(bf16[2,256,1024]{2,1,0:T(8,128)(2,1)} %collective-permute-done.3), channel_id=1, source_target_pairs={{0,1},{1,2},{2,3},{3,4},{4,5},{5,6},{6,7},{7,8},{8,9},{9,10},{10,1... | collective-permute-start | bytes 3145736 | tf_op jit(solution)/shard_map/ppermute | solution.py:18
  166.9 16.7 %collective-permute-start.5 = (bf16[2,256,1024]{2,1,0:T(8,128)(2,1)}, bf16[2,256,1024]{2,1,0:T(8,128)(2,1)}, u32[]{:S(2)}, u32[]{:S(2)}) collective-permute-start(bf16[2,256,1024]{2,1,0:T(8,128)(2,1)} %collective-permute-done.4), channel_id=1, source_target_pairs={{0,1},{1,2},{2,3},{3,4},{4,5},{5,6},{6,7},{7,8},{8,9},{9,10},{10,1... | collective-permute-start | bytes 3145736 | tf_op jit(solution)/shard_map/ppermute | solution.py:18
  183.6 16.5 %collective-permute-start.6 = (bf16[2,256,1024]{2,1,0:T(8,128)(2,1)}, bf16[2,256,1024]{2,1,0:T(8,128)(2,1)}, u32[]{:S(2)}, u32[]{:S(2)}) collective-permute-start(bf16[2,256,1024]{2,1,0:T(8,128)(2,1)} %collective-permute-done.5), channel_id=1, source_target_pairs={{0,1},{1,2},{2,3},{3,4},{4,5},{5,6},{6,7},{7,8},{8,9},{9,10},{10,1... | collective-permute-start | bytes 3145736 | tf_op jit(solution)/shard_map/ppermute | solution.py:18
  200.1 16.4 %collective-permute-start.7 = (bf16[2,256,1024]{2,1,0:T(8,128)(2,1)}, bf16[2,256,1024]{2,1,0:T(8,128)(2,1)}, u32[]{:S(2)}, u32[]{:S(2)}) collective-permute-start(bf16[2,256,1024]{2,1,0:T(8,128)(2,1)} %collective-permute-done.6), channel_id=1, source_target_pairs={{0,1},{1,2},{2,3},{3,4},{4,5},{5,6},{6,7},{7,8},{8,9},{9,10},{10,1... | collective-permute-start | bytes 3145736 | tf_op jit(solution)/shard_map/ppermute | solution.py:18
  234.7 60.2 %collective-permute-start.8 = (bf16[256,1024]{1,0:T(8,128)(2,1)}, bf16[256,1024]{1,0:T(8,128)(2,1)}, u32[]{:S(2)}, u32[]{:S(2)}) collective-permute-start(bf16[256,1024]{1,0:T(8,128)(2,1)} %add_add_fusion.1), channel_id=1, source_target_pairs={{1,0},{2,1},{3,2},{4,3},{5,4},{6,5},{7,6},{8,7},{9,8},{10,9},{11,1... | collective-permute-start | bytes 1572872 | tf_op jit(solution)/shard_map/ppermute | solution.py:18
  294.9 10.9 %collective-permute-start.10 = (bf16[256,1024]{1,0:T(8,128)(2,1)}, bf16[256,1024]{1,0:T(8,128)(2,1)}, u32[]{:S(2)}, u32[]{:S(2)}) collective-permute-start(bf16[256,1024]{1,0:T(8,128)(2,1)} %collective-permute-done.8), channel_id=1, source_target_pairs={{1,0},{2,1},{3,2},{4,3},{5,4},{6,5},{7,6},{8,7},{9,8},{10,9},{11,1... | collective-permute-start | bytes 1572872 | tf_op jit(solution)/shard_map/ppermute | solution.py:18
  305.9 10.8 %collective-permute-start.12 = (bf16[256,1024]{1,0:T(8,128)(2,1)}, bf16[256,1024]{1,0:T(8,128)(2,1)}, u32[]{:S(2)}, u32[]{:S(2)}) collective-permute-start(bf16[256,1024]{1,0:T(8,128)(2,1)} %collective-permute-done.10), channel_id=1, source_target_pairs={{1,0},{2,1},{3,2},{4,3},{5,4},{6,5},{7,6},{8,7},{9,8},{10,9},{11,1... | collective-permute-start | bytes 1572872 | tf_op jit(solution)/shard_map/ppermute | solution.py:18
  316.6 10.7 %collective-permute-start.14 = (bf16[256,1024]{1,0:T(8,128)(2,1)}, bf16[256,1024]{1,0:T(8,128)(2,1)}, u32[]{:S(2)}, u32[]{:S(2)}) collective-permute-start(bf16[256,1024]{1,0:T(8,128)(2,1)} %collective-permute-done.12), channel_id=1, source_target_pairs={{1,0},{2,1},{3,2},{4,3},{5,4},{6,5},{7,6},{8,7},{9,8},{10,9},{11,1... | collective-permute-start | bytes 1572872 | tf_op jit(solution)/shard_map/ppermute | solution.py:18
  327.4 11.2 %collective-permute-start.16 = (bf16[256,1024]{1,0:T(8,128)(2,1)}, bf16[256,1024]{1,0:T(8,128)(2,1)}, u32[]{:S(2)}, u32[]{:S(2)}) collective-permute-start(bf16[256,1024]{1,0:T(8,128)(2,1)} %collective-permute-done.14), channel_id=1, source_target_pairs={{1,0},{2,1},{3,2},{4,3},{5,4},{6,5},{7,6},{8,7},{9,8},{10,9},{11,1... | collective-permute-start | bytes 1572872 | tf_op jit(solution)/shard_map/ppermute | solution.py:18
  338.5 11.3 %collective-permute-start.18 = (bf16[256,1024]{1,0:T(8,128)(2,1)}, bf16[256,1024]{1,0:T(8,128)(2,1)}, u32[]{:S(2)}, u32[]{:S(2)}) collective-permute-start(bf16[256,1024]{1,0:T(8,128)(2,1)} %collective-permute-done.16), channel_id=1, source_target_pairs={{1,0},{2,1},{3,2},{4,3},{5,4},{6,5},{7,6},{8,7},{9,8},{10,9},{11,1... | collective-permute-start | bytes 1572872 | tf_op jit(solution)/shard_map/ppermute | solution.py:18
  349.8 11.4 %collective-permute-start.20 = (bf16[256,1024]{1,0:T(8,128)(2,1)}, bf16[256,1024]{1,0:T(8,128)(2,1)}, u32[]{:S(2)}, u32[]{:S(2)}) collective-permute-start(bf16[256,1024]{1,0:T(8,128)(2,1)} %collective-permute-done.18), channel_id=1, source_target_pairs={{1,0},{2,1},{3,2},{4,3},{5,4},{6,5},{7,6},{8,7},{9,8},{10,9},{11,1... | collective-permute-start | bytes 1572872 | tf_op jit(solution)/shard_map/ppermute | solution.py:18
  361.2 11.4 %collective-permute-start.22 = (bf16[256,1024]{1,0:T(8,128)(2,1)}, bf16[256,1024]{1,0:T(8,128)(2,1)}, u32[]{:S(2)}, u32[]{:S(2)}) collective-permute-start(bf16[256,1024]{1,0:T(8,128)(2,1)} %collective-permute-done.20), channel_id=1, source_target_pairs={{1,0},{2,1},{3,2},{4,3},{5,4},{6,5},{7,6},{8,7},{9,8},{10,9},{11,1... | collective-permute-start | bytes 1572872 | tf_op jit(solution)/shard_map/ppermute | solution.py:18
  (64 other events, 236.0 us)
Sparse Core Ops, SparseCore 0:
  398.8 212.8 reduce-scatter.1
where the time goes:
time: 630 us; the launch traced here: 619 us
  waiting for transfers between devices  204 us (32%)
  matrix products  198 us (31%)
  starting transfers between devices  102 us (16%)
  local copies, waits for them, and re-layouts  86.4 us (14%)
  between operations  15.5 us (2%)
  other arithmetic  13.9 us (2%)
    reduce_scatter x1, waiting for transfers between devices, per_device(): lax.psum_scatter(lax.dot_general(d_pre_b, normed, (((0,), (0,)), ((), ())...  202 us
    dot_general x35, matrix products, attend(): jnp.einsum('qhd,khd->hqk', qh, kh, preferred_element_type=jnp.float32)  118 us
    ppermute x24, starting transfers between devices, from_behind(): lax.ppermute(value, axis, [(source, source + steps) for source in range(f...  101 us
    dot_general x19, matrix products, attend(): jnp.einsum('hqk,khd->qhd', weights, vh, preferred_element_type=jnp.float32)  51.6 us
    unnamed x166, local copies, waits for them, and re-layouts  38.5 us
    reshape x9, local copies, waits for them, and re-layouts, attend(): qh = query.reshape(query.shape[0], HEADS, HD)  17.6 us
    another operation x8, local copies, waits for them, and re-layouts, attend(): kh = keys.reshape(keys.shape[0], HEADS, HD)  16.4 us
  transfers between devices with their start and end apart: 25, of which 4 were waited for; matrix products, arithmetic and copies ran while one was open for 39% of the time, Pallas kernels for 0%

commit v1 on v0

v1 whole, which is shorter than its diff:
```python
import functools

import jax
import jax.numpy as jnp
from jax import lax
from jax.experimental import pallas as pl
from jax.experimental.pallas import tpu as pltpu
from jax.sharding import Mesh, PartitionSpec as P

HEADS = 8
HD = 128
BLK = 128
MAXB = 16
SPAN = MAXB * BLK
TILE = 256
TILES = SPAN // TILE
HALF = 0.5 * HD ** (-0.5)

eps = 1e-05

NT = (((1,), (1,)), ((), ()))
F32, BF16 = jnp.float32, jnp.bfloat16

U, Q, V, K = (slice(i * HD, (i + 1) * HD) for i in range(4))
PLACE = (0, 2, 1, 3)
UQ, VK = slice(0, 2 * HD), slice(2 * HD, 4 * HD)


def block_info(counts, tails, base, blocks):
    ends = jnp.cumsum(counts)
    starts = ends - counts
    at = base + jnp.arange(blocks + 1, dtype=jnp.int32)
    user = jnp.sum((at[:, None] >= ends[None, :]).astype(jnp.int32), axis=1)
    pick = user[:, None] == jnp.arange(counts.shape[0], dtype=jnp.int32)[None, :]
    start = jnp.sum(jnp.where(pick, starts[None, :], 0), axis=1)
    last = jnp.sum(jnp.where(pick, ends[None, :] - 1, 0), axis=1)
    tail = jnp.sum(jnp.where(pick, tails[None, :], 0), axis=1)
    start = jnp.where(at < ends[-1], start, at)
    return (start - base) * BLK, jnp.where(at == last, tail, BLK)


def by_half(t, ref, shape, dim):
    side = lax.broadcasted_iota(jnp.int32, shape, dim)
    return jnp.where(side < BLK, ref[2 * t], ref[2 * t + 1])


def valid_rows(t, nv_ref):
    row = lax.broadcasted_iota(jnp.int32, (TILE, 1), 0)
    return (row & (BLK - 1)) < by_half(t, nv_ref, (TILE, 1), 0)


def rows_at(t):
    return pl.ds(pl.multiple_of(t * TILE, TILE), TILE)


def far_tiles(lo_ref):
    return sum((lo_ref[2 * t] < 0).astype(jnp.int32) for t in range(TILES))


class Copies:
    def __init__(self, sems):
        self.sems, self.used, self.open = sems, 0, []

    def __call__(self, src, dst):
        copy = pltpu.make_async_copy(src, dst, self.sems.at[self.used])
        self.used += 1
        copy.start()
        return copy

    def out(self, src, dst):
        self.open.append(self(src, dst))

    def finish(self):
        for copy in self.open:
            copy.wait()


class Tiled:
    def __init__(self, src, dst, sems, at, src_cols=slice(None), dst_cols=slice(None)):
        self.args = src, dst, sems, at, src_cols, dst_cols

    def tile(self, t):
        src, dst, sems, at, src_cols, dst_cols = self.args
        rows = rows_at(t) if not isinstance(t, int) else slice(t * TILE, (t + 1) * TILE)
        return pltpu.make_async_copy(src.at[rows, src_cols], dst.at[rows, dst_cols], sems.at[at + t])

    def start(self, t):
        self.tile(t).start()

    def start_all(self):
        for t in range(TILES):
            self.start(t)

    def wait(self, t):
        self.tile(t).wait()

    def wait_all(self):
        for t in range(TILES):
            self.wait(t)


def norm_rows(x):
    return x * lax.rsqrt(jnp.mean(x * x, axis=-1, keepdims=True) + eps)


def silu_and_slope(pre):
    s = 0.5 + 0.5 * jnp.tanh(0.5 * pre)
    return (pre * s).astype(BF16), (s * (1.0 + pre * (1.0 - s))).astype(BF16)


def proj_kernel(masks, pieces, head_ref, *refs):
    x_refs, w_ref = refs[: sum(pieces)], refs[sum(pieces)]
    normed_ref, act_ref, slope_ref, kv_ref, x_s, w_s, normed_s, act_s, slope_s, sems = refs[-10:]
    copies = Copies(sems)
    width = w_ref.shape[0]
    weights = [
        copies(w_ref.at[:, pl.ds(pl.multiple_of(PLACE[i] * width + head_ref[0] * HD, HD), HD)], w_s.at[:, i * HD : (i + 1) * HD])
        for i in range(4)
    ]
    loads, at = [], 0
    for i, count in enumerate(pieces):
        size = TILE // count
        loads.append([copies(x_refs[at + j], x_s.at[i, j * size : (j + 1) * size, :]) for j in range(count)])
        at += count
    for copy in weights:
        copy.wait()
    for i, mask in enumerate(masks):
        for copy in loads[i]:
            copy.wait()
        rows = rows_at(head_ref[0] ^ mask)
        xn = norm_rows(x_s[i].astype(F32)).astype(BF16)
        normed_s[i] = xn
        copies.out(normed_s.at[i], normed_ref.at[rows, :])
        act_s[i], slope_s[i] = silu_and_slope(jnp.dot(xn, w_s[...], preferred_element_type=F32))
        copies.out(act_s.at[i, :, VK], kv_ref.at[i * TILE : (i + 1) * TILE, :])
        copies.out(act_s.at[i], act_ref.at[rows, :])
        copies.out(slope_s.at[i], slope_ref.at[rows, :])
    copies.finish()


def project(head, masks, chunks, w, kept):
    width, n = w.shape[0], len(masks)
    pieces = tuple(len(chunk) for chunk in chunks)
    flat = [piece for chunk in chunks for piece in chunk]
    start = 2 + len(flat)
    return call(
        functools.partial(proj_kernel, masks, pieces),
        (head,),
        (*flat, w, *kept),
        [((SPAN, width), BF16), ((SPAN, 4 * HD), BF16), ((SPAN, 4 * HD), BF16), ((n * TILE, 2 * HD), BF16)],
        [
            pltpu.VMEM((n, TILE, width), BF16),
            pltpu.VMEM((width, 4 * HD), BF16),
            pltpu.VMEM((n, TILE, width), BF16),
            pltpu.VMEM((n, TILE, 4 * HD), BF16),
            pltpu.VMEM((n, TILE, 4 * HD), BF16),
        ],
        4 + len(flat) + 4 * n,
        {start + i: i for i in range(len(kept))},
    )


def cut_kernel(x_ref, y_ref, a_ref, b_ref, x_out, y_out, x_half, y_half, x_s, y_s, sems):
    copies = Copies(sems)
    x, y = copies(x_ref.at[:BLK, :], x_s), copies(y_ref.at[BLK:, :], y_s)
    x.wait()
    copies.out(x_s, x_half)
    y.wait()
    copies.out(y_s, y_half)
    copies.finish()


def gate_kernel(a_ref, b_ref, after_ref, a_out, b_out, sems):
    pass


def d_gated_kernel(g_ref, w_ref, after_ref, out_ref, g_s, w_s, out_s, sems):
    copies = Copies(sems)
    g = copies(g_ref, g_s)
    half = w_s.shape[0] // 2
    loads = [copies(w_ref.at[i * half : (i + 1) * half, :], w_s.at[i * half : (i + 1) * half, :]) for i in range(2)]
    g.wait()
    for i in range(2):
        loads[i].wait()
        d = lax.dot_general(g_s[...], w_s[i * half : (i + 1) * half, :], NT, preferred_element_type=F32).astype(BF16)
        for h in range(HEADS // 2):
            out_s[i * HEADS // 2 + h] = d[:, h * HD : (h + 1) * HD]
    copies.out(out_s, out_ref)
    copies.finish()


def turned(x):
    n = x.shape[1]
    eye = lax.broadcasted_iota(jnp.int32, (n, n), 0) == lax.broadcasted_iota(jnp.int32, (n, n), 1)
    return lax.dot_general(eye.astype(BF16), x, NT, preferred_element_type=F32).astype(BF16)


def sweep(first, last, one, carry):
    count = last - first
    carry = lax.fori_loop(0, count // 2, lambda i, c: one(first + 2 * i + 1, one(first + 2 * i, c)), carry)
    return lax.fori_loop(last - count % 2, last, one, carry)


def weigh(q, k, v, mask):
    half = lax.dot_general(q, k, NT, preferred_element_type=F32) * HALF
    w = half + half * jnp.tanh(half)
    w = jnp.where(mask, w, 0.0).astype(BF16)
    return jnp.dot(w, v, preferred_element_type=F32)


def fwd_own_kernel(lo_ref, nv_ref, act_ref, out_ref, act_s, out_s, sems):
    loads = Tiled(act_ref, act_s, sems, 0)
    stores = Tiled(out_s, out_ref, sems, TILES)
    loads.start_all()
    row = lax.broadcasted_iota(jnp.int32, (TILE, TILE), 0)
    col = lax.broadcasted_iota(jnp.int32, (TILE, TILE), 1)

    def q_tile(t, carry):
        loads.wait(t)
        lo = by_half(t, lo_ref, (TILE, 1), 0) - t * TILE
        q = act_s[rows_at(t), Q]
        acc = weigh(q, act_s[rows_at(t), K], act_s[rows_at(t), V], (col <= row) & (col >= lo))

        def k_tile(s, acc):
            return acc + weigh(q, act_s[rows_at(s), K], act_s[rows_at(s), V], col >= lo + (t - s) * TILE)

        first = jnp.maximum(lo_ref[2 * t], 0) // TILE
        acc = sweep(first, t, k_tile, acc)
        out_s[rows_at(t), :] = jnp.where(valid_rows(t, nv_ref), acc, 0.0)
        stores.start(t)
        return carry

    lax.fori_loop(0, TILES, q_tile, 0)
    stores.wait_all()


def load_far(head_ref, kv_refs, kv_s, copies):
    loads, slot = [], 0
    for ref in kv_refs:
        for at in range(0, ref.shape[0], TILE):
            loads.append(copies(ref.at[at : at + TILE, :], kv_s.at[rows_at(slot ^ head_ref[0]), :]))
            slot += 1
    return loads


def fwd_far_kernel(
    head_ref, lo_ref, nv_ref, act_ref, kva_ref, kvb_ref, kvc_ref, near_ref, dg_ref, out_ref, sum_ref,
    uq_s, kv_s, near_s, dg_s, out_s, sum_s, sems,
):
    uqs = Tiled(act_ref, uq_s, sems, 0, src_cols=UQ)
    nears = Tiled(near_ref, near_s, sems, TILES)
    dgs = Tiled(dg_ref, dg_s, sems, 2 * TILES)
    stores = Tiled(out_s, out_ref, sems, 3 * TILES)
    copies = Copies(sems)
    copies.used = 4 * TILES
    far = load_far(head_ref, (kva_ref, kvb_ref, kvc_ref), kv_s, copies)
    for t in reversed(range(TILES)):
        for loads in (uqs, nears, dgs):
            loads.start(t)
    col = lax.broadcasted_iota(jnp.int32, (TILE, TILE), 1)

    def finish(t, acc):
        attn = acc * (1.0 / SPAN)
        out_s[rows_at(t), :] = attn.astype(BF16)
        stores.start(t)
        d_n = dg_s[rows_at(t), :].astype(F32) * uq_s[rows_at(t), U].astype(F32)
        ones = jnp.ones((8, HD), BF16)
        square = lax.dot_general(ones, (attn * attn).astype(BF16), NT, preferred_element_type=F32)[:1]
        cross = lax.dot_general(ones, (attn * d_n).astype(BF16), NT, preferred_element_type=F32)[:1]
        for h in range(HEADS):
            sum_s[h, pl.ds(t, 1), :] = square
            sum_s[h, pl.ds(TILES + t, 1), :] = cross

    def wait(t):
        for loads in (uqs, nears, dgs):
            loads.wait(t)

    def near_tile(i, carry):
        t = TILES - 1 - i
        wait(t)
        finish(t, near_s[rows_at(t), :])
        return carry

    def far_tile(t, carry):
        wait(t)
        lo = by_half(t, lo_ref, (TILE, 1), 0) + SPAN
        q = uq_s[rows_at(t), Q]

        def k_tile(s, acc):
            return acc + weigh(q, kv_s[rows_at(s), HD:], kv_s[rows_at(s), :HD], col >= lo - s * TILE)

        first = (lo_ref[2 * t] + SPAN) // TILE
        acc = sweep(first, TILES, k_tile, jnp.zeros((TILE, HD), F32))
        finish(t, jnp.where(valid_rows(t, nv_ref), acc, 0.0) + near_s[rows_at(t), :])
        return carry

    count = far_tiles(lo_ref)
    lax.fori_loop(0, TILES - count, near_tile, 0)
    for copy in far:
        copy.wait()
    lax.fori_loop(0, count, far_tile, 0)
    copies.out(sum_s, sum_ref)
    copies.finish()
    stores.wait_all()


def row_scales(sum_s, scale_s):
    width = HEADS * HD
    total = jnp.sum(sum_s[...], axis=0)
    r = lax.rsqrt(total[:TILES] * (1.0 / width) + eps)
    c = total[TILES:] * (1.0 / width) * r
    scales = jnp.concatenate([r, c, jnp.zeros((HD - 2 * TILES, TILE), F32)], axis=0).T
    high = scales.astype(BF16)
    scale_s[:, :HD] = high
    scale_s[:, HD:] = (scales - high.astype(F32)).astype(BF16)


def spread(scale_s, i):
    row = lax.broadcasted_iota(jnp.int32, (2 * HD, HD), 0) & (HD - 1)
    return jnp.dot(scale_s[...], (row == i).astype(BF16), preferred_element_type=F32)


def cotangent(t, scale_s, nv_ref, u, attn, d_gated):
    r, c = spread(scale_s, t), spread(scale_s, TILES + t)
    n = attn.astype(F32) * r
    g = r * (d_gated * u.astype(F32) - n * c)
    return n, jnp.where(valid_rows(t, nv_ref), g, 0.0).astype(BF16)


def back(q, k, kt, v, g, mask):
    half = lax.dot_general(k, q, NT, preferred_element_type=F32) * HALF
    up = jnp.where(mask, 1.0 + jnp.tanh(half), 0.0)
    w = (half * up).astype(BF16)
    dw = lax.dot_general(v, g, NT, preferred_element_type=F32)
    ds = (dw * up * (1.0 + half * (2.0 - up))).astype(BF16)
    dv = jnp.dot(w, g, preferred_element_type=F32)
    dk = jnp.dot(ds, q, preferred_element_type=F32)
    dqt = jnp.dot(kt, ds, preferred_element_type=F32)
    return dv, dk, dqt


def bwd_far_kernel(
    head_ref, lo_ref, nv_ref, sum_ref, act_ref, attn_ref, dg_ref, kva_ref, kvb_ref, kvc_ref, dq_ref, dkv_ref,
    sum_s, uq_s, attn_s, dg_s, kv_s, kt_s, acc_s, scale_s, dq_s, dkv_s, sems,
):
    uqs = Tiled(act_ref, uq_s, sems, 0, src_cols=UQ)
    attns = Tiled(attn_ref, attn_s, sems, TILES)
    dgs = Tiled(dg_ref, dg_s, sems, 2 * TILES)
    dkvs = Tiled(dkv_s, dkv_ref, sems, 4 * TILES)
    copies = Copies(sems)
    copies.used = 5 * TILES
    count = far_tiles(lo_ref)
    first = jnp.minimum(lo_ref[0] + SPAN, SPAN) // TILE

    @pl.when(count > 0)
    def _():
        sums = copies(sum_ref, sum_s)
        far = load_far(head_ref, (kva_ref, kvb_ref, kvc_ref), kv_s, copies)

        def start(t, carry):
            for loads in (uqs, attns, dgs):
                loads.start(t)
            return carry

        lax.fori_loop(0, count, start, 0)
        sums.wait()
        row_scales(sum_s, scale_s)
        for copy in far:
            copy.wait()

        def prepare(s, carry):
            acc_s[rows_at(s), :] = jnp.zeros((TILE, 2 * HD), F32)
            kt_s[:, rows_at(s)] = turned(kv_s[rows_at(s), HD:])
            return carry

        lax.fori_loop(first, TILES, prepare, 0)

        def q_tile(t, carry):
            for loads in (uqs, attns, dgs):
                loads.wait(t)
            lo = by_half(t, lo_ref, (1, TILE), 1) + SPAN
            q = uq_s[rows_at(t), Q]
            d_gated = dg_s[rows_at(t), :].astype(F32)
            g = cotangent(t, scale_s, nv_ref, uq_s[rows_at(t), U], attn_s[rows_at(t), :], d_gated)[1]
            key = lax.broadcasted_iota(jnp.int32, (TILE, TILE), 0)

            def k_tile(s, dqt):
                k, v = kv_s[rows_at(s), HD:], kv_s[rows_at(s), :HD]
                dv, dk, dqt_part = back(q, k, kt_s[:, rows_at(s)], v, g, key >= lo - s * TILE)
                acc_s[rows_at(s), :HD] += dv
                acc_s[rows_at(s), HD:] += dk
                return dqt + dqt_part

            start = (lo_ref[2 * t] + SPAN) // TILE
            dqt = sweep(start, TILES, k_tile, jnp.zeros((HD, TILE), F32))
            dq_s[:, rows_at(t)] = dqt
            return carry

        lax.fori_loop(0, count, q_tile, 0)
        copies.out(dq_s, dq_ref)

        def store(s, carry):
            dkv_s[rows_at(s), :HD] = (acc_s[rows_at(s), :HD] * (1.0 / SPAN)).astype(BF16)
            dkv_s[rows_at(s), HD:] = (acc_s[rows_at(s), HD:] * (HALF / SPAN)).astype(BF16)
            dkvs.start(s)
            return carry

        lax.fori_loop(first, TILES, store, 0)
        lax.fori_loop(first, TILES, lambda s, carry: dkvs.wait(s) or carry, 0)
        copies.finish()


def bwd_own_kernel(
    lo_ref, nv_ref, sum_ref, act_ref, slope_ref, attn_ref, dg_ref, far_ref, rows_ref, cols_ref, dkv_ref,
    sum_s, act_s, slope_s, attn_s, dg_s, far_s, kt_s, acc_s, scale_s, rows_s, cols_s, dkv_s, sems,
):
    acts = Tiled(act_ref, act_s, sems, 0)
    slopes = Tiled(slope_ref, slope_s, sems, TILES, src_cols=UQ)
    attns = Tiled(attn_ref, attn_s, sems, 2 * TILES)
    dgs = Tiled(dg_ref, dg_s, sems, 3 * TILES)
    stores = Tiled(rows_s, rows_ref, sems, 5 * TILES)
    dkvs = Tiled(dkv_s, dkv_ref, sems, 6 * TILES)
    copies = Copies(sems)
    copies.used = 7 * TILES
    sums = copies(sum_ref, sum_s)
    for t in range(TILES):
        for loads in (acts, attns, dgs, slopes):
            loads.start(t)
    count = far_tiles(lo_ref)
    far = copies(far_ref, far_s)
    sums.wait()
    row_scales(sum_s, scale_s)

    def q_tile(t, carry):
        for loads in (acts, attns, dgs, slopes):
            loads.wait(t)
        lo = by_half(t, lo_ref, (1, TILE), 1) - t * TILE
        q, k, v = act_s[rows_at(t), Q], act_s[rows_at(t), K], act_s[rows_at(t), V]
        kt_s[:, rows_at(t)] = turned(k)
        d_gated = dg_s[rows_at(t), :].astype(F32)
        n, g = cotangent(t, scale_s, nv_ref, act_s[rows_at(t), U], attn_s[rows_at(t), :], d_gated)
        du = (d_gated * n).astype(BF16).astype(F32)
        cols_s[:HD, rows_at(t)] = turned((du * slope_s[rows_at(t), U].astype(F32)).astype(BF16))
        key = lax.broadcasted_iota(jnp.int32, (TILE, TILE), 0)
        query = lax.broadcasted_iota(jnp.int32, (TILE, TILE), 1)
        mask = (key <= query) & (key >= lo)
        dv, dk, dqt = back(q, k, kt_s[:, rows_at(t)], v, g, mask)
        acc_s[rows_at(t), :HD] = dv
        acc_s[rows_at(t), HD:] = dk

        def k_tile(s, dqt):
            mask = key >= lo + (t - s) * TILE
            dv, dk, dqt_part = back(q, act_s[rows_at(s), K], kt_s[:, rows_at(s)], act_s[rows_at(s), V], g, mask)
            acc_s[rows_at(s), :HD] += dv
            acc_s[rows_at(s), HD:] += dk
            return dqt + dqt_part

        first = jnp.maximum(lo_ref[2 * t], 0) // TILE
        dqt = sweep(first, t, k_tile, dqt)

        dq = dqt + jnp.where(t < count, far_s[:, rows_at(t)], 0.0)
        dq = (dq * (HALF / SPAN)).astype(BF16).astype(F32)
        dq = (dq * turned(slope_s[rows_at(t), Q]).astype(F32)).astype(BF16)
        cols_s[HD:, rows_at(t)] = dq
        rows_s[rows_at(t), :] = turned(dq)
        stores.start(t)
        return carry

    far.wait()
    lax.fori_loop(0, TILES, q_tile, 0)
    copies.out(cols_s, cols_ref)

    def store(s, carry):
        dkv_s[rows_at(s), :HD] = (acc_s[rows_at(s), :HD] * (1.0 / SPAN)).astype(BF16)
        dkv_s[rows_at(s), HD:] = (acc_s[rows_at(s), HD:] * (HALF / SPAN)).astype(BF16)
        dkvs.start(s)
        return carry

    lax.fori_loop(0, TILES, store, 0)
    copies.finish()
    stores.wait_all()
    dkvs.wait_all()


def key_kernel(lo_ref, nv_ref, own_ref, far_ref, slope_ref, rows_ref, cols_ref, own_s, far_s, slope_s, rows_s, cols_s, sems):
    owns = Tiled(own_ref, own_s, sems, 0)
    fars = Tiled(far_ref, far_s, sems, TILES)
    slopes = Tiled(slope_ref, slope_s, sems, 2 * TILES, src_cols=VK)
    stores = Tiled(rows_s, rows_ref, sems, 3 * TILES)
    copies = Copies(sems)
    copies.used = 4 * TILES
    first = jnp.minimum(lo_ref[2 * TILES], SPAN) // TILE
    for t in range(TILES):
        owns.start(t)
        slopes.start(t)
    lax.fori_loop(first, TILES, lambda t, carry: fars.start(t) or carry, 0)

    def tile(t, carry):
        owns.wait(t)
        slopes.wait(t)

        @pl.when(t >= first)
        def _():
            fars.wait(t)

        far = jnp.where(t >= first, far_s[rows_at(t), :].astype(F32), 0.0)
        d = (own_s[rows_at(t), :].astype(F32) + far).astype(BF16).astype(F32)
        d = (d * slope_s[rows_at(t), :].astype(F32)).astype(BF16)
        rows_s[rows_at(t), :] = d
        stores.start(t)
        cols_s[:, rows_at(t)] = turned(d)
        return carry

    lax.fori_loop(0, TILES, tile, 0)
    copies.out(cols_s, cols_ref)
    copies.finish()
    stores.wait_all()


def joined(ref, part):
    return jnp.concatenate([ref[h, :, part * HD : (part + 1) * HD] for h in range(HEADS)], axis=1)


def rows_kernel(
    attn_ref, q_ref, dg_ref, tokens_ref, w_out_ref, w_in_ref, out_ref, dn_ref,
    attn_s, q_s, dg_s, x_s, wo_s, wu_s, wq_s, out_s, dn_s, sems,
):
    width = w_out_ref.shape[0]
    copies = Copies(sems)
    first = [copies(tokens_ref, x_s), copies(w_in_ref.at[:, :width], wu_s)]
    second = [copies(*pair) for pair in ((attn_ref, attn_s), (w_out_ref, wo_s), (dg_ref, dg_s))]
    third = [copies(q_ref, q_s), copies(w_in_ref.at[:, 2 * width : 3 * width], wq_s)]
    for copy in first:
        copy.wait()
    x = x_s[...].astype(F32)
    u, slope = silu_and_slope(jnp.dot(norm_rows(x).astype(BF16), wu_s[...], preferred_element_type=F32))
    for copy in second:
        copy.wait()
    n = norm_rows(joined(attn_s, 0).astype(F32))
    gated = (n * u.astype(F32)).astype(BF16)
    y = jnp.dot(gated, wo_s[...], preferred_element_type=F32)
    out_s[...] = (x + y).astype(BF16)
    copies.out(out_s, out_ref)
    du = (joined(dg_s, 0).astype(F32) * n).astype(BF16).astype(F32)
    du = (du * slope.astype(F32)).astype(BF16)
    dn_s[...] = lax.dot_general(du, wu_s[...], NT, preferred_element_type=F32)
    for copy in third:
        copy.wait()
    dn_s[...] += lax.dot_general(joined(q_s, 0), wq_s[...], NT, preferred_element_type=F32)
    copies.out(dn_s, dn_ref)
    copies.finish()


def pieces_kernel(groups, group_ref, a_ref, b_ref, normed_ref, *refs):
    outs, (a_s, b_s, normed_s, all_s, sems) = refs[:groups], refs[groups:]
    copies = Copies(sems)
    parts = [slice(i * 2 * TILE, (i + 1) * 2 * TILE) for i in range(TILES // 2)]
    sides = copies(a_ref, a_s), copies(b_ref, b_s)
    loads = [copies(normed_ref.at[part, :], normed_s.at[part, :]) for part in parts]
    for copy in sides:
        copy.wait()
    totals = [0.0, 0.0]
    for part, load in zip(parts, loads):
        load.wait()
        for i, side in enumerate((a_s, b_s)):
            totals[i] += jnp.dot(side[:, part], normed_s[part, :], preferred_element_type=F32)
    for i in range(2):
        all_s[i * HD : (i + 1) * HD, :] = totals[i][:HD].astype(BF16)
        all_s[(2 + i) * HD : (3 + i) * HD, :] = totals[i][HD:].astype(BF16)
    rows = 4 * HD // groups
    for mask in range(groups):
        at = pl.multiple_of((group_ref[0] ^ mask) * rows, rows)
        copies.out(all_s.at[pl.ds(at, rows), :], outs[mask])
    copies.finish()


def last_kernel(groups, kv_ref, dn_ref, tokens_ref, grad_ref, w_in_ref, *refs):
    pieces, (out_ref, share_ref) = refs[:groups], refs[groups : groups + 2]
    kv_s, dn_s, x_s, g_s, wv_s, wk_s, pieces_s, out_s, share_s, sems = refs[groups + 2 :]
    width = w_in_ref.shape[0]
    copies = Copies(sems)
    kv = copies(kv_ref, kv_s)
    wv = copies(w_in_ref.at[:, width : 2 * width], wv_s)
    wk = copies(w_in_ref.at[:, 3 * width :], wk_s)
    rest = [copies(*pair) for pair in ((dn_ref, dn_s), (tokens_ref, x_s), (grad_ref, g_s))]
    loads = [copies(ref, pieces_s.at[i]) for i, ref in enumerate(pieces)]
    kv.wait()
    wv.wait()
    dn = lax.dot_general(joined(kv_s, 0), wv_s[...], NT, preferred_element_type=F32)
    wk.wait()
    dn += lax.dot_general(joined(kv_s, 1), wk_s[...], NT, preferred_element_type=F32)
    for copy in rest:
        copy.wait()
    dn += dn_s[...]
    x = x_s[...].astype(F32)
    r = lax.rsqrt(jnp.mean(x * x, axis=-1, keepdims=True) + eps)
    n = x * r
    dx = r * (dn - n * jnp.mean(dn * n, axis=-1, keepdims=True))
    out_s[...] = (g_s[...].astype(F32) + dx).astype(BF16)
    copies.out(out_s, out_ref)
    for copy in loads:
        copy.wait()
    total = pieces_s[0].astype(F32)
    for i in range(1, groups):
        total += pieces_s[i].astype(F32)
    share_s[...] = total
    copies.out(share_s, share_ref)
    copies.finish()


def call(kernel, scalars, arrays, outs, scratch=(), sems=1, aliases=None, limit=52):
    smem = pl.BlockSpec(memory_space=pltpu.SMEM)
    anywhere = pl.BlockSpec(memory_space=pl.ANY)
    return pl.pallas_call(
        kernel,
        out_shape=[jax.ShapeDtypeStruct(*out) for out in outs],
        in_specs=[smem] * len(scalars) + [anywhere] * len(arrays),
        out_specs=[anywhere] * len(outs),
        scratch_shapes=[*scratch, pltpu.SemaphoreType.DMA((sems,))],
        input_output_aliases=aliases or {},
        compiler_params=pltpu.CompilerParams(vmem_limit_bytes=limit * 2**20),
        cost_estimate=pl.CostEstimate(flops=0, bytes_accessed=0, transcendentals=0),
    )(*scalars, *arrays)


def per_device(groups, tokens, w_in, w_out, block_counts, tails, grad_out):
    count, width = tokens.shape
    group = lax.axis_index("g").astype(jnp.int32)
    head = lax.axis_index("h").astype(jnp.int32).reshape(1)
    info = block_info(block_counts, tails, group * MAXB, MAXB)

    def swap(x, mask):
        return lax.ppermute(x, "h", [(i, i ^ mask) for i in range(HEADS)])

    def exchange(x):
        x = x.reshape(HEADS, -1, x.shape[-1])
        return lax.all_to_all(x, "h", 0, 0, tiled=True)

    def onward(x):
        return lax.ppermute(x, "g", [(i, i + 1) for i in range(groups - 1)])

    def vmem(shape, dtype=BF16):
        return pltpu.VMEM(shape, dtype)

    own, tall, wide = (count, width), (SPAN, HD), (SPAN, 2 * HD)
    across, by_head, square = (2 * HD, SPAN), (HEADS, count, HD), (width, width)
    sum_shape = (HEADS, 2 * TILES, TILE)

    half = ((BLK, width), BF16)
    x_rows, y_rows = swap(tokens, 2), swap(tokens, 4)
    other = swap(tokens, 1)
    *kept, kv = project(head, (0, 1), ((tokens,), (other,)), w_in, ())
    far_kv = [onward(kv)]
    d_gated_rows = call(
        d_gated_kernel, (), (grad_out, w_out, kv), [(by_head, BF16)], [vmem(own), vmem(square), vmem(by_head)], 4
    )[0]
    d_gated = exchange(d_gated_rows).reshape(SPAN, HD)
    x_rows, y_rows, x_half, y_half = call(
        cut_kernel,
        (),
        (x_rows, y_rows, far_kv[0], d_gated_rows),
        [(own, BF16), (own, BF16), half, half],
        [vmem((BLK, width)), vmem((BLK, width))],
        4,
        {0: 0, 1: 1},
        4,
    )
    corner = swap(x_half, 4), swap(y_half, 2)
    chunks = ((x_rows,), (swap(x_rows, 1),), (y_rows,), (swap(y_rows, 1),))
    *kept, kv = project(head, (2, 3, 4, 5), chunks, w_in, kept)
    far_kv.append(onward(kv))
    corner = call(gate_kernel, (), (*corner, kv), [half, half], aliases={0: 0, 1: 1}, limit=4)
    *kept, kv = project(head, (6, 7), (corner, [swap(x, 1) for x in corner]), w_in, kept)
    far_kv.append(onward(kv))
    normed, act, slope = kept

    near = call(fwd_own_kernel, info, (act,), [(tall, F32)], [vmem((SPAN, 4 * HD)), vmem(tall, F32)], 2 * TILES)[0]
    attn, sums = call(
        fwd_far_kernel,
        (head, *info),
        (act, *far_kv, near, d_gated),
        [(tall, BF16), (sum_shape, F32)],
        [vmem(wide), vmem(wide), vmem(tall, F32), vmem(tall), vmem(tall), vmem(sum_shape, F32)],
        4 * TILES + HEADS + 1,
    )
    sums = exchange(sums)

    dq_far, dkv_far = call(
        bwd_far_kernel,
        (head, *info),
        (sums, act, attn, d_gated, *far_kv),
        [((HD, SPAN), F32), (wide, BF16)],
        [vmem(sum_shape, F32), vmem(wide), vmem(tall), vmem(tall), vmem(wide), vmem((HD, SPAN)), vmem(wide, F32)]
        + [vmem((TILE, 2 * HD)), vmem((HD, SPAN), F32), vmem(wide)],
        5 * TILES + HEADS + 2,
    )
    dkv_far = lax.ppermute(dkv_far, "g", [(i + 1, i) for i in range(groups - 1)])
    attn_rows = exchange(attn)
    d_q, cols_a, dkv = call(
        bwd_own_kernel,
        info,
        (sums, act, slope, attn, d_gated, dq_far),
        [(tall, BF16), (across, BF16), (wide, BF16)],
        [vmem(sum_shape, F32), vmem((SPAN, 4 * HD)), vmem(wide), vmem(tall), vmem(tall), vmem((HD, SPAN), F32), vmem((HD, SPAN))]
        + [vmem(wide, F32), vmem((TILE, 2 * HD)), vmem(tall), vmem(across), vmem(wide)],
        7 * TILES + 3,
    )
    d_q = exchange(d_q)
    layer_out, d_normed = call(
        rows_kernel,
        (),
        (attn_rows, d_q, d_gated_rows, tokens, w_out, w_in),
        [(own, BF16), (own, F32)],
        [vmem(by_head), vmem(by_head), vmem(by_head), vmem(own), vmem(square), vmem(square), vmem(square)]
        + [vmem(own), vmem(own, F32)],
        9,
    )
    d_kv, cols_b = call(
        key_kernel,
        info,
        (dkv, dkv_far, slope),
        [(wide, BF16), (across, BF16)],
        [vmem(wide), vmem(wide), vmem(wide), vmem(wide), vmem(across)],
        4 * TILES + 1,
    )
    d_kv = exchange(d_kv)
    rows = 4 * HD // groups
    pieces = call(
        functools.partial(pieces_kernel, groups),
        (group.reshape(1),),
        (cols_a, cols_b, normed),
        [((rows, width), BF16)] * groups,
        [vmem(across), vmem(across), vmem((SPAN, width)), vmem((4 * HD, width))],
        TILES // 2 + 2 + groups,
    )
    pieces = [pieces[0]] + [
        lax.ppermute(pieces[mask], "g", [(i, i ^ mask) for i in range(groups)]) for mask in range(1, groups)
    ]
    grad_tokens, grad_w_in = call(
        functools.partial(last_kernel, groups),
        (),
        (d_kv, d_normed, tokens, grad_out, w_in, *pieces),
        [(own, BF16), ((rows, width), F32)],
        [vmem((HEADS, count, 2 * HD)), vmem(own, F32), vmem(own), vmem(own), vmem(square), vmem(square)]
        + [vmem((groups, rows, width)), vmem(own), vmem((rows, width), F32)],
        8 + groups,
    )
    parts = groups // 4
    if parts > 1:
        perm = [
            (i * HEADS + j, ((i // parts) * HEADS + j) * parts + i % parts)
            for i in range(groups)
            for j in range(HEADS)
        ]
        grad_w_in = lax.ppermute(grad_w_in, ("g", "h"), perm)
    return (layer_out, grad_tokens, grad_w_in)


def solution(mesh):
    groups = mesh.shape["seq"] // HEADS
    split = Mesh(mesh.devices.reshape(groups, HEADS), ("g", "h"))
    rows = P(("g", "h"), None)
    return jax.shard_map(
        functools.partial(per_device, groups),
        mesh=split,
        in_specs=(rows, P(), P(), P(), P(), rows),
        out_specs=(rows, rows, rows),
        check_vma=False,
    )
```

time: 630 us -> 166 us (0.26)
  the two profiles are of different devices: /device:TPU:0 before, /device:TPU:18 now
where the time goes in v1:
time: 166 us; the launch traced here: 165 us
  Pallas kernels  74.4 us (45%)
  starting transfers between devices  49.1 us (30%)
  waiting for transfers between devices  26 us (16%)
  blocking collectives  8.09 us (5%)
  local copies, waits for them, and re-layouts  5.53 us (3%)
    pallas_call x14, Pallas kernels, call(): pl.pallas_call(kernel, out_shape=[jax.ShapeDtypeStruct(*out) for out in o...  74.4 us
    all_to_all x4, starting transfers between devices, exchange(): return lax.all_to_all(x, 'h', 0, 0, tiled=True)  18.6 us
    ppermute x3, waiting for transfers between devices, per_device(): lax.ppermute(pieces[mask], 'g', [(i, i ^ mask) for i in range(groups)])  17 us
    ppermute x1, starting transfers between devices, per_device(): lax.ppermute(dkv_far, 'g', [(i + 1, i) for i in range(groups - 1)])  12.7 us
    ppermute x3, starting transfers between devices, onward(): return lax.ppermute(x, 'g', [(i, i + 1) for i in range(groups - 1)])  8.87 us
    all_to_all x1, blocking collectives, exchange(): return lax.all_to_all(x, 'h', 0, 0, tiled=True)  8.09 us
    ppermute x9, starting transfers between devices, swap(): return lax.ppermute(x, 'h', [(i, i ^ mask) for i in range(HEADS)])  5.4 us
    unnamed x26, local copies, waits for them, and re-layouts  4.93 us
  transfers between devices with their start and end apart: 20, of which 10 were waited for; matrix products, arithmetic and copies ran while one was open for 1% of the time, Pallas kernels for 34%

profile of v1, /device:TPU:18, one launch (start us, length us, event | category | flops | bytes accessed | tf_op | source)
XLA Modules:
  0.0 165.3 jit_solution(9900049759152380504)
XLA Ops:
  1.3 1.5 collective-permute-start.1
  3.9 3.6 %shard_map.85 = (bf16[2048,1024]{1,0:T(8,128)(2,1)}, bf16[2048,512]{1,0:T(8,128)(2,1)}, bf16[2048,512]{1,0:T(8,128)(2,1)}, bf16[512,256]{1,0:T(8,128)(2,1)S(1)}) custom-call(s32[1]{0:T(128)} %bitcast.head_ref, bf16[256,1024]{1,0:T(8,128)(2,1)S(1)} %copy-done.3, bf16[256,1024]{1,0:T(8,128)(2,1)S(1)} %collective-permute-done.2.refs_1_, bf16[1024,4096]{1,0:T(8,128)(2,1)} %w_in_ref.3), custom_call_target="tpu_custom_call" | custom-call | tf_op jit(solution)/shard_map/pallas_call | solution.py:614
  7.5 3.5 %collective-permute-start.3 = (bf16[512,256]{1,0:T(8,128)(2,1)S(1)}, bf16[512,256]{1,0:T(8,128)(2,1)S(1)}, u32[]{:S(2)}, u32[]{:S(2)}) collective-permute-start(bf16[512,256]{1,0:T(8,128)(2,1)S(1)} %get-tuple-element.38.after_ref), channel_id=1, source_target_pairs={{0,8},{8,16},{16,24},{1,9},{9,17},{17,25},{2,10},{10,18},{18,26},{... | collective-permute-start | bytes 786440 | tf_op jit(solution)/shard_map/ppermute | solution.py:640
  11.0 3.0 %shard_map.86.b_ref.dg_ref = bf16[8,256,128]{2,1,0:T(8,128)(2,1)} custom-call(bf16[256,1024]{1,0:T(8,128)(2,1)S(1)} %copy-done.7, bf16[1024,1024]{1,0:T(8,128)(2,1)} %w_out_ref.1, bf16[512,256]{1,0:T(8,128)(2,1)S(1)} %get-tuple-element.38.after_ref), custom_call_target="tpu_custom_call" | custom-call | tf_op jit(solution)/shard_map/pallas_call | solution.py:614
  14.0 1.2 collective-permute-done.x_ref
  15.5 2.2 %collective-permute-done.3.a_ref.kva_ref = bf16[512,256]{1,0:T(8,128)(2,1)S(1)} collective-permute-done((bf16[512,256]{1,0:T(8,128)(2,1)S(1)}, bf16[512,256]{1,0:T(8,128)(2,1)S(1)}, u32[]{:S(2)}, u32[]{:S(2)}) %collective-permute-start.3) | collective-permute-done | bytes 262176 | tf_op jit(solution)/shard_map/ppermute | solution.py:640
  18.4 1.5 collective-permute-start.4
  21.5 5.0 %shard_map.88 = (bf16[2048,1024]{1,0:T(8,128)(2,1)}, bf16[2048,512]{1,0:T(8,128)(2,1)}, bf16[2048,512]{1,0:T(8,128)(2,1)}, bf16[1024,256]{1,0:T(8,128)(2,1)S(1)}) custom-call(s32[1]{0:T(128)} %bitcast.head_ref, bf16[256,1024]{1,0:T(8,128)(2,1)S(1)} %get-tuple-element.41.refs_0_, ...), custom_call_target="tpu_custom_call", output_to_operand_aliasing={{0}: (6, {}), {1}: (7, {}), {2}: (8, {})} | custom-call | tf_op jit(solution)/shard_map/pallas_call | solution.py:614
  26.7 1.3 collective-permute-done.5.b_ref
  28.5 3.9 %all-to-all-start = ((bf16[8,256,128]{2,1,0:T(8,128)(2,1)}), bf16[8,256,128]{2,1,0:T(8,128)(2,1)S(1)}, u32[]{:S(2)}, u32[]{:S(2)}) async-start(bf16[8,256,128]{2,1,0:T(8,128)(2,1)} %shard_map.86.b_ref.dg_ref), calls=%async_computation | async-start | bytes 1048576 | tf_op jit(solution)/shard_map/all_to_all | solution.py:637
  32.5 3.5 %collective-permute-start.10 = (bf16[1024,256]{1,0:T(8,128)(2,1)S(1)}, bf16[1024,256]{1,0:T(8,128)(2,1)S(1)}, u32[]{:S(2)}, u32[]{:S(2)}) collective-permute-start(bf16[1024,256]{1,0:T(8,128)(2,1)S(1)} %get-tuple-element.46.after_ref), channel_id=1, source_target_pairs={{0,8},{8,16},{16,24},{1,9},{9,17},{17,25},{2,10},{10,18},{18,26},{... | collective-permute-start | bytes 1572872 | tf_op jit(solution)/shard_map/ppermute | solution.py:640
  36.1 3.6 %shard_map.90 = (bf16[2048,1024]{1,0:T(8,128)(2,1)}, bf16[2048,512]{1,0:T(8,128)(2,1)}, bf16[2048,512]{1,0:T(8,128)(2,1)}, bf16[512,256]{1,0:T(8,128)(2,1)S(1)}) custom-call(s32[1]{0:T(128)} %bitcast.head_ref, bf16[128,1024]{1,0:T(8,128)(2,1)S(1)} %get-tuple-element.47.refs_0_, ...), custom_call_target="tpu_custom_call", output_to_operand_aliasing={{0}: (6, {}), {1}: (7, {}), {2}: (8, {})} | custom-call | tf_op jit(solution)/shard_map/pallas_call | solution.py:614
  39.7 1.9 %collective-permute-start.11 = (bf16[512,256]{1,0:T(8,128)(2,1)S(1)}, bf16[512,256]{1,0:T(8,128)(2,1)S(1)}, u32[]{:S(2)}, u32[]{:S(2)}) collective-permute-start(bf16[512,256]{1,0:T(8,128)(2,1)S(1)} %get-tuple-element.53), channel_id=1, source_target_pairs={{0,8},{8,16},{16,24},{1,9},{9,17},{17,25},{2,10},{10,18},{18,26},{... | collective-permute-start | bytes 786440 | tf_op jit(solution)/shard_map/ppermute | solution.py:640
  42.9 8.8 %shard_map.91.near_ref = f32[2048,128]{1,0:T(8,128)S(1)} custom-call(s32[17]{0:T(128)S(1)} %get-tuple-element.79.lo_ref, s32[17]{0:T(128)S(1)} %get-tuple-element.78.nv_ref, bf16[2048,512]{1,0:T(8,128)(2,1)} %get-tuple-element.52.act_ref), custom_call_target="tpu_custom_call" | custom-call | tf_op jit(solution)/shard_map/pallas_call | solution.py:614
  52.7 1.2 collective-permute-done.11.kvc_ref
  54.0 6.3 %shard_map.92 = (bf16[2048,128]{1,0:T(8,128)(2,1)}, f32[8,16,256]{2,1,0:T(8,128)S(1)}) custom-call(s32[1]{0:T(128)} %bitcast.head_ref, s32[17]{0:T(128)S(1)} %get-tuple-element.79.lo_ref, s32[17]{0:T(128)S(1)} %get-tuple-element.78.nv_ref, bf16[2048,512]{1,0:T(8,128)(2,1)} %get-tuple-element.52.act_ref, ...), custom_call_target="tpu_custom_call" | custom-call | tf_op jit(solution)/shard_map/pallas_call | solution.py:614
  60.3 8.1 %all_to_all.25.sum_ref = f32[8,16,256]{2,1,0:T(8,128)S(1)} all-to-all(f32[8,16,256]{2,1,0:T(8,128)S(1)} %get-tuple-element.55), channel_id=1, replica_groups=mesh['g'=4,'h'=8] {'h'}, dimensions={0} | all-to-all | bytes 262144 | tf_op jit(solution)/shard_map/all_to_all | solution.py:637
  69.4 6.1 %shard_map.93 = (f32[128,2048]{1,0:T(8,128)}, bf16[2048,256]{1,0:T(8,128)(2,1)}) custom-call(s32[1]{0:T(128)} %bitcast.head_ref, s32[17]{0:T(128)S(1)} %get-tuple-element.79.lo_ref, s32[17]{0:T(128)S(1)} %get-tuple-element.78.nv_ref, f32[8,16,256]{2,1,0:T(8,128)S(1)} %all_to_all.25.sum_ref, bf16[2048,512]{1,0:T(8,128)(2,1)} %get-tuple-element.52.act_ref, ...), custom_call_target="tpu_custom_call" | custom-call | tf_op jit(solution)/shard_map/pallas_call | solution.py:614
  75.5 12.7 %collective-permute-start.12 = (bf16[2048,256]{1,0:T(8,128)(2,1)}, bf16[2048,256]{1,0:T(8,128)(2,1)S(1)}, u32[]{:S(2)}, u32[]{:S(2)}) collective-permute-start(bf16[2048,256]{1,0:T(8,128)(2,1)} %get-tuple-element.61), channel_id=1, source_target_pairs={{8,0},{16,8},{24,16},{9,1},{17,9},{25,17},{10,2},{18,10},{26,18},{... | collective-permute-start | bytes 3145736 | tf_op jit(solution)/shard_map/ppermute | solution.py:697
  88.2 4.9 %all-to-all-start.1 = ((bf16[8,256,128]{2,1,0:T(8,128)(2,1)}), bf16[8,256,128]{2,1,0:T(8,128)(2,1)S(1)}, u32[]{:S(2)}, u32[]{:S(2)}) async-start(bf16[8,256,128]{2,1,0:T(8,128)(2,1)} %bitcast.4), calls=%async_computation.1 | async-start | bytes 1048576 | tf_op jit(solution)/shard_map/all_to_all | solution.py:637
  93.1 17.1 %shard_map.94 = (bf16[2048,128]{1,0:T(8,128)(2,1)}, bf16[256,2048]{1,0:T(8,128)(2,1)}, bf16[2048,256]{1,0:T(8,128)(2,1)}) custom-call(s32[17]{0:T(128)S(1)} %get-tuple-element.79.lo_ref, s32[17]{0:T(128)S(1)} %get-tuple-element.78.nv_ref, f32[8,16,256]{2,1,0:T(8,128)S(1)} %all_to_all.25.sum_ref, bf16[2048,512]{1,0:T(8,128)(2,1)} %get-tuple-element.52.act_ref, ...), custom_call_target="tpu_custom_call" | custom-call | tf_op jit(solution)/shard_map/pallas_call | solution.py:614
  110.2 4.2 %all-to-all-start.3 = ((bf16[8,256,128]{2,1,0:T(8,128)(2,1)}), bf16[8,256,128]{2,1,0:T(8,128)(2,1)S(1)}, u32[]{:S(2)}, u32[]{:S(2)}) async-start(bf16[8,256,128]{2,1,0:T(8,128)(2,1)} %bitcast.5), calls=%async_computation.3 | async-start | bytes 1048576 | tf_op jit(solution)/shard_map/all_to_all | solution.py:637
  115.4 4.7 %shard_map.96 = (bf16[2048,256]{1,0:T(8,128)(2,1)}, bf16[256,2048]{1,0:T(8,128)(2,1)}) custom-call(s32[17]{0:T(128)S(1)} %get-tuple-element.79.lo_ref, s32[17]{0:T(128)S(1)} %get-tuple-element.78.nv_ref, bf16[2048,256]{1,0:T(8,128)(2,1)} %get-tuple-element.60.own_ref, bf16[2048,256]{1,0:T(8,128)(2,1)} %copy-done.9, bf16[2048,512]{1,0:T(8,128)(2,1)} %get-tuple-element.56.slope_ref), custom_call_target="tpu_custom_call" | custom-call | tf_op jit(solution)/shard_map/pallas_call | solution.py:614
  120.1 2.6 %all-to-all-done.3.q_ref = bf16[8,256,128]{2,1,0:T(8,128)(2,1)S(1)} async-done(((bf16[8,256,128]{2,1,0:T(8,128)(2,1)}), bf16[8,256,128]{2,1,0:T(8,128)(2,1)S(1)}, u32[]{:S(2)}, u32[]{:S(2)}) %all-to-all-start.3) | async-done | bytes 524320 | tf_op jit(solution)/shard_map/all_to_all | solution.py:637
  122.7 5.6 %all-to-all-start.4 = ((bf16[8,256,256]{2,1,0:T(8,128)(2,1)}), bf16[8,256,256]{2,1,0:T(8,128)(2,1)}, u32[]{:S(2)}, u32[]{:S(2)}) async-start(bf16[8,256,256]{2,1,0:T(8,128)(2,1)} %bitcast.6), calls=%async_computation.4 | async-start | bytes 2097152 | tf_op jit(solution)/shard_map/all_to_all | solution.py:637
  128.3 4.8 %shard_map.97 = (bf16[128,1024]{1,0:T(8,128)(2,1)S(1)}, bf16[128,1024]{1,0:T(8,128)(2,1)S(1)}, bf16[128,1024]{1,0:T(8,128)(2,1)S(1)}, bf16[128,1024]{1,0:T(8,128)(2,1)S(1)}) custom-call(s32[1]{0:T(128)} %bitcast.7.group_ref, bf16[256,2048]{1,0:T(8,128)(2,1)} %get-tuple-element.64.a_ref, bf16[256,2048]{1,0:T(8,128)(2,1)} %get-tuple-element.65.b_ref, ...), custom_call_target="tpu_custom_call" | custom-call | tf_op jit(solution)/shard_map/pallas_call | solution.py:614
  133.2 1.4 collective-permute-start.14
  134.6 2.0 %collective-permute-start.15 = (bf16[128,1024]{1,0:T(8,128)(2,1)S(1)}, bf16[128,1024]{1,0:T(8,128)(2,1)S(1)}, u32[]{:S(2)}, u32[]{:S(2)}) collective-permute-start(bf16[128,1024]{1,0:T(8,128)(2,1)S(1)} %get-tuple-element.70), channel_id=1, source_target_pairs={{0,24},{8,16},{16,8},{24,0},{1,25},{9,17},{17,9},{25,1},{2,26},{10... | collective-permute-start | bytes 786440 | tf_op jit(solution)/shard_map/ppermute | solution.py:737
  136.6 5.9 %shard_map.95 = (bf16[256,1024]{1,0:T(8,128)(2,1)}, f32[256,1024]{1,0:T(8,128)}) custom-call(bf16[8,256,128]{2,1,0:T(8,128)(2,1)S(1)} %all-to-all-done.1.attn_ref, bf16[8,256,128]{2,1,0:T(8,128)(2,1)S(1)} %all-to-all-done.3.q_ref, bf16[8,256,128]{2,1,0:T(8,128)(2,1)} %shard_map.86.b_ref.dg_ref, bf16[256,1024]{1,0:T(8,128)(2,1)} %tokens_ref.3, ...), custom_call_target="tpu_custom_call" | custom-call | tf_op jit(solution)/shard_map/pallas_call | solution.py:614
  143.2 9.2 %collective-permute-done.14.refs_2_ = bf16[128,1024]{1,0:T(8,128)(2,1)S(1)} collective-permute-done((bf16[128,1024]{1,0:T(8,128)(2,1)S(1)}, bf16[128,1024]{1,0:T(8,128)(2,1)S(1)}, u32[]{:S(2)}, u32[]{:S(2)}) %collective-permute-start.14) | collective-permute-done | bytes 262176 | tf_op jit(solution)/shard_map/ppermute | solution.py:737
  152.4 7.2 %collective-permute-done.15.refs_3_ = bf16[128,1024]{1,0:T(8,128)(2,1)S(1)} collective-permute-done((bf16[128,1024]{1,0:T(8,128)(2,1)S(1)}, bf16[128,1024]{1,0:T(8,128)(2,1)S(1)}, u32[]{:S(2)}, u32[]{:S(2)}) %collective-permute-start.15) | collective-permute-done | bytes 262176 | tf_op jit(solution)/shard_map/ppermute | solution.py:737
  159.6 5.5 %shard_map.98 = (bf16[256,1024]{1,0:T(8,128)(2,1)}, f32[128,1024]{1,0:T(8,128)}) custom-call(bf16[8,256,256]{2,1,0:T(8,128)(2,1)} %all-to-all-done.4.kv_ref, f32[256,1024]{1,0:T(8,128)} %get-tuple-element.63.dn_ref, bf16[256,1024]{1,0:T(8,128)(2,1)S(1)} %copy-done.4, bf16[256,1024]{1,0:T(8,128)(2,1)} %grad_ref.1, bf16[1024,4096]{1,0:T(8,128)(2,1)} %w_in_ref.3, ...), custom_call_target="tpu_custom_call" | custom-call | tf_op jit(solution)/shard_map/pallas_call | solution.py:614
  (58 shorter events, 10.2 us)
Async XLA Ops:
  0.6 2.2 %collective-permute-start.2 = (bf16[256,1024]{1,0:T(8,128)(2,1)}, bf16[256,1024]{1,0:T(8,128)(2,1)S(1)}, u32[]{:S(2)}, u32[]{:S(2)}) collective-permute-start(bf16[256,1024]{1,0:T(8,128)(2,1)} %tokens_ref.3), channel_id=1, source_target_pairs={{0,1},{1,0},{2,3},{3,2},{4,5},{5,4},{6,7},{7,6},{8,9},{9,8},{10,11... | collective-permute-start | bytes 1572872 | tf_op jit(solution)/shard_map/ppermute | solution.py:633
  0.7 14.5 %collective-permute-start = (bf16[256,1024]{1,0:T(8,128)(2,1)}, bf16[256,1024]{1,0:T(8,128)(2,1)S(1)}, u32[]{:S(2)}, u32[]{:S(2)}) collective-permute-start(bf16[256,1024]{1,0:T(8,128)(2,1)} %tokens_ref.3), channel_id=1, source_target_pairs={{0,2},{1,3},{2,0},{3,1},{4,6},{5,7},{6,4},{7,5},{8,10},{9,11},{10,... | collective-permute-start | bytes 1572872 | tf_op jit(solution)/shard_map/ppermute | solution.py:633
  1.3 14.2 %collective-permute-start.1 = (bf16[256,1024]{1,0:T(8,128)(2,1)}, bf16[256,1024]{1,0:T(8,128)(2,1)S(1)}, u32[]{:S(2)}, u32[]{:S(2)}) collective-permute-start(bf16[256,1024]{1,0:T(8,128)(2,1)} %tokens_ref.3), channel_id=1, source_target_pairs={{0,4},{1,5},{2,6},{3,7},{4,0},{5,1},{6,2},{7,3},{8,12},{9,13},{10,... | collective-permute-start | bytes 1572872 | tf_op jit(solution)/shard_map/ppermute | solution.py:633
  2.8 1.1 copy-start.3
  3.9 7.1 %copy-start.7 = (bf16[256,1024]{1,0:T(8,128)(2,1)S(1)}, bf16[256,1024]{1,0:T(8,128)(2,1)}, u32[]{:S(2)}) copy-start(bf16[256,1024]{1,0:T(8,128)(2,1)} %grad_ref.1) | copy-start | bytes 1572868
  7.5 13.0 %copy-start.11 = (s32[16]{0:T(128)S(1)}, s32[16]{0:T(128)}, u32[]{:S(2)}) copy-start(s32[16]{0:T(128)} %param.9) | copy-start | bytes 196
  7.5 10.2 %collective-permute-start.3 = (bf16[512,256]{1,0:T(8,128)(2,1)S(1)}, bf16[512,256]{1,0:T(8,128)(2,1)S(1)}, u32[]{:S(2)}, u32[]{:S(2)}) collective-permute-start(bf16[512,256]{1,0:T(8,128)(2,1)S(1)} %get-tuple-element.38.after_ref), channel_id=1, source_target_pairs={{0,8},{8,16},{16,24},{1,9},{9,17},{17,25},{2,10},{10,18},{18,26},{... | collective-permute-start | bytes 786440 | tf_op jit(solution)/shard_map/ppermute | solution.py:640
  17.8 3.7 %copy-start.6 = (bf16[256,1024]{1,0:T(8,128)(2,1)}, bf16[256,1024]{1,0:T(8,128)(2,1)S(1)}, u32[]{:S(2)}) copy-start(bf16[256,1024]{1,0:T(8,128)(2,1)S(1)} %get-tuple-element.42.refs_2_) | copy-start | bytes 1572868
  17.8 2.9 %collective-permute-start.6 = (bf16[256,1024]{1,0:T(8,128)(2,1)S(1)}, bf16[256,1024]{1,0:T(8,128)(2,1)S(1)}, u32[]{:S(2)}, u32[]{:S(2)}) collective-permute-start(bf16[256,1024]{1,0:T(8,128)(2,1)S(1)} %get-tuple-element.41.refs_0_), channel_id=1, source_target_pairs={{0,1},{1,0},{2,3},{3,2},{4,5},{5,4},{6,7},{7,6},{8,9},{9,8},{10,11... | collective-permute-start | bytes 1572872 | tf_op jit(solution)/shard_map/ppermute | solution.py:633
  17.9 2.8 %collective-permute-start.7 = (bf16[256,1024]{1,0:T(8,128)(2,1)S(1)}, bf16[256,1024]{1,0:T(8,128)(2,1)S(1)}, u32[]{:S(2)}, u32[]{:S(2)}) collective-permute-start(bf16[256,1024]{1,0:T(8,128)(2,1)S(1)} %get-tuple-element.42.refs_2_), channel_id=1, source_target_pairs={{0,1},{1,0},{2,3},{3,2},{4,5},{5,4},{6,7},{7,6},{8,9},{9,8},{10,11... | collective-permute-start | bytes 1572872 | tf_op jit(solution)/shard_map/ppermute | solution.py:633
  18.4 8.3 %collective-permute-start.4 = (bf16[128,1024]{1,0:T(8,128)(2,1)S(1)}, bf16[128,1024]{1,0:T(8,128)(2,1)S(1)}, u32[]{:S(2)}, u32[]{:S(2)}) collective-permute-start(bf16[128,1024]{1,0:T(8,128)(2,1)S(1)} %get-tuple-element.39), channel_id=1, source_target_pairs={{0,4},{1,5},{2,6},{3,7},{4,0},{5,1},{6,2},{7,3},{8,12},{9,13},{10,... | collective-permute-start | bytes 786440 | tf_op jit(solution)/shard_map/ppermute | solution.py:633
  19.9 8.0 %collective-permute-start.5 = (bf16[128,1024]{1,0:T(8,128)(2,1)S(1)}, bf16[128,1024]{1,0:T(8,128)(2,1)S(1)}, u32[]{:S(2)}, u32[]{:S(2)}) collective-permute-start(bf16[128,1024]{1,0:T(8,128)(2,1)S(1)} %get-tuple-element.40), channel_id=1, source_target_pairs={{0,2},{1,3},{2,0},{3,1},{4,6},{5,7},{6,4},{7,5},{8,10},{9,11},{10,... | collective-permute-start | bytes 786440 | tf_op jit(solution)/shard_map/ppermute | solution.py:633
  28.0 8.1 %collective-permute-start.8 = (bf16[128,1024]{1,0:T(8,128)(2,1)S(1)}, bf16[128,1024]{1,0:T(8,128)(2,1)S(1)}, u32[]{:S(2)}, u32[]{:S(2)}) collective-permute-start(bf16[128,1024]{1,0:T(8,128)(2,1)S(1)} %get-tuple-element.47.refs_0_), channel_id=1, source_target_pairs={{0,1},{1,0},{2,3},{3,2},{4,5},{5,4},{6,7},{7,6},{8,9},{9,8},{10,11... | collective-permute-start | bytes 786440 | tf_op jit(solution)/shard_map/ppermute | solution.py:633
  28.0 8.0 %collective-permute-start.9 = (bf16[128,1024]{1,0:T(8,128)(2,1)S(1)}, bf16[128,1024]{1,0:T(8,128)(2,1)S(1)}, u32[]{:S(2)}, u32[]{:S(2)}) collective-permute-start(bf16[128,1024]{1,0:T(8,128)(2,1)S(1)} %get-tuple-element.48.refs_1_), channel_id=1, source_target_pairs={{0,1},{1,0},{2,3},{3,2},{4,5},{5,4},{6,7},{7,6},{8,9},{9,8},{10,11... | collective-permute-start | bytes 786440 | tf_op jit(solution)/shard_map/ppermute | solution.py:633
  28.5 24.2 %all-to-all-start = ((bf16[8,256,128]{2,1,0:T(8,128)(2,1)}), bf16[8,256,128]{2,1,0:T(8,128)(2,1)S(1)}, u32[]{:S(2)}, u32[]{:S(2)}) async-start(bf16[8,256,128]{2,1,0:T(8,128)(2,1)} %shard_map.86.b_ref.dg_ref), calls=%async_computation | async-start | bytes 1048576 | tf_op jit(solution)/shard_map/all_to_all | solution.py:637
  32.5 21.5 %collective-permute-start.10 = (bf16[1024,256]{1,0:T(8,128)(2,1)S(1)}, bf16[1024,256]{1,0:T(8,128)(2,1)S(1)}, u32[]{:S(2)}, u32[]{:S(2)}) collective-permute-start(bf16[1024,256]{1,0:T(8,128)(2,1)S(1)} %get-tuple-element.46.after_ref), channel_id=1, source_target_pairs={{0,8},{8,16},{16,24},{1,9},{9,17},{17,25},{2,10},{10,18},{18,26},{... | collective-permute-start | bytes 1572872 | tf_op jit(solution)/shard_map/ppermute | solution.py:640
  36.1 5.5 %copy-start.12 = (s32[16]{0:T(128)S(1)}, s32[16]{0:T(128)}, u32[]{:S(2)}) copy-start(s32[16]{0:T(128)} %param.10) | copy-start | bytes 196
  39.7 14.3 %collective-permute-start.11 = (bf16[512,256]{1,0:T(8,128)(2,1)S(1)}, bf16[512,256]{1,0:T(8,128)(2,1)S(1)}, u32[]{:S(2)}, u32[]{:S(2)}) collective-permute-start(bf16[512,256]{1,0:T(8,128)(2,1)S(1)} %get-tuple-element.53), channel_id=1, source_target_pairs={{0,8},{8,16},{16,24},{1,9},{9,17},{17,25},{2,10},{10,18},{18,26},{... | collective-permute-start | bytes 786440 | tf_op jit(solution)/shard_map/ppermute | solution.py:640
  51.7 1.0 copy-start.5
  52.7 1.3 copy-start
  54.0 6.3 %copy-start.8 = (bf16[1024,256]{1,0:T(8,128)(2,1)}, bf16[1024,256]{1,0:T(8,128)(2,1)S(1)}, u32[]{:S(2)}) copy-start(bf16[1024,256]{1,0:T(8,128)(2,1)S(1)} %collective-permute-done.10.kvb_ref) | copy-start | bytes 1572868
  68.4 1.0 copy-start.1
  69.4 23.6 %copy-start.2 = (bf16[8,256,128]{2,1,0:T(8,128)(2,1)S(1)}, bf16[8,256,128]{2,1,0:T(8,128)(2,1)}, u32[]{:S(2)}) copy-start(bf16[8,256,128]{2,1,0:T(8,128)(2,1)} %copy-done) | copy-start | bytes 1572868
  75.5 38.9 %collective-permute-start.12 = (bf16[2048,256]{1,0:T(8,128)(2,1)}, bf16[2048,256]{1,0:T(8,128)(2,1)S(1)}, u32[]{:S(2)}, u32[]{:S(2)}) collective-permute-start(bf16[2048,256]{1,0:T(8,128)(2,1)} %get-tuple-element.61), channel_id=1, source_target_pairs={{8,0},{16,8},{24,16},{9,1},{17,9},{25,17},{10,2},{18,10},{26,18},{... | collective-permute-start | bytes 3145736 | tf_op jit(solution)/shard_map/ppermute | solution.py:697
  88.2 22.0 %all-to-all-start.1 = ((bf16[8,256,128]{2,1,0:T(8,128)(2,1)}), bf16[8,256,128]{2,1,0:T(8,128)(2,1)S(1)}, u32[]{:S(2)}, u32[]{:S(2)}) async-start(bf16[8,256,128]{2,1,0:T(8,128)(2,1)} %bitcast.4), calls=%async_computation.1 | async-start | bytes 1048576 | tf_op jit(solution)/shard_map/all_to_all | solution.py:637
  110.2 12.5 %all-to-all-start.3 = ((bf16[8,256,128]{2,1,0:T(8,128)(2,1)}), bf16[8,256,128]{2,1,0:T(8,128)(2,1)S(1)}, u32[]{:S(2)}, u32[]{:S(2)}) async-start(bf16[8,256,128]{2,1,0:T(8,128)(2,1)} %bitcast.5), calls=%async_computation.3 | async-start | bytes 1048576 | tf_op jit(solution)/shard_map/all_to_all | solution.py:637
  114.4 1.0 copy-start.9
  122.7 36.9 %all-to-all-start.4 = ((bf16[8,256,256]{2,1,0:T(8,128)(2,1)}), bf16[8,256,256]{2,1,0:T(8,128)(2,1)}, u32[]{:S(2)}, u32[]{:S(2)}) async-start(bf16[8,256,256]{2,1,0:T(8,128)(2,1)} %bitcast.6), calls=%async_computation.4 | async-start | bytes 2097152 | tf_op jit(solution)/shard_map/all_to_all | solution.py:637
  133.1 10.1 %collective-permute-start.13 = (bf16[128,1024]{1,0:T(8,128)(2,1)S(1)}, bf16[128,1024]{1,0:T(8,128)(2,1)S(1)}, u32[]{:S(2)}, u32[]{:S(2)}) collective-permute-start(bf16[128,1024]{1,0:T(8,128)(2,1)S(1)} %get-tuple-element.68), channel_id=1, source_target_pairs={{0,8},{8,0},{16,24},{24,16},{1,9},{9,1},{17,25},{25,17},{2,10},{10... | collective-permute-start | bytes 786440 | tf_op jit(solution)/shard_map/ppermute | solution.py:737
  133.2 19.2 %collective-permute-start.14 = (bf16[128,1024]{1,0:T(8,128)(2,1)S(1)}, bf16[128,1024]{1,0:T(8,128)(2,1)S(1)}, u32[]{:S(2)}, u32[]{:S(2)}) collective-permute-start(bf16[128,1024]{1,0:T(8,128)(2,1)S(1)} %get-tuple-element.69), channel_id=1, source_target_pairs={{0,16},{8,24},{16,0},{24,8},{1,17},{9,25},{17,1},{25,9},{2,18},{10... | collective-permute-start | bytes 786440 | tf_op jit(solution)/shard_map/ppermute | solution.py:737
  134.6 25.0 %copy-start.4 = (bf16[256,1024]{1,0:T(8,128)(2,1)S(1)}, bf16[256,1024]{1,0:T(8,128)(2,1)}, u32[]{:S(2)}) copy-start(bf16[256,1024]{1,0:T(8,128)(2,1)} %tokens_ref.3) | copy-start | bytes 1572868
  134.6 25.0 %collective-permute-start.15 = (bf16[128,1024]{1,0:T(8,128)(2,1)S(1)}, bf16[128,1024]{1,0:T(8,128)(2,1)S(1)}, u32[]{:S(2)}, u32[]{:S(2)}) collective-permute-start(bf16[128,1024]{1,0:T(8,128)(2,1)S(1)} %get-tuple-element.70), channel_id=1, source_target_pairs={{0,24},{8,16},{16,8},{24,0},{1,25},{9,17},{17,9},{25,1},{2,26},{10... | collective-permute-start | bytes 786440 | tf_op jit(solution)/shard_map/ppermute | solution.py:737
  (1 other events, 0.8 us)

commit v2 on v0

v2 whole, which is shorter than its diff:
```python
import functools

import jax
import jax.numpy as jnp
from jax import lax
from jax.experimental import pallas as pl
from jax.experimental.pallas import tpu as pltpu
from jax.sharding import Mesh, PartitionSpec as P

HEADS = 8
HD = 128
BLK = 128
MAXB = 16
SPAN = MAXB * BLK
TILE = 256
TILES = SPAN // TILE
CHUNK = 512
CHUNKS = SPAN // CHUNK
HALF = 0.5 * HD ** (-0.5)

eps = 1e-05

NT = (((1,), (1,)), ((), ()))
F32, BF16 = jnp.float32, jnp.bfloat16

U, Q, V, K = (slice(i * HD, (i + 1) * HD) for i in range(4))
PLACE = (0, 2, 1, 3)
UQ, VK = slice(0, 2 * HD), slice(2 * HD, 4 * HD)


def info_kernel(counts_ref, tails_ref, lo_ref, nv_ref, at_ref):
    group = lax.axis_index("g").astype(jnp.int32)
    at_ref[0] = group
    at_ref[1] = lax.axis_index("h").astype(jnp.int32)
    base = group * MAXB
    for j in range(MAXB + 1):
        lo_ref[j] = j * BLK
        nv_ref[j] = BLK

    def user(n, start):
        end = start + counts_ref[n]

        def block(j, carry):
            lo_ref[j] = (start - base) * BLK
            nv_ref[j] = jnp.where(j == end - 1 - base, tails_ref[n], BLK)
            return carry

        lax.fori_loop(jnp.maximum(start - base, 0), jnp.minimum(end - base, MAXB + 1), block, 0)
        return end

    lax.fori_loop(0, counts_ref.shape[0], user, jnp.int32(0))


def by_half(t, ref, shape, dim):
    side = lax.broadcasted_iota(jnp.int32, shape, dim)
    return jnp.where(side < BLK, ref[2 * t], ref[2 * t + 1])


def valid_rows(t, nv_ref):
    row = lax.broadcasted_iota(jnp.int32, (TILE, 1), 0)
    return (row & (BLK - 1)) < by_half(t, nv_ref, (TILE, 1), 0)


def rows_at(t):
    return pl.ds(pl.multiple_of(t * TILE, TILE), TILE)


def chunk_at(c):
    return pl.ds(pl.multiple_of(c * CHUNK, CHUNK), CHUNK)


def lanes_at(i):
    return pl.ds(pl.multiple_of(i * HD, HD), HD)


def norm_rows(x):
    return x * lax.rsqrt(jnp.mean(x * x, axis=-1, keepdims=True) + eps)


def silu_and_slope(pre):
    s = 0.5 + 0.5 * jnp.tanh(0.5 * pre)
    return (pre * s).astype(BF16), (s * (1.0 + pre * (1.0 - s))).astype(BF16)


def proj_kernel(masks, pieces, first, at_ref, *refs):
    x_refs, w_ref = refs[: sum(pieces)], refs[sum(pieces)]
    head, width = at_ref[1], w_ref.shape[0]
    if first:
        normed_ref, act_ref, slope_ref, kv_ref, wh_ref = refs[-5:]
        for i in range(4):
            wh_ref[:, i * HD : (i + 1) * HD] = w_ref[:, lanes_at(PLACE[i] * (width // HD) + head)]
    else:
        normed_ref, act_ref, slope_ref, kv_ref = refs[-4:]
        wh_ref = w_ref
    for i, mask in enumerate(masks):
        parts = [ref[...] for ref in x_refs[sum(pieces[:i]) : sum(pieces[: i + 1])]]
        x = parts[0] if len(parts) == 1 else jnp.concatenate(parts, axis=0)
        rows = rows_at(head ^ mask)
        xn = norm_rows(x.astype(F32)).astype(BF16)
        normed_ref[rows, :] = xn
        act, slope = silu_and_slope(jnp.dot(xn, wh_ref[...], preferred_element_type=F32))
        act_ref[rows, :] = act
        slope_ref[rows, :] = slope
        kv_ref[i * TILE : (i + 1) * TILE, :] = act[:, VK]


def project(info, masks, chunks, w, kept):
    width, n = w.shape[0], len(masks)
    first = not kept
    pieces = tuple(len(chunk) for chunk in chunks)
    flat = [piece for chunk in chunks for piece in chunk]
    start = 2 + len(flat)
    outs = [((SPAN, width), BF16), ((SPAN, 4 * HD), BF16), ((SPAN, 4 * HD), BF16), ((n * TILE, 2 * HD), BF16)]
    if first:
        outs.append(((width, 4 * HD), BF16))
    return call(
        functools.partial(proj_kernel, masks, pieces, first),
        (info[2],),
        (*flat, w),
        outs,
        after=kept,
        aliases={start + i: i for i in range(len(kept))},
    )


def cut_kernel(x_ref, y_ref, a_ref, b_ref, x_out, y_out, x_half, y_half):
    x_half[...] = x_ref[:BLK, :]
    y_half[...] = y_ref[BLK:, :]


def gate_kernel(a_ref, b_ref, after_ref, a_out, b_out):
    pass


def d_gated_kernel(at_ref, g_ref, w_ref, after_ref, *refs):
    outs, d_s = refs[:-1], refs[-1]
    d_s[...] = lax.dot_general(g_ref[...], w_ref[...], NT, preferred_element_type=F32).astype(BF16)
    for mask in range(HEADS):
        outs[mask][...] = d_s[:, lanes_at(at_ref[1] ^ mask)]


def weigh(q, kt, v, mask):
    half = jnp.dot(q, kt, preferred_element_type=F32) * HALF
    w = half + half * jnp.tanh(half)
    w = jnp.where(mask, w, 0.0).astype(BF16)
    return jnp.dot(w, v, preferred_element_type=F32)


def fwd_own_kernel(lo_ref, nv_ref, act_ref, slope_ref, out_ref, kt_ref, qt_ref, slope_qt_ref):
    for t in range(TILES):
        rows = slice(t * TILE, (t + 1) * TILE)
        kt_ref[:, rows] = act_ref[rows, K].T
    row = lax.broadcasted_iota(jnp.int32, (TILE, CHUNK), 0)
    col = lax.broadcasted_iota(jnp.int32, (TILE, CHUNK), 1)

    def q_tile(t, carry):
        lo = by_half(t, lo_ref, (TILE, 1), 0)
        q = act_ref[rows_at(t), Q]

        def k_chunk(c, acc):
            mask = (col >= lo - c * CHUNK) & (col - row <= t * TILE - c * CHUNK)
            return acc + weigh(q, kt_ref[:, chunk_at(c)], act_ref[chunk_at(c), V], mask)

        first = jnp.maximum(lo_ref[2 * t], 0) // CHUNK
        acc = lax.fori_loop(first, t // 2 + 1, k_chunk, jnp.zeros((TILE, HD), F32))
        out_ref[rows_at(t), :] = jnp.where(valid_rows(t, nv_ref), acc, 0.0)
        return carry

    lax.fori_loop(0, TILES, q_tile, 0)
    for t in range(TILES):
        rows = slice(t * TILE, (t + 1) * TILE)
        qt_ref[:, rows] = act_ref[rows, Q].T
        slope_qt_ref[:, rows] = slope_ref[rows, Q].T


def fwd_far_kernel(
    lo_ref, nv_ref, at_ref, act_ref, kva_ref, kvb_ref, kvc_ref, near_ref, *refs
):
    dg_refs, (out_ref, sum_ref, kv_ref, kt_ref), pieces, (attn_s, dg_s) = refs[:HEADS], refs[HEADS : HEADS + 4], refs[HEADS + 4 : -2], refs[-2:]
    head = at_ref[1]
    slot = 0
    for ref in (kva_ref, kvb_ref, kvc_ref):
        for at in range(0, ref.shape[0], TILE):
            kv_ref[rows_at(slot ^ head), :] = ref[at : at + TILE, :]
            slot += 1
    for mask in range(HEADS):
        dg_s[rows_at(head ^ mask), :] = dg_refs[mask][...]
    first = jnp.minimum(lo_ref[0] + SPAN, SPAN) // CHUNK
    for t in range(TILES):
        rows = slice(t * TILE, (t + 1) * TILE)

        @pl.when(t // 2 >= first)
        def _():
            kt_ref[:, rows] = kv_ref[rows, HD:].T

    attn_s[...] = near_ref[...]
    col = lax.broadcasted_iota(jnp.int32, (TILE, CHUNK), 1)

    def q_tile(t, carry):
        lo = by_half(t, lo_ref, (TILE, 1), 0) + SPAN
        q = act_ref[rows_at(t), Q]

        def k_chunk(c, acc):
            return acc + weigh(q, kt_ref[:, chunk_at(c)], kv_ref[chunk_at(c), :HD], col >= lo - c * CHUNK)

        start = (lo_ref[2 * t] + SPAN) // CHUNK
        acc = lax.fori_loop(start, CHUNKS, k_chunk, jnp.zeros((TILE, HD), F32))
        attn_s[rows_at(t), :] += jnp.where(valid_rows(t, nv_ref), acc, 0.0)
        return carry

    lax.fori_loop(0, far_tiles(lo_ref), q_tile, 0)
    ones = jnp.ones((8, HD), BF16)
    for t in range(TILES):
        rows = slice(t * TILE, (t + 1) * TILE)
        attn = attn_s[rows, :] * (1.0 / SPAN)
        out_ref[rows, :] = attn.astype(BF16)
        d_n = dg_s[rows, :].astype(F32) * act_ref[rows, U].astype(F32)
        square = lax.dot_general(ones, (attn * attn).astype(BF16), NT, preferred_element_type=F32)
        cross = lax.dot_general(ones, (attn * d_n).astype(BF16), NT, preferred_element_type=F32)
        sum_ref[t : t + 1, :] = square[:1]
        sum_ref[TILES + t : TILES + t + 1, :] = cross[:1]
    for mask in range(HEADS):
        pieces[mask][...] = out_ref[rows_at(head ^ mask), :]


def far_tiles(lo_ref):
    return sum((lo_ref[2 * t] < 0).astype(jnp.int32) for t in range(TILES))


def row_scales(sum_refs):
    width = HEADS * HD
    total = sum_refs[0][...]
    for ref in sum_refs[1:]:
        total += ref[...]
    r = lax.rsqrt(total[:TILES] * (1.0 / width) + eps)
    c = total[TILES:] * (1.0 / width) * r
    return jnp.concatenate([r, c], axis=0).T


def place_d_gated(at_ref, dg_refs, dg_s):
    for mask in range(HEADS):
        dg_s[rows_at(at_ref[1] ^ mask), :] = dg_refs[mask][...]


def cotangent(t, scales, nv_ref, u, attn, d_gated):
    r, c = scales[:, t : t + 1], scales[:, TILES + t : TILES + t + 1]
    n = attn.astype(F32) * r
    g = r * (d_gated * u.astype(F32) - n * c)
    return n, jnp.where(valid_rows(t, nv_ref), g, 0.0).astype(BF16)


def back(q, qt, k, kt, v, g, gt, mask):
    half = jnp.dot(k, qt, preferred_element_type=F32) * HALF
    up = jnp.where(mask, 1.0 + jnp.tanh(half), 0.0)
    w = (half * up).astype(BF16)
    dw = jnp.dot(v, gt, preferred_element_type=F32)
    ds = (dw * up * (1.0 + half * (2.0 - up))).astype(BF16)
    dv = jnp.dot(w, g, preferred_element_type=F32)
    dk = jnp.dot(ds, q, preferred_element_type=F32)
    dqt = jnp.dot(kt, ds, preferred_element_type=F32)
    return dv, dk, dqt


def bwd_far_kernel(lo_ref, nv_ref, at_ref, act_ref, qt_ref, attn_ref, kv_ref, kt_ref, *refs):
    sum_refs, dg_refs, (dqt_ref, dkv_ref, dg_s, acc_s) = refs[:HEADS], refs[HEADS : 2 * HEADS], refs[2 * HEADS :]
    first = jnp.minimum(lo_ref[0] + SPAN, SPAN) // CHUNK

    @pl.when(first < CHUNKS)
    def _():
        place_d_gated(at_ref, dg_refs, dg_s)
        scales = row_scales(sum_refs)

        def clear(c, carry):
            acc_s[chunk_at(c), :] = jnp.zeros((CHUNK, 2 * HD), F32)
            return carry

        lax.fori_loop(first, CHUNKS, clear, 0)
        for t in range(TILES):

            @pl.when(lo_ref[2 * t] < 0)
            def _():
                lo = by_half(t, lo_ref, (1, TILE), 1) + SPAN
                rows = slice(t * TILE, (t + 1) * TILE)
                q, qt = act_ref[rows, Q], qt_ref[:, rows]
                g = cotangent(t, scales, nv_ref, act_ref[rows, U], attn_ref[rows, :], dg_s[rows, :].astype(F32))[1]
                gt = g.T
                key = lax.broadcasted_iota(jnp.int32, (CHUNK, TILE), 0)

                def k_chunk(c, dqt):
                    at = chunk_at(c)
                    dv, dk, part = back(q, qt, kv_ref[at, HD:], kt_ref[:, at], kv_ref[at, :HD], g, gt, key >= lo - c * CHUNK)
                    acc_s[at, :HD] += dv
                    acc_s[at, HD:] += dk
                    return dqt + part

                start = (lo_ref[2 * t] + SPAN) // CHUNK
                dqt_ref[:, rows] = lax.fori_loop(start, CHUNKS, k_chunk, jnp.zeros((HD, TILE), F32))

        def store(c, carry):
            dkv_ref[chunk_at(c), :HD] = (acc_s[chunk_at(c), :HD] * (1.0 / SPAN)).astype(BF16)
            dkv_ref[chunk_at(c), HD:] = (acc_s[chunk_at(c), HD:] * (HALF / SPAN)).astype(BF16)
            return carry

        lax.fori_loop(first, CHUNKS, store, 0)


def bwd_own_kernel(lo_ref, nv_ref, at_ref, act_ref, slope_ref, slope_qt_ref, attn_ref, qt_ref, kt_ref, far_ref, *refs):
    sum_refs, dg_refs, (cols_ref, dkv_ref) = refs[:HEADS], refs[HEADS : 2 * HEADS], refs[2 * HEADS : 2 * HEADS + 2]
    pieces, (dg_s, g_s, gt_s, rows_s) = refs[2 * HEADS + 2 : -4], refs[-4:]
    place_d_gated(at_ref, dg_refs, dg_s)
    scales = row_scales(sum_refs)
    count = far_tiles(lo_ref)
    for t in range(TILES):
        rows = slice(t * TILE, (t + 1) * TILE)
        d_gated = dg_s[rows, :].astype(F32)
        n, g = cotangent(t, scales, nv_ref, act_ref[rows, U], attn_ref[rows, :], d_gated)
        g_s[rows, :] = g
        gt_s[:, rows] = g.T
        du = (d_gated * n).astype(BF16).astype(F32)
        cols_ref[:HD, rows] = (du * slope_ref[rows, U].astype(F32)).astype(BF16).T
    for c in range(CHUNKS):
        dkv_ref[c * CHUNK : (c + 1) * CHUNK, :] = jnp.zeros((CHUNK, 2 * HD), F32)
    key = lax.broadcasted_iota(jnp.int32, (CHUNK, TILE), 0)
    query = lax.broadcasted_iota(jnp.int32, (CHUNK, TILE), 1)

    def q_tile(t, carry):
        lo = by_half(t, lo_ref, (1, TILE), 1)
        q, qt = act_ref[rows_at(t), Q], qt_ref[:, rows_at(t)]
        g, gt = g_s[rows_at(t), :], gt_s[:, rows_at(t)]

        def k_chunk(c, dqt):
            at = chunk_at(c)
            mask = (key >= lo - c * CHUNK) & (key - query <= t * TILE - c * CHUNK)
            dv, dk, part = back(q, qt, act_ref[at, K], kt_ref[:, at], act_ref[at, V], g, gt, mask)
            dkv_ref[at, :HD] += dv
            dkv_ref[at, HD:] += dk
            return dqt + part

        first = jnp.maximum(lo_ref[2 * t], 0) // CHUNK
        dqt = lax.fori_loop(first, t // 2 + 1, k_chunk, jnp.zeros((HD, TILE), F32))
        dq = dqt + jnp.where(t < count, far_ref[:, rows_at(t)], 0.0)
        dq = (dq * (HALF / SPAN)).astype(BF16).astype(F32)
        dq = (dq * slope_qt_ref[:, rows_at(t)].astype(F32)).astype(BF16)
        cols_ref[HD:, rows_at(t)] = dq
        rows_s[rows_at(t), :] = dq.T
        return carry

    lax.fori_loop(0, TILES, q_tile, 0)
    for mask in range(HEADS):
        pieces[mask][...] = rows_s[rows_at(at_ref[1] ^ mask), :]


def key_kernel(groups, lo_ref, at_ref, own_ref, far_ref, slope_ref, cols_ref, normed_ref, *refs):
    pieces, shares, (cols_s, all_s) = refs[:HEADS], refs[HEADS:-2], refs[-2:]
    first = jnp.minimum(lo_ref[2 * TILES], SPAN) // CHUNK
    scale = jnp.where(lax.broadcasted_iota(jnp.int32, (1, 2 * HD), 1) < HD, 1.0 / SPAN, HALF / SPAN)
    for mask in range(HEADS):
        t = at_ref[1] ^ mask
        rows = rows_at(t)
        far = jnp.where(t // 2 >= first, far_ref[rows, :].astype(F32), 0.0)
        d = (own_ref[rows, :] * scale + far).astype(BF16).astype(F32)
        d = (d * slope_ref[rows, VK].astype(F32)).astype(BF16)
        pieces[mask][...] = d
        cols_s[:, rows] = d.T
    share = jnp.dot(cols_ref[...], normed_ref[...], preferred_element_type=F32).astype(BF16)
    all_s[:HD, :], all_s[2 * HD : 3 * HD, :] = share[:HD], share[HD:]
    share = jnp.dot(cols_s[...], normed_ref[...], preferred_element_type=F32).astype(BF16)
    all_s[HD : 2 * HD, :], all_s[3 * HD :, :] = share[:HD], share[HD:]
    size = 4 * HD // groups
    for mask in range(groups):
        at = pl.multiple_of((at_ref[0] ^ mask) * size, size)
        shares[mask][...] = all_s[pl.ds(at, size), :]


def assemble(at_ref, refs, cols, out_s):
    for mask in range(HEADS):
        out_s[:, lanes_at(at_ref[1] ^ mask)] = refs[mask][:, cols]
    return out_s[...]


def through(x, w_ref, branch):
    width = w_ref.shape[0]
    return lax.dot_general(x, w_ref[:, branch * width : (branch + 1) * width], NT, preferred_element_type=F32)


def rows_kernel(at_ref, *refs):
    attn_refs, q_refs, dg_refs = refs[:HEADS], refs[HEADS : 2 * HEADS], refs[2 * HEADS : 3 * HEADS]
    tokens_ref, w_out_ref, w_in_ref, out_ref, dn_ref, row_s = refs[3 * HEADS :]
    width = w_out_ref.shape[0]
    x = tokens_ref[...].astype(F32)
    u, slope = silu_and_slope(jnp.dot(norm_rows(x).astype(BF16), w_in_ref[:, :width], preferred_element_type=F32))
    n = norm_rows(assemble(at_ref, attn_refs, slice(None), row_s).astype(F32))
    gated = (n * u.astype(F32)).astype(BF16)
    y = jnp.dot(gated, w_out_ref[...], preferred_element_type=F32)
    out_ref[...] = (x + y).astype(BF16)
    du = (assemble(at_ref, dg_refs, slice(None), row_s).astype(F32) * n).astype(BF16).astype(F32)
    du = (du * slope.astype(F32)).astype(BF16)
    dn_ref[...] = through(du, w_in_ref, 0) + through(assemble(at_ref, q_refs, slice(None), row_s), w_in_ref, 2)


def last_kernel(groups, at_ref, *refs):
    vk_refs, shares, (dn_ref, tokens_ref, grad_ref, w_in_ref) = refs[:HEADS], refs[HEADS : HEADS + groups], refs[HEADS + groups : -3]
    out_ref, share_ref, row_s = refs[-3:]
    dn = dn_ref[...] + through(assemble(at_ref, vk_refs, slice(HD), row_s), w_in_ref, 1)
    dn += through(assemble(at_ref, vk_refs, slice(HD, 2 * HD), row_s), w_in_ref, 3)
    x = tokens_ref[...].astype(F32)
    r = lax.rsqrt(jnp.mean(x * x, axis=-1, keepdims=True) + eps)
    n = x * r
    dx = r * (dn - n * jnp.mean(dn * n, axis=-1, keepdims=True))
    out_ref[...] = (grad_ref[...].astype(F32) + dx).astype(BF16)
    total = shares[0][...].astype(F32)
    for ref in shares[1:]:
        total += ref[...].astype(F32)
    share_ref[...] = total


def call(kernel, scalars, arrays, outs, scratch=(), after=(), aliases=None, limit=16):
    smem = pl.BlockSpec(memory_space=pltpu.SMEM)
    vmem = pl.BlockSpec(memory_space=pltpu.VMEM)
    anywhere = pl.BlockSpec(memory_space=pl.ANY)
    return pl.pallas_call(
        kernel,
        out_shape=[jax.ShapeDtypeStruct(*out) for out in outs],
        in_specs=[smem] * len(scalars) + [vmem] * len(arrays) + [anywhere] * len(after),
        out_specs=[smem if out[1] == jnp.int32 else vmem for out in outs],
        scratch_shapes=[pltpu.VMEM(*shape) for shape in scratch],
        input_output_aliases=aliases or {},
        compiler_params=pltpu.CompilerParams(vmem_limit_bytes=limit * 2**20),
        cost_estimate=pl.CostEstimate(flops=0, bytes_accessed=0, transcendentals=0),
    )(*scalars, *arrays, *after)


def per_device(groups, tokens, w_in, w_out, block_counts, tails, grad_out):
    count, width = tokens.shape
    own, tall, wide, tall_t = (count, width), (SPAN, HD), (SPAN, 2 * HD), (HD, SPAN)
    piece, half, sums_shape = (count, HD), (BLK, width), (2 * TILES, TILE)

    def swap(x, mask):
        return lax.ppermute(x, "h", [(i, i ^ mask) for i in range(HEADS)])

    def trade(pieces):
        return [pieces[0]] + [swap(pieces[mask], mask) for mask in range(1, HEADS)]

    def onward(x):
        return lax.ppermute(x, "g", [(i, i + 1) for i in range(groups - 1)])

    info = call(info_kernel, (block_counts, tails), (), [((MAXB + 1,), jnp.int32)] * 2 + [((2,), jnp.int32)])

    x_rows, y_rows = swap(tokens, 2), swap(tokens, 4)
    *kept, kv, w_head = project(info, (0, 1), ((tokens,), (swap(tokens, 1),)), w_in, ())
    far_kv = [onward(kv)]
    dg_own = call(d_gated_kernel, (info[2],), (grad_out, w_out), [(piece, BF16)] * HEADS, [(own, BF16)], (kv,))
    d_gated = trade(dg_own)
    x_rows, y_rows, x_half, y_half = call(
        cut_kernel,
        (),
        (x_rows, y_rows),
        [(own, BF16), (own, BF16), (half, BF16), (half, BF16)],
        after=(far_kv[0], dg_own[0]),
        aliases={0: 0, 1: 1},
        limit=4,
    )
    corner = swap(x_half, 4), swap(y_half, 2)
    chunks = ((x_rows,), (swap(x_rows, 1),), (y_rows,), (swap(y_rows, 1),))
    *kept, kv = project(info, (2, 3, 4, 5), chunks, w_head, kept)
    far_kv.append(onward(kv))
    corner = call(gate_kernel, (), (), [(half, BF16), (half, BF16)], after=(*corner, kv), aliases={0: 0, 1: 1}, limit=4)
    *kept, kv = project(info, (6, 7), (corner, [swap(x, 1) for x in corner]), w_head, kept)
    far_kv.append(onward(kv))
    normed, act, slope = kept

    near, kt, qt, slope_qt = call(fwd_own_kernel, info[:2], (act, slope), [(tall, F32)] + [(tall_t, BF16)] * 3)
    attn, sums, kv, far_kt, *attn_pieces = call(
        fwd_far_kernel,
        info,
        (act, *far_kv, near, *d_gated),
        [(tall, BF16), (sums_shape, F32), (wide, BF16), (tall_t, BF16)] + [(piece, BF16)] * HEADS,
        [(tall, F32), (tall, BF16)],
    )
    sums = trade([sums] * HEADS)

    dqt_far, dkv_far = call(
        bwd_far_kernel,
        info,
        (act, qt, attn, kv, far_kt, *sums, *d_gated),
        [(tall_t, F32), (wide, BF16)],
        [(tall, BF16), (wide, F32)],
    )
    dkv_far = lax.ppermute(dkv_far, "g", [(i + 1, i) for i in range(groups - 1)])
    attn_rows = trade(attn_pieces)
    cols, dkv, *d_q = call(
        bwd_own_kernel,
        info,
        (act, slope, slope_qt, attn, qt, kt, dqt_far, *sums, *d_gated),
        [((2 * HD, SPAN), BF16), (wide, F32)] + [(piece, BF16)] * HEADS,
        [(tall, BF16), (tall, BF16), (tall_t, BF16), (tall, BF16)],
    )
    d_q = trade(d_q)
    rows = 4 * HD // groups
    outs = call(
        functools.partial(key_kernel, groups),
        (info[0], info[2]),
        (dkv, dkv_far, slope, cols, normed),
        [((count, 2 * HD), BF16)] * HEADS + [((rows, width), BF16)] * groups,
        [((2 * HD, SPAN), BF16), ((4 * HD, width), BF16)],
    )
    d_vk, shares = outs[:HEADS], outs[HEADS:]
    shares = [shares[0]] + [
        lax.ppermute(shares[mask], "g", [(i, i ^ mask) for i in range(groups)]) for mask in range(1, groups)
    ]
    d_vk = trade(d_vk)
    layer_out, d_normed = call(
        rows_kernel,
        (info[2],),
        (*attn_rows, *d_q, *dg_own, tokens, w_out, w_in),
        [(own, BF16), (own, F32)],
        [(own, BF16)],
    )
    grad_tokens, grad_w_in = call(
        functools.partial(last_kernel, groups),
        (info[2],),
        (*d_vk, *shares, d_normed, tokens, grad_out, w_in),
        [(own, BF16), ((rows, width), F32)],
        [(own, BF16)],
    )
    parts = groups // 4
    if parts > 1:
        perm = [
            (i * HEADS + j, ((i // parts) * HEADS + j) * parts + i % parts)
            for i in range(groups)
            for j in range(HEADS)
        ]
        grad_w_in = lax.ppermute(grad_w_in, ("g", "h"), perm)
    return (layer_out, grad_tokens, grad_w_in)


def solution(mesh):
    groups = mesh.shape["seq"] // HEADS
    split = Mesh(mesh.devices.reshape(groups, HEADS), ("g", "h"))
    rows = P(("g", "h"), None)
    return jax.shard_map(
        functools.partial(per_device, groups),
        mesh=split,
        in_specs=(rows, P(), P(), P(), P(), rows),
        out_specs=(rows, rows, rows),
        check_vma=False,
    )
```

time: 630 us -> 150 us (0.24)
  the two profiles are of different devices: /device:TPU:0 before, /device:TPU:9 now
where the time goes in v2:
time: 150 us; the launch traced here: 152 us
  starting transfers between devices  56.8 us (38%)
  Pallas kernels  45.4 us (30%)
  waiting for transfers between devices  43 us (29%)
  local copies, waits for them, and re-layouts  5.75 us (4%)
    pallas_call x14, Pallas kernels, call(): pl.pallas_call(kernel, out_shape=[jax.ShapeDtypeStruct(*out) for out in o...  45.4 us
    ppermute x44, starting transfers between devices, swap(): return lax.ppermute(x, 'h', [(i, i ^ mask) for i in range(HEADS)])  42.6 us
    ppermute x44, waiting for transfers between devices, swap(): return lax.ppermute(x, 'h', [(i, i ^ mask) for i in range(HEADS)])  18.2 us
    ppermute x3, waiting for transfers between devices, per_device(): lax.ppermute(shares[mask], 'g', [(i, i ^ mask) for i in range(groups)])  13 us
    ppermute x3, starting transfers between devices, onward(): return lax.ppermute(x, 'g', [(i, i + 1) for i in range(groups - 1)])  9.59 us
    ppermute x1, waiting for transfers between devices, per_device(): lax.ppermute(dkv_far, 'g', [(i + 1, i) for i in range(groups - 1)])  7.37 us
    unnamed x18, local copies, waits for them, and re-layouts  5.75 us
    ppermute x3, waiting for transfers between devices, onward(): return lax.ppermute(x, 'g', [(i, i + 1) for i in range(groups - 1)])  4.46 us
  transfers between devices with their start and end apart: 51, of which 16 were waited for; matrix products, arithmetic and copies ran while one was open for 0% of the time, Pallas kernels for 23%

profile of v2, /device:TPU:9, one launch (start us, length us, event | category | flops | bytes accessed | tf_op | source)
XLA Modules:
  0.0 151.9 jit_solution(7491567876851194756)
XLA Ops:
  5.1 1.6 %shard_map.85 = (s32[17]{0:T(128)S(1)}, s32[17]{0:T(128)S(1)}, s32[2]{0:T(128)S(1)}) custom-call(s32[16]{0:T(128)S(1)} %copy-done.5, s32[16]{0:T(128)S(1)} %copy-done.6), custom_call_target="tpu_custom_call" | custom-call | tf_op jit(solution)/shard_map/pallas_call | solution.py:421
  6.7 3.4 %copy-done = bf16[1024,4096]{1,0:T(8,128)(2,1)S(1)} copy-done((bf16[1024,4096]{1,0:T(8,128)(2,1)S(1)}, bf16[1024,4096]{1,0:T(8,128)(2,1)}, u32[]{:S(2)}) %copy-start) | copy-done | bytes 8388632
  11.2 1.8 %shard_map.86 = (bf16[2048,1024]{1,0:T(8,128)(2,1)S(1)}, bf16[2048,512]{1,0:T(8,128)(2,1)S(1)}, bf16[2048,512]{1,0:T(8,128)(2,1)S(1)}, bf16[512,256]{1,0:T(8,128)(2,1)S(1)}, bf16[1024,512]{1,0:T(8,128)(2,1)S(1)}) custom-call(s32[2]{0:T(128)S(1)} %get-tuple-element.77.at_ref, bf16[256,1024]{1,0:T(8,128)(2,1)S(1)} %copy-done.2, ...), custom_call_target="tpu_custom_call" | custom-call | tf_op jit(solution)/shard_map/pallas_call | solution.py:421
  13.0 3.2 %collective-permute-start.3 = (bf16[512,256]{1,0:T(8,128)(2,1)S(1)}, bf16[512,256]{1,0:T(8,128)(2,1)S(1)}, u32[]{:S(2)}, u32[]{:S(2)}) collective-permute-start(bf16[512,256]{1,0:T(8,128)(2,1)S(1)} %get-tuple-element.80.after_ref), channel_id=1, source_target_pairs={{0,8},{8,16},{16,24},{1,9},{9,17},{17,25},{2,10},{10,18},{18,26},{... | collective-permute-start | bytes 786440 | tf_op jit(solution)/shard_map/ppermute | solution.py:445
  17.7 4.5 %collective-permute-done.3.a_ref.kva_ref = bf16[512,256]{1,0:T(8,128)(2,1)S(1)} collective-permute-done((bf16[512,256]{1,0:T(8,128)(2,1)S(1)}, bf16[512,256]{1,0:T(8,128)(2,1)S(1)}, u32[]{:S(2)}, u32[]{:S(2)}) %collective-permute-start.3) | collective-permute-done | bytes 262176 | tf_op jit(solution)/shard_map/ppermute | solution.py:445
  26.0 2.6 %shard_map.89 = (bf16[2048,1024]{1,0:T(8,128)(2,1)S(1)}, bf16[2048,512]{1,0:T(8,128)(2,1)S(1)}, bf16[2048,512]{1,0:T(8,128)(2,1)S(1)}, bf16[1024,256]{1,0:T(8,128)(2,1)S(1)}) custom-call(s32[2]{0:T(128)S(1)} %get-tuple-element.77.at_ref, bf16[256,1024]{1,0:T(8,128)(2,1)S(1)} %get-tuple-element.84.refs_0_, ...), custom_call_target="tpu_custom_call", output_to_operand_aliasing={{0}: (6, {}), {1}: (7, {}), {2}: (8, {})} | custom-call | tf_op jit(solution)/shard_map/pallas_call | solution.py:421
  28.5 2.7 %collective-permute-done.4.a_ref = bf16[128,1024]{1,0:T(8,128)(2,1)S(1)} collective-permute-done((bf16[128,1024]{1,0:T(8,128)(2,1)S(1)}, bf16[128,1024]{1,0:T(8,128)(2,1)S(1)}, u32[]{:S(2)}, u32[]{:S(2)}) %collective-permute-start.4) | collective-permute-done | bytes 262176 | tf_op jit(solution)/shard_map/ppermute | solution.py:439
  32.7 3.2 %collective-permute-start.10 = (bf16[1024,256]{1,0:T(8,128)(2,1)S(1)}, bf16[1024,256]{1,0:T(8,128)(2,1)S(1)}, u32[]{:S(2)}, u32[]{:S(2)}) collective-permute-start(bf16[1024,256]{1,0:T(8,128)(2,1)S(1)} %get-tuple-element.90.after_ref), channel_id=1, source_target_pairs={{0,8},{8,16},{16,24},{1,9},{9,17},{17,25},{2,10},{10,18},{18,26},{... | collective-permute-start | bytes 1572872 | tf_op jit(solution)/shard_map/ppermute | solution.py:445
  36.0 1.7 %shard_map.91 = (bf16[2048,1024]{1,0:T(8,128)(2,1)S(1)}, bf16[2048,512]{1,0:T(8,128)(2,1)S(1)}, bf16[2048,512]{1,0:T(8,128)(2,1)S(1)}, bf16[512,256]{1,0:T(8,128)(2,1)S(1)}) custom-call(s32[2]{0:T(128)S(1)} %get-tuple-element.77.at_ref, bf16[128,1024]{1,0:T(8,128)(2,1)S(1)} %get-tuple-element.91.refs_0_, ...), custom_call_target="tpu_custom_call", output_to_operand_aliasing={{0}: (6, {}), {1}: (7, {}), {2}: (8, {})} | custom-call | tf_op jit(solution)/shard_map/pallas_call | solution.py:421
  37.6 3.2 %collective-permute-start.11 = (bf16[512,256]{1,0:T(8,128)(2,1)S(1)}, bf16[512,256]{1,0:T(8,128)(2,1)S(1)}, u32[]{:S(2)}, u32[]{:S(2)}) collective-permute-start(bf16[512,256]{1,0:T(8,128)(2,1)S(1)} %get-tuple-element.97), channel_id=1, source_target_pairs={{0,8},{8,16},{16,24},{1,9},{9,17},{17,25},{2,10},{10,18},{18,26},{... | collective-permute-start | bytes 786440 | tf_op jit(solution)/shard_map/ppermute | solution.py:445
  45.6 2.4 %collective-permute-start.16 = (bf16[256,128]{1,0:T(8,128)(2,1)S(1)}, bf16[256,128]{1,0:T(8,128)(2,1)S(1)}, u32[]{:S(2)}, u32[]{:S(2)}) collective-permute-start(bf16[256,128]{1,0:T(8,128)(2,1)S(1)} %get-tuple-element.104.refs_21_), channel_id=1, source_target_pairs={{0,5},{1,4},{2,7},{3,6},{4,1},{5,0},{6,3},{7,2},{8,13},{9,12},{10,... | collective-permute-start | bytes 196616 | tf_op jit(solution)/shard_map/ppermute | solution.py:439
  50.0 7.0 %shard_map.92 = (f32[2048,128]{1,0:T(8,128)S(1)}, bf16[128,2048]{1,0:T(8,128)(2,1)S(1)}, bf16[128,2048]{1,0:T(8,128)(2,1)S(1)}, bf16[128,2048]{1,0:T(8,128)(2,1)S(1)}) custom-call(s32[17]{0:T(128)S(1)} %get-tuple-element.78.lo_ref, s32[17]{0:T(128)S(1)} %get-tuple-element.79.nv_ref, bf16[2048,512]{1,0:T(8,128)(2,1)S(1)} %get-tuple-element.96.act_ref, ...), custom_call_target="tpu_custom_call" | custom-call | tf_op jit(solution)/shard_map/pallas_call | solution.py:421
  57.0 3.0 %shard_map.93 = (bf16[2048,128]{1,0:T(8,128)(2,1)S(1)}, f32[16,256]{1,0:T(8,128)S(1)}, bf16[2048,256]{1,0:T(8,128)(2,1)S(1)}, bf16[128,2048]{1,0:T(8,128)(2,1)S(...) custom-call(s32[17]{0:T(128)S(1)} %get-tuple-element.78.lo_ref, ...), custom_call_target="tpu_custom_call" | custom-call | tf_op jit(solution)/shard_map/pallas_call | solution.py:421
  60.9 1.7 %collective-permute-start.28 = (f32[16,256]{1,0:T(8,128)S(1)}, f32[16,256]{1,0:T(8,128)S(1)}, u32[]{:S(2)}, u32[]{:S(2)}) collective-permute-start(f32[16,256]{1,0:T(8,128)S(1)} %get-tuple-element.121.refs_0_), channel_id=1, source_target_pairs={{0,3},{1,2},{2,1},{3,0},{4,7},{5,6},{6,5},{7,4},{8,11},{9,10},{10,... | collective-permute-start | bytes 49160 | tf_op jit(solution)/shard_map/ppermute | solution.py:439
  65.1 1.9 %collective-permute-start.32 = (f32[16,256]{1,0:T(8,128)S(1)}, f32[16,256]{1,0:T(8,128)S(1)}, u32[]{:S(2)}, u32[]{:S(2)}) collective-permute-start(f32[16,256]{1,0:T(8,128)S(1)} %get-tuple-element.121.refs_0_), channel_id=1, source_target_pairs={{0,7},{1,6},{2,5},{3,4},{4,3},{5,2},{6,1},{7,0},{8,15},{9,14},{10,... | collective-permute-start | bytes 49160 | tf_op jit(solution)/shard_map/ppermute | solution.py:439
  67.9 1.5 %collective-permute-done.32.refs_7_ = f32[16,256]{1,0:T(8,128)S(1)} collective-permute-done((f32[16,256]{1,0:T(8,128)S(1)}, f32[16,256]{1,0:T(8,128)S(1)}, u32[]{:S(2)}, u32[]{:S(2)}) %collective-permute-start.32) | collective-permute-done | bytes 16416 | tf_op jit(solution)/shard_map/ppermute | solution.py:439
  69.5 3.9 %shard_map.94 = (f32[128,2048]{1,0:T(8,128)S(1)}, bf16[2048,256]{1,0:T(8,128)(2,1)S(1)}) custom-call(s32[17]{0:T(128)S(1)} %get-tuple-element.78.lo_ref, s32[17]{0:T(128)S(1)} %get-tuple-element.79.nv_ref, s32[2]{0:T(128)S(1)} %get-tuple-element.77.at_ref, bf16[2048,512]{1,0:T(8,128)(2,1)S(1)} %get-tuple-element.96.act_ref, ...), custom_call_target="tpu_custom_call" | custom-call | tf_op jit(solution)/shard_map/pallas_call | solution.py:421
  73.4 1.9 %collective-permute-start.40 = (bf16[2048,256]{1,0:T(8,128)(2,1)S(1)}, bf16[2048,256]{1,0:T(8,128)(2,1)S(1)}, u32[]{:S(2)}, u32[]{:S(2)}) collective-permute-start(bf16[2048,256]{1,0:T(8,128)(2,1)S(1)} %get-tuple-element.133), channel_id=1, source_target_pairs={{8,0},{16,8},{24,16},{9,1},{17,9},{25,17},{10,2},{18,10},{26,18},{... | collective-permute-start | bytes 3145736 | tf_op jit(solution)/shard_map/ppermute | solution.py:489
  81.4 1.7 %collective-permute-start.25 = (bf16[256,128]{1,0:T(8,128)(2,1)S(1)}, bf16[256,128]{1,0:T(8,128)(2,1)S(1)}, u32[]{:S(2)}, u32[]{:S(2)}) collective-permute-start(bf16[256,128]{1,0:T(8,128)(2,1)S(1)} %get-tuple-element.114), channel_id=1, source_target_pairs={{0,7},{1,6},{2,5},{3,4},{4,3},{5,2},{6,1},{7,0},{8,15},{9,14},{10,... | collective-permute-start | bytes 196616 | tf_op jit(solution)/shard_map/ppermute | solution.py:439
  83.1 11.4 %shard_map.95 = (bf16[256,2048]{1,0:T(8,128)(2,1)S(1)}, f32[2048,256]{1,0:T(8,128)S(1)}, bf16[256,128]{1,0:T(8,128)(2,1)S(1)}, bf16[256,128]{1,0:T(8,128)(2,1)S(...) custom-call(s32[17]{0:T(128)S(1)} %get-tuple-element.78.lo_ref, ...), custom_call_target="tpu_custom_call" | custom-call | tf_op jit(solution)/shard_map/pallas_call | solution.py:421
  97.1 7.4 %collective-permute-done.40.far_ref = bf16[2048,256]{1,0:T(8,128)(2,1)S(1)} collective-permute-done((bf16[2048,256]{1,0:T(8,128)(2,1)S(1)}, bf16[2048,256]{1,0:T(8,128)(2,1)S(1)}, u32[]{:S(2)}, u32[]{:S(2)}) %collective-permute-start.40) | collective-permute-done | bytes 1048608 | tf_op jit(solution)/shard_map/ppermute | solution.py:489
  105.6 3.4 %shard_map.97 = (bf16[256,256]{1,0:T(8,128)(2,1)S(1)}, bf16[256,256]{1,0:T(8,128)(2,1)S(1)}, bf16[256,256]{1,0:T(8,128)(2,1)S(1)}, bf16[256,256]{1,0:T(8,128)(2,...) custom-call(s32[17]{0:T(128)S(1)} %get-tuple-element.78.lo_ref, ...), custom_call_target="tpu_custom_call" | custom-call | tf_op jit(solution)/shard_map/pallas_call | solution.py:421
  111.3 1.9 %collective-permute-start.38 = (bf16[256,128]{1,0:T(8,128)(2,1)S(1)}, bf16[256,128]{1,0:T(8,128)(2,1)S(1)}, u32[]{:S(2)}, u32[]{:S(2)}) collective-permute-start(bf16[256,128]{1,0:T(8,128)(2,1)S(1)} %get-tuple-element.129), channel_id=1, source_target_pairs={{0,6},{1,7},{2,4},{3,5},{4,2},{5,3},{6,0},{7,1},{8,14},{9,15},{10,... | collective-permute-start | bytes 196616 | tf_op jit(solution)/shard_map/ppermute | solution.py:439
  113.9 4.7 %collective-permute-done.38.refs_14_ = bf16[256,128]{1,0:T(8,128)(2,1)S(1)} collective-permute-done((bf16[256,128]{1,0:T(8,128)(2,1)S(1)}, bf16[256,128]{1,0:T(8,128)(2,1)S(1)}, u32[]{:S(2)}, u32[]{:S(2)}) %collective-permute-start.38) | collective-permute-done | bytes 65568 | tf_op jit(solution)/shard_map/ppermute | solution.py:439
  119.0 1.9 %collective-permute-done.39.refs_15_ = bf16[256,128]{1,0:T(8,128)(2,1)S(1)} collective-permute-done((bf16[256,128]{1,0:T(8,128)(2,1)S(1)}, bf16[256,128]{1,0:T(8,128)(2,1)S(1)}, u32[]{:S(2)}, u32[]{:S(2)}) %collective-permute-start.39) | collective-permute-done | bytes 65568 | tf_op jit(solution)/shard_map/ppermute | solution.py:439
  120.9 1.6 %collective-permute-start.45 = (bf16[256,256]{1,0:T(8,128)(2,1)S(1)}, bf16[256,256]{1,0:T(8,128)(2,1)S(1)}, u32[]{:S(2)}, u32[]{:S(2)}) collective-permute-start(bf16[256,256]{1,0:T(8,128)(2,1)S(1)} %get-tuple-element.141), channel_id=1, source_target_pairs={{0,5},{1,4},{2,7},{3,6},{4,1},{5,0},{6,3},{7,2},{8,13},{9,12},{10,... | collective-permute-start | bytes 393224 | tf_op jit(solution)/shard_map/ppermute | solution.py:439
  122.6 2.6 %collective-permute-start.49 = (bf16[128,1024]{1,0:T(8,128)(2,1)S(1)}, bf16[128,1024]{1,0:T(8,128)(2,1)S(1)}, u32[]{:S(2)}, u32[]{:S(2)}) collective-permute-start(bf16[128,1024]{1,0:T(8,128)(2,1)S(1)} %get-tuple-element.146), channel_id=1, source_target_pairs={{0,16},{8,24},{16,0},{24,8},{1,17},{9,25},{17,1},{25,9},{2,18},{10... | collective-permute-start | bytes 786440 | tf_op jit(solution)/shard_map/ppermute | solution.py:509
  126.7 1.6 %collective-permute-done.45.refs_5_ = bf16[256,256]{1,0:T(8,128)(2,1)S(1)} collective-permute-done((bf16[256,256]{1,0:T(8,128)(2,1)S(1)}, bf16[256,256]{1,0:T(8,128)(2,1)S(1)}, u32[]{:S(2)}, u32[]{:S(2)}) %collective-permute-start.45) | collective-permute-done | bytes 131104 | tf_op jit(solution)/shard_map/ppermute | solution.py:439
  129.8 4.2 %shard_map.96 = (bf16[256,1024]{1,0:T(8,128)(2,1)}, f32[256,1024]{1,0:T(8,128)S(1)}) custom-call(s32[2]{0:T(128)S(1)} %get-tuple-element.77.at_ref, bf16[256,128]{1,0:T(8,128)(2,1)S(1)} %get-tuple-element.107.refs_0_, bf16[256,128]{1,0:T(8,128)(2,1)S(1)} %collective-permute-done.19.refs_1_, bf16[256,128]{1,0:T(8,128)(2,1)S(1)} %collective-permute-done.20.refs_2_, ...), custom_call_target="tpu_custom_call" | custom-call | tf_op jit(solution)/shard_map/pallas_call | solution.py:421
  135.6 7.0 %collective-permute-done.49.refs_10_ = bf16[128,1024]{1,0:T(8,128)(2,1)S(1)} collective-permute-done((bf16[128,1024]{1,0:T(8,128)(2,1)S(1)}, bf16[128,1024]{1,0:T(8,128)(2,1)S(1)}, u32[]{:S(2)}, u32[]{:S(2)}) %collective-permute-start.49) | collective-permute-done | bytes 262176 | tf_op jit(solution)/shard_map/ppermute | solution.py:509
  142.6 5.9 %collective-permute-done.50.refs_11_ = bf16[128,1024]{1,0:T(8,128)(2,1)S(1)} collective-permute-done((bf16[128,1024]{1,0:T(8,128)(2,1)S(1)}, bf16[128,1024]{1,0:T(8,128)(2,1)S(1)}, u32[]{:S(2)}, u32[]{:S(2)}) %collective-permute-start.50) | collective-permute-done | bytes 262176 | tf_op jit(solution)/shard_map/ppermute | solution.py:509
  148.6 3.3 %shard_map.98 = (bf16[256,1024]{1,0:T(8,128)(2,1)}, f32[128,1024]{1,0:T(8,128)}) custom-call(s32[2]{0:T(128)S(1)} %get-tuple-element.77.at_ref, bf16[256,256]{1,0:T(8,128)(2,1)S(1)} %get-tuple-element.136.refs_0_, bf16[256,256]{1,0:T(8,128)(2,1)S(1)} %collective-permute-done.41.refs_1_, bf16[256,256]{1,0:T(8,128)(2,1)S(1)} %collective-permute-done.42.refs_2_, ...), custom_call_target="tpu_custom_call" | custom-call | tf_op jit(solution)/shard_map/pallas_call | solution.py:421
  (103 shorter events, 40.9 us)
Async XLA Ops:
  1.4 16.3 %collective-permute-start = (bf16[256,1024]{1,0:T(8,128)(2,1)}, bf16[256,1024]{1,0:T(8,128)(2,1)S(1)}, u32[]{:S(2)}, u32[]{:S(2)}) collective-permute-start(bf16[256,1024]{1,0:T(8,128)(2,1)} %refs_13_.1), channel_id=1, source_target_pairs={{0,2},{1,3},{2,0},{3,1},{4,6},{5,7},{6,4},{7,5},{8,10},{9,11},{10,... | collective-permute-start | bytes 1572872 | tf_op jit(solution)/shard_map/ppermute | solution.py:439
  2.6 15.1 %collective-permute-start.1 = (bf16[256,1024]{1,0:T(8,128)(2,1)}, bf16[256,1024]{1,0:T(8,128)(2,1)S(1)}, u32[]{:S(2)}, u32[]{:S(2)}) collective-permute-start(bf16[256,1024]{1,0:T(8,128)(2,1)} %refs_13_.1), channel_id=1, source_target_pairs={{0,4},{1,5},{2,6},{3,7},{4,0},{5,1},{6,2},{7,3},{8,12},{9,13},{10,... | collective-permute-start | bytes 1572872 | tf_op jit(solution)/shard_map/ppermute | solution.py:439
  13.0 9.1 %collective-permute-start.3 = (bf16[512,256]{1,0:T(8,128)(2,1)S(1)}, bf16[512,256]{1,0:T(8,128)(2,1)S(1)}, u32[]{:S(2)}, u32[]{:S(2)}) collective-permute-start(bf16[512,256]{1,0:T(8,128)(2,1)S(1)} %get-tuple-element.80.after_ref), channel_id=1, source_target_pairs={{0,8},{8,16},{16,24},{1,9},{9,17},{17,25},{2,10},{10,18},{18,26},{... | collective-permute-start | bytes 786440 | tf_op jit(solution)/shard_map/ppermute | solution.py:445
  23.8 7.4 %collective-permute-start.4 = (bf16[128,1024]{1,0:T(8,128)(2,1)S(1)}, bf16[128,1024]{1,0:T(8,128)(2,1)S(1)}, u32[]{:S(2)}, u32[]{:S(2)}) collective-permute-start(bf16[128,1024]{1,0:T(8,128)(2,1)S(1)} %get-tuple-element.82), channel_id=1, source_target_pairs={{0,4},{1,5},{2,6},{3,7},{4,0},{5,1},{6,2},{7,3},{8,12},{9,13},{10,... | collective-permute-start | bytes 786440 | tf_op jit(solution)/shard_map/ppermute | solution.py:439
  24.0 7.2 %collective-permute-start.5 = (bf16[128,1024]{1,0:T(8,128)(2,1)S(1)}, bf16[128,1024]{1,0:T(8,128)(2,1)S(1)}, u32[]{:S(2)}, u32[]{:S(2)}) collective-permute-start(bf16[128,1024]{1,0:T(8,128)(2,1)S(1)} %get-tuple-element.83), channel_id=1, source_target_pairs={{0,2},{1,3},{2,0},{3,1},{4,6},{5,7},{6,4},{7,5},{8,10},{9,11},{10,... | collective-permute-start | bytes 786440 | tf_op jit(solution)/shard_map/ppermute | solution.py:439
  32.7 24.3 %collective-permute-start.10 = (bf16[1024,256]{1,0:T(8,128)(2,1)S(1)}, bf16[1024,256]{1,0:T(8,128)(2,1)S(1)}, u32[]{:S(2)}, u32[]{:S(2)}) collective-permute-start(bf16[1024,256]{1,0:T(8,128)(2,1)S(1)} %get-tuple-element.90.after_ref), channel_id=1, source_target_pairs={{0,8},{8,16},{16,24},{1,9},{9,17},{17,25},{2,10},{10,18},{18,26},{... | collective-permute-start | bytes 1572872 | tf_op jit(solution)/shard_map/ppermute | solution.py:445
  37.6 19.4 %collective-permute-start.11 = (bf16[512,256]{1,0:T(8,128)(2,1)S(1)}, bf16[512,256]{1,0:T(8,128)(2,1)S(1)}, u32[]{:S(2)}, u32[]{:S(2)}) collective-permute-start(bf16[512,256]{1,0:T(8,128)(2,1)S(1)} %get-tuple-element.97), channel_id=1, source_target_pairs={{0,8},{8,16},{16,24},{1,9},{9,17},{17,25},{2,10},{10,18},{18,26},{... | collective-permute-start | bytes 786440 | tf_op jit(solution)/shard_map/ppermute | solution.py:445
  45.6 11.3 %collective-permute-start.16 = (bf16[256,128]{1,0:T(8,128)(2,1)S(1)}, bf16[256,128]{1,0:T(8,128)(2,1)S(1)}, u32[]{:S(2)}, u32[]{:S(2)}) collective-permute-start(bf16[256,128]{1,0:T(8,128)(2,1)S(1)} %get-tuple-element.104.refs_21_), channel_id=1, source_target_pairs={{0,5},{1,4},{2,7},{3,6},{4,1},{5,0},{6,3},{7,2},{8,13},{9,12},{10,... | collective-permute-start | bytes 196616 | tf_op jit(solution)/shard_map/ppermute | solution.py:439
  48.1 8.9 %collective-permute-start.17 = (bf16[256,128]{1,0:T(8,128)(2,1)S(1)}, bf16[256,128]{1,0:T(8,128)(2,1)S(1)}, u32[]{:S(2)}, u32[]{:S(2)}) collective-permute-start(bf16[256,128]{1,0:T(8,128)(2,1)S(1)} %get-tuple-element.105.refs_22_), channel_id=1, source_target_pairs={{0,6},{1,7},{2,4},{3,5},{4,2},{5,3},{6,0},{7,1},{8,14},{9,15},{10,... | collective-permute-start | bytes 196616 | tf_op jit(solution)/shard_map/ppermute | solution.py:439
  48.7 8.3 %collective-permute-start.18 = (bf16[256,128]{1,0:T(8,128)(2,1)S(1)}, bf16[256,128]{1,0:T(8,128)(2,1)S(1)}, u32[]{:S(2)}, u32[]{:S(2)}) collective-permute-start(bf16[256,128]{1,0:T(8,128)(2,1)S(1)} %get-tuple-element.106.refs_23_), channel_id=1, source_target_pairs={{0,7},{1,6},{2,5},{3,4},{4,3},{5,2},{6,1},{7,0},{8,15},{9,14},{10,... | collective-permute-start | bytes 196616 | tf_op jit(solution)/shard_map/ppermute | solution.py:439
  73.4 31.1 %collective-permute-start.40 = (bf16[2048,256]{1,0:T(8,128)(2,1)S(1)}, bf16[2048,256]{1,0:T(8,128)(2,1)S(1)}, u32[]{:S(2)}, u32[]{:S(2)}) collective-permute-start(bf16[2048,256]{1,0:T(8,128)(2,1)S(1)} %get-tuple-element.133), channel_id=1, source_target_pairs={{8,0},{16,8},{24,16},{9,1},{17,9},{25,17},{10,2},{18,10},{26,18},{... | collective-permute-start | bytes 3145736 | tf_op jit(solution)/shard_map/ppermute | solution.py:489
  77.5 17.0 %collective-permute-start.22 = (bf16[256,128]{1,0:T(8,128)(2,1)S(1)}, bf16[256,128]{1,0:T(8,128)(2,1)S(1)}, u32[]{:S(2)}, u32[]{:S(2)}) collective-permute-start(bf16[256,128]{1,0:T(8,128)(2,1)S(1)} %get-tuple-element.111), channel_id=1, source_target_pairs={{0,4},{1,5},{2,6},{3,7},{4,0},{5,1},{6,2},{7,3},{8,12},{9,13},{10,... | collective-permute-start | bytes 196616 | tf_op jit(solution)/shard_map/ppermute | solution.py:439
  77.8 16.8 %collective-permute-start.23 = (bf16[256,128]{1,0:T(8,128)(2,1)S(1)}, bf16[256,128]{1,0:T(8,128)(2,1)S(1)}, u32[]{:S(2)}, u32[]{:S(2)}) collective-permute-start(bf16[256,128]{1,0:T(8,128)(2,1)S(1)} %get-tuple-element.112), channel_id=1, source_target_pairs={{0,5},{1,4},{2,7},{3,6},{4,1},{5,0},{6,3},{7,2},{8,13},{9,12},{10,... | collective-permute-start | bytes 196616 | tf_op jit(solution)/shard_map/ppermute | solution.py:439
  79.5 16.4 %collective-permute-start.24 = (bf16[256,128]{1,0:T(8,128)(2,1)S(1)}, bf16[256,128]{1,0:T(8,128)(2,1)S(1)}, u32[]{:S(2)}, u32[]{:S(2)}) collective-permute-start(bf16[256,128]{1,0:T(8,128)(2,1)S(1)} %get-tuple-element.113), channel_id=1, source_target_pairs={{0,6},{1,7},{2,4},{3,5},{4,2},{5,3},{6,0},{7,1},{8,14},{9,15},{10,... | collective-permute-start | bytes 196616 | tf_op jit(solution)/shard_map/ppermute | solution.py:439
  81.4 15.4 %collective-permute-start.25 = (bf16[256,128]{1,0:T(8,128)(2,1)S(1)}, bf16[256,128]{1,0:T(8,128)(2,1)S(1)}, u32[]{:S(2)}, u32[]{:S(2)}) collective-permute-start(bf16[256,128]{1,0:T(8,128)(2,1)S(1)} %get-tuple-element.114), channel_id=1, source_target_pairs={{0,7},{1,6},{2,5},{3,4},{4,3},{5,2},{6,1},{7,0},{8,15},{9,14},{10,... | collective-permute-start | bytes 196616 | tf_op jit(solution)/shard_map/ppermute | solution.py:439
  94.5 14.5 %collective-permute-start.33 = (bf16[256,128]{1,0:T(8,128)(2,1)S(1)}, bf16[256,128]{1,0:T(8,128)(2,1)S(1)}, u32[]{:S(2)}, u32[]{:S(2)}) collective-permute-start(bf16[256,128]{1,0:T(8,128)(2,1)S(1)} %get-tuple-element.124), channel_id=1, source_target_pairs={{0,1},{1,0},{2,3},{3,2},{4,5},{5,4},{6,7},{7,6},{8,9},{9,8},{10,11... | collective-permute-start | bytes 196616 | tf_op jit(solution)/shard_map/ppermute | solution.py:439
  94.6 14.5 %collective-permute-start.34 = (bf16[256,128]{1,0:T(8,128)(2,1)S(1)}, bf16[256,128]{1,0:T(8,128)(2,1)S(1)}, u32[]{:S(2)}, u32[]{:S(2)}) collective-permute-start(bf16[256,128]{1,0:T(8,128)(2,1)S(1)} %get-tuple-element.125), channel_id=1, source_target_pairs={{0,2},{1,3},{2,0},{3,1},{4,6},{5,7},{6,4},{7,5},{8,10},{9,11},{10,... | collective-permute-start | bytes 196616 | tf_op jit(solution)/shard_map/ppermute | solution.py:439
  95.9 14.7 %collective-permute-start.35 = (bf16[256,128]{1,0:T(8,128)(2,1)S(1)}, bf16[256,128]{1,0:T(8,128)(2,1)S(1)}, u32[]{:S(2)}, u32[]{:S(2)}) collective-permute-start(bf16[256,128]{1,0:T(8,128)(2,1)S(1)} %get-tuple-element.126), channel_id=1, source_target_pairs={{0,3},{1,2},{2,1},{3,0},{4,7},{5,6},{6,5},{7,4},{8,11},{9,10},{10,... | collective-permute-start | bytes 196616 | tf_op jit(solution)/shard_map/ppermute | solution.py:439
  96.7 14.5 %collective-permute-start.36 = (bf16[256,128]{1,0:T(8,128)(2,1)S(1)}, bf16[256,128]{1,0:T(8,128)(2,1)S(1)}, u32[]{:S(2)}, u32[]{:S(2)}) collective-permute-start(bf16[256,128]{1,0:T(8,128)(2,1)S(1)} %get-tuple-element.127), channel_id=1, source_target_pairs={{0,4},{1,5},{2,6},{3,7},{4,0},{5,1},{6,2},{7,3},{8,12},{9,13},{10,... | collective-permute-start | bytes 196616 | tf_op jit(solution)/shard_map/ppermute | solution.py:439
  104.5 8.6 %collective-permute-start.37 = (bf16[256,128]{1,0:T(8,128)(2,1)S(1)}, bf16[256,128]{1,0:T(8,128)(2,1)S(1)}, u32[]{:S(2)}, u32[]{:S(2)}) collective-permute-start(bf16[256,128]{1,0:T(8,128)(2,1)S(1)} %get-tuple-element.128), channel_id=1, source_target_pairs={{0,5},{1,4},{2,7},{3,6},{4,1},{5,0},{6,3},{7,2},{8,13},{9,12},{10,... | collective-permute-start | bytes 196616 | tf_op jit(solution)/shard_map/ppermute | solution.py:439
  109.0 13.5 %collective-permute-start.41 = (bf16[256,256]{1,0:T(8,128)(2,1)S(1)}, bf16[256,256]{1,0:T(8,128)(2,1)S(1)}, u32[]{:S(2)}, u32[]{:S(2)}) collective-permute-start(bf16[256,256]{1,0:T(8,128)(2,1)S(1)} %get-tuple-element.137), channel_id=1, source_target_pairs={{0,1},{1,0},{2,3},{3,2},{4,5},{5,4},{6,7},{7,6},{8,9},{9,8},{10,11... | collective-permute-start | bytes 393224 | tf_op jit(solution)/shard_map/ppermute | solution.py:439
  109.1 13.4 %collective-permute-start.42 = (bf16[256,256]{1,0:T(8,128)(2,1)S(1)}, bf16[256,256]{1,0:T(8,128)(2,1)S(1)}, u32[]{:S(2)}, u32[]{:S(2)}) collective-permute-start(bf16[256,256]{1,0:T(8,128)(2,1)S(1)} %get-tuple-element.138), channel_id=1, source_target_pairs={{0,2},{1,3},{2,0},{3,1},{4,6},{5,7},{6,4},{7,5},{8,10},{9,11},{10,... | collective-permute-start | bytes 393224 | tf_op jit(solution)/shard_map/ppermute | solution.py:439
  110.6 14.6 %collective-permute-start.43 = (bf16[256,256]{1,0:T(8,128)(2,1)S(1)}, bf16[256,256]{1,0:T(8,128)(2,1)S(1)}, u32[]{:S(2)}, u32[]{:S(2)}) collective-permute-start(bf16[256,256]{1,0:T(8,128)(2,1)S(1)} %get-tuple-element.139), channel_id=1, source_target_pairs={{0,3},{1,2},{2,1},{3,0},{4,7},{5,6},{6,5},{7,4},{8,11},{9,10},{10,... | collective-permute-start | bytes 393224 | tf_op jit(solution)/shard_map/ppermute | solution.py:439
  111.3 7.4 %collective-permute-start.38 = (bf16[256,128]{1,0:T(8,128)(2,1)S(1)}, bf16[256,128]{1,0:T(8,128)(2,1)S(1)}, u32[]{:S(2)}, u32[]{:S(2)}) collective-permute-start(bf16[256,128]{1,0:T(8,128)(2,1)S(1)} %get-tuple-element.129), channel_id=1, source_target_pairs={{0,6},{1,7},{2,4},{3,5},{4,2},{5,3},{6,0},{7,1},{8,14},{9,15},{10,... | collective-permute-start | bytes 196616 | tf_op jit(solution)/shard_map/ppermute | solution.py:439
  113.1 7.8 %collective-permute-start.39 = (bf16[256,128]{1,0:T(8,128)(2,1)S(1)}, bf16[256,128]{1,0:T(8,128)(2,1)S(1)}, u32[]{:S(2)}, u32[]{:S(2)}) collective-permute-start(bf16[256,128]{1,0:T(8,128)(2,1)S(1)} %get-tuple-element.130), channel_id=1, source_target_pairs={{0,7},{1,6},{2,5},{3,4},{4,3},{5,2},{6,1},{7,0},{8,15},{9,14},{10,... | collective-permute-start | bytes 196616 | tf_op jit(solution)/shard_map/ppermute | solution.py:439
  118.7 6.6 %collective-permute-start.44 = (bf16[256,256]{1,0:T(8,128)(2,1)S(1)}, bf16[256,256]{1,0:T(8,128)(2,1)S(1)}, u32[]{:S(2)}, u32[]{:S(2)}) collective-permute-start(bf16[256,256]{1,0:T(8,128)(2,1)S(1)} %get-tuple-element.140), channel_id=1, source_target_pairs={{0,4},{1,5},{2,6},{3,7},{4,0},{5,1},{6,2},{7,3},{8,12},{9,13},{10,... | collective-permute-start | bytes 393224 | tf_op jit(solution)/shard_map/ppermute | solution.py:439
  120.9 7.4 %collective-permute-start.45 = (bf16[256,256]{1,0:T(8,128)(2,1)S(1)}, bf16[256,256]{1,0:T(8,128)(2,1)S(1)}, u32[]{:S(2)}, u32[]{:S(2)}) collective-permute-start(bf16[256,256]{1,0:T(8,128)(2,1)S(1)} %get-tuple-element.141), channel_id=1, source_target_pairs={{0,5},{1,4},{2,7},{3,6},{4,1},{5,0},{6,3},{7,2},{8,13},{9,12},{10,... | collective-permute-start | bytes 393224 | tf_op jit(solution)/shard_map/ppermute | solution.py:439
  122.6 13.0 %collective-permute-start.48 = (bf16[128,1024]{1,0:T(8,128)(2,1)S(1)}, bf16[128,1024]{1,0:T(8,128)(2,1)S(1)}, u32[]{:S(2)}, u32[]{:S(2)}) collective-permute-start(bf16[128,1024]{1,0:T(8,128)(2,1)S(1)} %get-tuple-element.145), channel_id=1, source_target_pairs={{0,8},{8,0},{16,24},{24,16},{1,9},{9,1},{17,25},{25,17},{2,10},{10... | collective-permute-start | bytes 786440 | tf_op jit(solution)/shard_map/ppermute | solution.py:509
  122.6 20.0 %collective-permute-start.49 = (bf16[128,1024]{1,0:T(8,128)(2,1)S(1)}, bf16[128,1024]{1,0:T(8,128)(2,1)S(1)}, u32[]{:S(2)}, u32[]{:S(2)}) collective-permute-start(bf16[128,1024]{1,0:T(8,128)(2,1)S(1)} %get-tuple-element.146), channel_id=1, source_target_pairs={{0,16},{8,24},{16,0},{24,8},{1,17},{9,25},{17,1},{25,9},{2,18},{10... | collective-permute-start | bytes 786440 | tf_op jit(solution)/shard_map/ppermute | solution.py:509
  125.2 23.3 %collective-permute-start.50 = (bf16[128,1024]{1,0:T(8,128)(2,1)S(1)}, bf16[128,1024]{1,0:T(8,128)(2,1)S(1)}, u32[]{:S(2)}, u32[]{:S(2)}) collective-permute-start(bf16[128,1024]{1,0:T(8,128)(2,1)S(1)} %get-tuple-element.147), channel_id=1, source_target_pairs={{0,24},{8,16},{16,8},{24,0},{1,25},{9,17},{17,9},{25,1},{2,26},{10... | collective-permute-start | bytes 786440 | tf_op jit(solution)/shard_map/ppermute | solution.py:509
  125.2 8.9 %collective-permute-start.46 = (bf16[256,256]{1,0:T(8,128)(2,1)S(1)}, bf16[256,256]{1,0:T(8,128)(2,1)S(1)}, u32[]{:S(2)}, u32[]{:S(2)}) collective-permute-start(bf16[256,256]{1,0:T(8,128)(2,1)S(1)} %get-tuple-element.142), channel_id=1, source_target_pairs={{0,6},{1,7},{2,4},{3,5},{4,2},{5,3},{6,0},{7,1},{8,14},{9,15},{10,... | collective-permute-start | bytes 393224 | tf_op jit(solution)/shard_map/ppermute | solution.py:439
  128.3 7.3 %collective-permute-start.47 = (bf16[256,256]{1,0:T(8,128)(2,1)S(1)}, bf16[256,256]{1,0:T(8,128)(2,1)S(1)}, u32[]{:S(2)}, u32[]{:S(2)}) collective-permute-start(bf16[256,256]{1,0:T(8,128)(2,1)S(1)} %get-tuple-element.143), channel_id=1, source_target_pairs={{0,7},{1,6},{2,5},{3,4},{4,3},{5,2},{6,1},{7,0},{8,15},{9,14},{10,... | collective-permute-start | bytes 393224 | tf_op jit(solution)/shard_map/ppermute | solution.py:439
  (28 other events, 189.1 us)

commit v3 on v2

v3 whole, which is shorter than its diff:
```python
import functools

import jax
import jax.numpy as jnp
from jax import lax
from jax.experimental import pallas as pl
from jax.experimental.pallas import tpu as pltpu
from jax.sharding import Mesh, PartitionSpec as P

HEADS = 8
HD = 128
BLK = 128
MAXB = 16
SPAN = MAXB * BLK
TILE = 256
TILES = SPAN // TILE
CHUNK = 512
CHUNKS = SPAN // CHUNK
SCALE = HD ** (-0.5)
LOG2E = 1.4426950408889634

eps = 1e-05

NT = (((1,), (1,)), ((), ()))
F32, BF16 = jnp.float32, jnp.bfloat16

U, Q, V, K = (slice(i * HD, (i + 1) * HD) for i in range(4))
PLACE = (0, 2, 1, 3)
UQ, VK = slice(0, 2 * HD), slice(2 * HD, 4 * HD)


def info_kernel(counts_ref, tails_ref, lo_ref, nv_ref, at_ref):
    group = lax.axis_index("g").astype(jnp.int32)
    at_ref[0] = group
    at_ref[1] = lax.axis_index("h").astype(jnp.int32)
    base = group * MAXB
    for j in range(2 * MAXB):
        lo_ref[j] = j * BLK
        nv_ref[j] = BLK

    def user(n, start):
        end = start + counts_ref[n]

        def block(j, carry):
            lo_ref[j] = (start - base) * BLK
            nv_ref[j] = jnp.where(j == end - 1 - base, tails_ref[n], BLK)
            return carry

        lax.fori_loop(jnp.maximum(start - base, 0), jnp.minimum(end - base, 2 * MAXB), block, 0)
        return end

    lax.fori_loop(0, counts_ref.shape[0], user, jnp.int32(0))


def by_half(t, ref, shape, dim):
    side = lax.broadcasted_iota(jnp.int32, shape, dim)
    return jnp.where(side < BLK, ref[2 * t], ref[2 * t + 1])


def from_start(t, lo_ref, at, keys, dim):
    parts = [part >= lo_ref[2 * t + i] - at for i, part in enumerate(jnp.split(keys, 2, axis=1 - dim))]
    return jnp.concatenate(parts, axis=1 - dim)


def valid_rows(t, nv_ref):
    row = lax.broadcasted_iota(jnp.int32, (TILE, 1), 0)
    return (row & (BLK - 1)) < by_half(t, nv_ref, (TILE, 1), 0)


def rows_at(t):
    return pl.ds(pl.multiple_of(t * TILE, TILE), TILE)


def chunk_at(c):
    return pl.ds(pl.multiple_of(c * CHUNK, CHUNK), CHUNK)


def lanes_at(i):
    return pl.ds(pl.multiple_of(i * HD, HD), HD)


def norm_rows(x):
    return x * lax.rsqrt(jnp.mean(x * x, axis=-1, keepdims=True) + eps)


def silu_and_slope(pre):
    s = 0.5 + 0.5 * jnp.tanh(0.5 * pre)
    return (pre * s).astype(BF16), (s * (1.0 + pre * (1.0 - s))).astype(BF16)


def store_rows(x, place, wh_ref, normed_ref, act_ref, slope_ref, kv_ref, i):
    rows = rows_at(place)
    xn = norm_rows(x.astype(F32)).astype(BF16)
    normed_ref[rows, :] = xn
    act, slope = silu_and_slope(jnp.dot(xn, wh_ref[...], preferred_element_type=F32))
    act_ref[rows, :] = act
    slope_ref[rows, :] = slope
    kv_ref[i * TILE : (i + 1) * TILE, :] = act[:, VK]


def first_kernel(other_ref, tokens_ref, w_ref, normed_ref, act_ref, slope_ref, kv_ref, wh_ref, x_s, sems):
    head, width = lax.axis_index("h").astype(jnp.int32), w_ref.shape[0]
    copies = [pltpu.make_async_copy(tokens_ref, x_s, sems.at[4])]
    for i in range(4):
        source = w_ref.at[:, lanes_at(PLACE[i] * (width // HD) + head)]
        copies.append(pltpu.make_async_copy(source, wh_ref.at[:, i * HD : (i + 1) * HD], sems.at[i]))
    for copy in copies:
        copy.start()
    for copy in copies:
        copy.wait()
    outs = wh_ref, normed_ref, act_ref, slope_ref, kv_ref
    store_rows(x_s[...], head, *outs, 0)
    store_rows(other_ref[...], head ^ 1, *outs, 1)


def proj_kernel(masks, pieces, last, at_ref, *refs):
    x_refs, wh_ref = refs[: sum(pieces)], refs[sum(pieces)]
    outs = refs[-5:-1] if last else refs[-4:]
    for i, mask in enumerate(masks):
        parts = [ref[...] for ref in x_refs[sum(pieces[:i]) : sum(pieces[: i + 1])]]
        x = parts[0] if len(parts) == 1 else jnp.concatenate(parts, axis=0)
        store_rows(x, at_ref[1] ^ mask, wh_ref, *outs, i)
    if last:
        refs[-1][...] = outs[1][:, Q]


def proj_outs(width, n):
    return [((SPAN, width), BF16), ((SPAN, 4 * HD), BF16), ((SPAN, 4 * HD), BF16), ((n * TILE, 2 * HD), BF16)]


def project(info, masks, chunks, w, kept, last=False):
    pieces = tuple(len(chunk) for chunk in chunks)
    flat = [piece for chunk in chunks for piece in chunk]
    start = 2 + len(flat)
    return call(
        functools.partial(proj_kernel, masks, pieces, last),
        (info[2],),
        (*flat, w),
        proj_outs(w.shape[0], len(masks)) + ([((SPAN, HD), BF16)] if last else []),
        after=kept,
        aliases={start + i: i for i in range(len(kept))},
    )


def cut_kernel(x_ref, y_ref, *refs):
    x_half, y_half = refs[-2:]
    x_half[...] = x_ref[:BLK, :]
    y_half[...] = y_ref[BLK:, :]


def gate_kernel(*refs):
    pass


def d_gated_kernel(g_ref, w_ref, after_ref, *refs):
    outs, d_s = refs[:-1], refs[-1]
    d_s[...] = lax.dot_general(g_ref[...], w_ref[...], NT, preferred_element_type=F32).astype(BF16)
    for mask in range(HEADS):
        outs[mask][...] = d_s[:, lanes_at(lax.axis_index("h").astype(jnp.int32) ^ mask)]


def sigmoid(s):
    return pl.reciprocal(1.0 + jnp.exp2(s * (-SCALE * LOG2E)), approx=True)


def weigh(q, kt, v, mask):
    s = jnp.dot(q, kt, preferred_element_type=F32)
    w = jnp.where(mask, s * sigmoid(s), 0.0).astype(BF16)
    return jnp.dot(w, v, preferred_element_type=F32)


def fwd_own_kernel(lo_ref, nv_ref, act_ref, slope_ref, out_ref, kt_ref, qt_ref, slope_qt_ref):
    for t in range(TILES):
        rows = slice(t * TILE, (t + 1) * TILE)
        kt_ref[:, rows] = act_ref[rows, K].T
    row = lax.broadcasted_iota(jnp.int32, (TILE, CHUNK), 0)
    col = lax.broadcasted_iota(jnp.int32, (TILE, CHUNK), 1)

    def q_tile(t, carry):
        q = act_ref[rows_at(t), Q]

        def k_chunk(c, acc):
            mask = from_start(t, lo_ref, c * CHUNK, col, 1) & (col - row <= t * TILE - c * CHUNK)
            return acc + weigh(q, kt_ref[:, chunk_at(c)], act_ref[chunk_at(c), V], mask)

        first = jnp.maximum(lo_ref[2 * t], 0) // CHUNK
        acc = lax.fori_loop(first, t // 2 + 1, k_chunk, jnp.zeros((TILE, HD), F32))
        out_ref[rows_at(t), :] = jnp.where(valid_rows(t, nv_ref), acc, 0.0)
        return carry

    lax.fori_loop(0, TILES, q_tile, 0)
    for t in range(TILES):
        rows = slice(t * TILE, (t + 1) * TILE)
        qt_ref[:, rows] = act_ref[rows, Q].T
        slope_qt_ref[:, rows] = slope_ref[rows, Q].T


def fwd_far_kernel(
    lo_ref, nv_ref, at_ref, act_ref, kva_ref, kvb_ref, kvc_ref, near_ref, *refs,
):
    dg_refs, (out_ref, kv_ref, kt_ref), pieces, (sum_s, attn_s, dg_s) = refs[:HEADS], refs[HEADS : HEADS + 3], refs[HEADS + 3 : -3], refs[-3:]
    head = at_ref[1]
    slot = 0
    for ref in (kva_ref, kvb_ref, kvc_ref):
        for at in range(0, ref.shape[0], TILE):
            kv_ref[rows_at(slot ^ head), :] = ref[at : at + TILE, :]
            slot += 1
    for mask in range(HEADS):
        dg_s[rows_at(head ^ mask), :] = dg_refs[mask][...]
    first = jnp.minimum(lo_ref[0] + SPAN, SPAN) // CHUNK
    for t in range(TILES):
        rows = slice(t * TILE, (t + 1) * TILE)

        @pl.when(t // 2 >= first)
        def _():
            kt_ref[:, rows] = kv_ref[rows, HD:].T

    attn_s[...] = near_ref[...]
    col = lax.broadcasted_iota(jnp.int32, (TILE, CHUNK), 1)

    def q_tile(t, carry):
        q = act_ref[rows_at(t), Q]

        def k_chunk(c, acc):
            mask = from_start(t, lo_ref, c * CHUNK - SPAN, col, 1)
            return acc + weigh(q, kt_ref[:, chunk_at(c)], kv_ref[chunk_at(c), :HD], mask)

        start = (lo_ref[2 * t] + SPAN) // CHUNK
        acc = lax.fori_loop(start, CHUNKS, k_chunk, jnp.zeros((TILE, HD), F32))
        attn_s[rows_at(t), :] += jnp.where(valid_rows(t, nv_ref), acc, 0.0)
        return carry

    lax.fori_loop(0, far_tiles(lo_ref), q_tile, 0)
    ones = jnp.ones((8, HD), BF16)
    for t in range(TILES):
        rows = slice(t * TILE, (t + 1) * TILE)
        attn = attn_s[rows, :] * (SCALE / SPAN)
        out_ref[rows, :] = attn.astype(BF16)
        d_n = dg_s[rows, :].astype(F32) * act_ref[rows, U].astype(F32)
        square = lax.dot_general(ones, (attn * attn).astype(BF16), NT, preferred_element_type=F32)
        cross = lax.dot_general(ones, (attn * d_n).astype(BF16), NT, preferred_element_type=F32)
        sum_s[t : t + 1, :] = square[:1]
        sum_s[TILES + t : TILES + t + 1, :] = cross[:1]
    sums = sum_s[...]
    high = sums.astype(BF16)
    low = (sums - high.astype(F32)).astype(BF16)
    sums = jnp.concatenate([high[:, :HD], high[:, HD:], low[:, :HD], low[:, HD:]], axis=0)
    for mask in range(HEADS):
        pieces[mask][:TILE, :] = out_ref[rows_at(head ^ mask), :]
        pieces[mask][TILE:, :] = sums


def far_tiles(lo_ref):
    return sum((lo_ref[2 * t] < 0).astype(jnp.int32) for t in range(TILES))


def row_scales(sum_refs):
    width = HEADS * HD
    total = 0.0
    for ref in sum_refs:
        total += ref[TILE:, :].astype(F32)
    n = 2 * TILES
    total = jnp.concatenate([total[:n] + total[2 * n : 3 * n], total[n : 2 * n] + total[3 * n :]], axis=1)
    r = lax.rsqrt(total[:TILES] * (1.0 / width) + eps)
    c = total[TILES:] * (1.0 / width) * r
    return jnp.concatenate([r, c], axis=0).T


def cotangent(t, scales, nv_ref, u, attn, d_gated):
    r, c = scales[:, t : t + 1], scales[:, TILES + t : TILES + t + 1]
    n = attn.astype(F32) * r
    g = r * (d_gated * u.astype(F32) - n * c)
    return n, jnp.where(valid_rows(t, nv_ref), g, 0.0).astype(BF16)


def back_scores(qt, k, v, gt, mask):
    s = jnp.dot(k, qt, preferred_element_type=F32)
    sig = jnp.where(mask, sigmoid(s), 0.0)
    dw = jnp.dot(v, gt, preferred_element_type=F32)
    ds = dw * sig * (1.0 + (s * SCALE) * (1.0 - sig))
    return (s * sig).astype(BF16), ds.astype(BF16)


def cotangent_kernel(nv_ref, at_ref, act_ref, slope_ref, attn_ref, *refs):
    sum_refs, dg_refs, (g_ref, cols_ref, dg_s) = refs[:HEADS], refs[HEADS : 2 * HEADS], refs[-3:]
    for mask in range(HEADS):
        dg_s[rows_at(at_ref[1] ^ mask), :] = dg_refs[mask][...]
    scales = row_scales(sum_refs)
    for t in range(TILES):
        rows = slice(t * TILE, (t + 1) * TILE)
        d_gated = dg_s[rows, :].astype(F32)
        n, g = cotangent(t, scales, nv_ref, act_ref[rows, U], attn_ref[rows, :], d_gated)
        g_ref[rows, :] = g
        du = (d_gated * n).astype(BF16).astype(F32)
        cols_ref[:, rows] = (du * slope_ref[rows, U].astype(F32)).astype(BF16).T


def queries_kernel(lo_ref, act_ref, slope_qt_ref, qt_ref, kt_ref, g_ref, kv_ref, far_kt_ref, cols_ref, rows_ref, dkv_ref, gt_s):
    for t in range(TILES):
        rows = slice(t * TILE, (t + 1) * TILE)
        gt_s[:, rows] = g_ref[rows, :].T
    for c in range(CHUNKS):
        dkv_ref[c * CHUNK : (c + 1) * CHUNK, :] = jnp.zeros((CHUNK, 2 * HD), F32)
    key = lax.broadcasted_iota(jnp.int32, (CHUNK, TILE), 0)
    query = lax.broadcasted_iota(jnp.int32, (CHUNK, TILE), 1)

    def q_tile(t, carry):
        q, qt = act_ref[rows_at(t), Q], qt_ref[:, rows_at(t)]
        g, gt = g_ref[rows_at(t), :], gt_s[:, rows_at(t)]

        def far_chunk(c, dqt):
            at = chunk_at(c)
            mask = from_start(t, lo_ref, c * CHUNK - SPAN, key, 0)
            ds = back_scores(qt, kv_ref[at, HD:], kv_ref[at, :HD], gt, mask)[1]
            return dqt + jnp.dot(far_kt_ref[:, at], ds, preferred_element_type=F32)

        def k_chunk(c, dqt):
            at = chunk_at(c)
            mask = from_start(t, lo_ref, c * CHUNK, key, 0) & (key - query <= t * TILE - c * CHUNK)
            w, ds = back_scores(qt, act_ref[at, K], act_ref[at, V], gt, mask)
            dkv_ref[at, :HD] += jnp.dot(w, g, preferred_element_type=F32)
            dkv_ref[at, HD:] += jnp.dot(ds, q, preferred_element_type=F32)
            return dqt + jnp.dot(kt_ref[:, at], ds, preferred_element_type=F32)

        first = lo_ref[2 * t]
        start = jnp.minimum(first + SPAN, SPAN) // CHUNK
        dqt = lax.fori_loop(start, CHUNKS, far_chunk, jnp.zeros((HD, TILE), F32))
        dqt = lax.fori_loop(jnp.maximum(first, 0) // CHUNK, t // 2 + 1, k_chunk, dqt)
        dq = (dqt * (SCALE / SPAN)).astype(BF16).astype(F32)
        dq = (dq * slope_qt_ref[:, rows_at(t)].astype(F32)).astype(BF16)
        cols_ref[:, rows_at(t)] = dq
        rows_ref[rows_at(t), :] = dq.T
        return carry

    lax.fori_loop(0, TILES, q_tile, 0)


def halving(groups):
    return [0] if groups == 1 else [2 * i for i in halving(groups // 2)] + [2 * i + 1 for i in halving(groups // 2)]


def keys_kernel(
    groups, lo_ref, at_ref, own_ref, act_ref, slope_ref, q_ref, g_ref, u_cols_ref, q_cols_ref, dq_ref, normed_ref, *refs
):
    own_piece, other, pairs, (keep, send, cols_s, all_s, acc_s) = refs[0], refs[1], refs[2:5], refs[5:]
    first = jnp.minimum(lo_ref[2 * TILES], SPAN) // CHUNK
    key = lax.broadcasted_iota(jnp.int32, (CHUNK, TILE), 0)

    def clear(c, carry):
        acc_s[chunk_at(c), :] = jnp.zeros((CHUNK, 2 * HD), F32)
        return carry

    lax.fori_loop(first, CHUNKS, clear, 0)

    def q_tile(t, carry):
        q, g = q_ref[rows_at(t), :], g_ref[rows_at(t), :]
        qt, gt = q.T, g.T

        def k_chunk(c, carry):
            at = chunk_at(c)
            mask = from_start(TILES + t, lo_ref, c * CHUNK, key, 0)
            w, ds = back_scores(qt, act_ref[at, K], act_ref[at, V], gt, mask)
            acc_s[at, :HD] += jnp.dot(w, g, preferred_element_type=F32)
            acc_s[at, HD:] += jnp.dot(ds, q, preferred_element_type=F32)
            return carry

        return lax.fori_loop(lo_ref[2 * (TILES + t)] // CHUNK, CHUNKS, k_chunk, carry)

    count = sum((lo_ref[2 * (TILES + t)] < SPAN).astype(jnp.int32) for t in range(TILES))
    lax.fori_loop(0, count, q_tile, 0)
    places = {0: (own_piece, 0)}
    for i in range(4):
        places[2 * i + 1] = other, i * TILE
    for i in range(3):
        places[2 * i + 2] = pairs[i], 0
    for mask in range(HEADS):
        t = at_ref[1] ^ mask
        rows = rows_at(t)
        d = own_ref[rows, :] + jnp.where(t // 2 >= first, acc_s[rows, :], 0.0)
        d = (d * (SCALE / SPAN)).astype(BF16).astype(F32)
        d = (d * slope_ref[rows, VK].astype(F32)).astype(BF16)
        ref, at = places[mask]
        ref[at : at + TILE, :HD] = dq_ref[rows, :]
        ref[at : at + TILE, HD:] = d
        cols_s[:, rows] = d.T
    share = jnp.dot(cols_s[...], normed_ref[...], preferred_element_type=F32).astype(BF16)
    all_s[HD : 2 * HD, :], all_s[3 * HD :, :] = share[:HD], share[HD:]
    all_s[:HD, :] = jnp.dot(u_cols_ref[...], normed_ref[...], preferred_element_type=F32).astype(BF16)
    all_s[2 * HD : 3 * HD, :] = jnp.dot(q_cols_ref[...], normed_ref[...], preferred_element_type=F32).astype(BF16)
    size = 4 * HD // groups
    for i, mask in enumerate(halving(groups)):
        at = pl.multiple_of((at_ref[0] ^ mask) * size, size)
        part = all_s[pl.ds(at, size), :]
        if i < groups // 2:
            keep[i * size : (i + 1) * size, :] = part.astype(F32)
        else:
            send[(i - groups // 2) * size : (i + 1 - groups // 2) * size, :] = part


def merge_kernel(other_ref, *refs):
    for i, ref in enumerate(refs[-3:]):
        ref[TILE:, :] = other_ref[(i + 1) * TILE : (i + 2) * TILE, :]


def assemble(at_ref, refs, cols, out_s):
    for mask in range(HEADS):
        out_s[:, lanes_at(at_ref[1] ^ mask)] = refs[mask][:TILE, cols]
    return out_s[...]


def through(x, w_ref, branch):
    width = w_ref.shape[0]
    return lax.dot_general(x, w_ref[:, branch * width : (branch + 1) * width], NT, preferred_element_type=F32)


def rows_kernel(at_ref, *refs):
    attn_refs, dg_refs = refs[:HEADS], refs[HEADS : 2 * HEADS]
    tokens_ref, w_out_ref, w_in_ref, out_ref, dn_ref, row_s = refs[2 * HEADS :]
    width = w_out_ref.shape[0]
    x = tokens_ref[...].astype(F32)
    u, slope = silu_and_slope(jnp.dot(norm_rows(x).astype(BF16), w_in_ref[:, :width], preferred_element_type=F32))
    n = norm_rows(assemble(at_ref, attn_refs, slice(None), row_s).astype(F32))
    gated = (n * u.astype(F32)).astype(BF16)
    y = jnp.dot(gated, w_out_ref[...], preferred_element_type=F32)
    out_ref[...] = (x + y).astype(BF16)
    du = (assemble(at_ref, dg_refs, slice(None), row_s).astype(F32) * n).astype(BF16).astype(F32)
    du = (du * slope.astype(F32)).astype(BF16)
    dn_ref[...] = through(du, w_in_ref, 0)


def half_kernel(keep_ref, got_ref, *refs):
    half = keep_ref.shape[0] // len(refs)
    refs[0][...] = keep_ref[:half, :] + got_ref[:half, :].astype(F32)
    if len(refs) > 1:
        refs[1][...] = (keep_ref[half:, :] + got_ref[half:, :].astype(F32)).astype(BF16)


def last_kernel(at_ref, own_ref, other_ref, *refs):
    pairs, (dn_ref, tokens_ref, grad_ref, w_in_ref, after_ref, out_ref, row_s) = refs[:3], refs[3:]
    pieces = [(own_ref, 0), (other_ref, 0)] + [(ref, at) for ref in pairs for at in (0, TILE)]
    dn = dn_ref[...]
    for i, branch in enumerate((2, 1, 3)):
        for mask, (ref, at) in enumerate(pieces):
            row_s[:, lanes_at(at_ref[1] ^ mask)] = ref[at : at + TILE, i * HD : (i + 1) * HD]
        dn += through(row_s[...], w_in_ref, branch)
    x = tokens_ref[...].astype(F32)
    r = lax.rsqrt(jnp.mean(x * x, axis=-1, keepdims=True) + eps)
    n = x * r
    dx = r * (dn - n * jnp.mean(dn * n, axis=-1, keepdims=True))
    out_ref[...] = (grad_ref[...].astype(F32) + dx).astype(BF16)


def call(kernel, scalars, arrays, outs, scratch=(), after=(), aliases=None, limit=16, sems=0):
    smem = pl.BlockSpec(memory_space=pltpu.SMEM)
    vmem = pl.BlockSpec(memory_space=pltpu.VMEM)
    anywhere = pl.BlockSpec(memory_space=pl.ANY)
    return pl.pallas_call(
        kernel,
        out_shape=[jax.ShapeDtypeStruct(*out) for out in outs],
        in_specs=[smem] * len(scalars) + [vmem] * len(arrays) + [anywhere] * len(after),
        out_specs=[smem if out[1] == jnp.int32 else vmem for out in outs],
        scratch_shapes=[pltpu.VMEM(*shape) for shape in scratch] + ([pltpu.SemaphoreType.DMA((sems,))] if sems else []),
        input_output_aliases=aliases or {},
        compiler_params=pltpu.CompilerParams(vmem_limit_bytes=limit * 2**20),
        cost_estimate=pl.CostEstimate(flops=0, bytes_accessed=0, transcendentals=0),
    )(*scalars, *arrays, *after)


def per_device(groups, tokens, w_in, w_out, block_counts, tails, grad_out):
    count, width = tokens.shape
    own, tall, wide, tall_t = (count, width), (SPAN, HD), (SPAN, 2 * HD), (HD, SPAN)
    piece, half, sums_shape = (count, HD), (BLK, width), (2 * TILES, TILE)

    def swap(x, mask):
        return lax.ppermute(x, "h", [(i, i ^ mask) for i in range(HEADS)])

    def trade(pieces):
        return [pieces[0]] + [swap(pieces[mask], mask) for mask in range(1, HEADS)]

    def onward(x):
        return lax.ppermute(x, "g", [(i, i + 1) for i in range(groups - 1)])

    def backward(x):
        return lax.ppermute(x, "g", [(i + 1, i) for i in range(groups - 1)])

    x_rows, y_rows = swap(tokens, 2), swap(tokens, 4)
    *kept, kv, w_head = call(
        first_kernel,
        (),
        (swap(tokens, 1),),
        proj_outs(width, 2) + [((width, 4 * HD), BF16)],
        [(own, BF16)],
        (tokens, w_in),
        limit=48,
        sems=5,
    )
    far_kv = [onward(kv)]
    dg_own = call(d_gated_kernel, (), (grad_out, w_out), [(piece, BF16)] * HEADS, [(own, BF16)], (kv,))
    d_gated = trade(dg_own)
    info = call(info_kernel, (block_counts, tails), (), [((2 * MAXB,), jnp.int32)] * 2 + [((2,), jnp.int32)])
    x_rows, y_rows, x_half, y_half = call(
        cut_kernel,
        (),
        (x_rows, y_rows),
        [(own, BF16), (own, BF16), (half, BF16), (half, BF16)],
        after=(far_kv[0], *d_gated[1:5]),
        aliases={0: 0, 1: 1},
        limit=4,
    )
    corner = swap(x_half, 4), swap(y_half, 2)
    chunks = ((x_rows,), (swap(x_rows, 1),), (y_rows,), (swap(y_rows, 1),))
    *kept, kv = project(info, (2, 3, 4, 5), chunks, w_head, kept)
    far_kv.append(onward(kv))
    corner = call(gate_kernel, (), (), [(half, BF16), (half, BF16)], after=(*corner, kv, *d_gated[5:]), aliases={0: 0, 1: 1}, limit=4)
    *kept, kv, q = project(info, (6, 7), (corner, [swap(x, 1) for x in corner]), w_head, kept, True)
    far_kv.append(onward(kv))
    q_next = backward(q)
    normed, act, slope = kept

    near, kt, qt, slope_qt = call(fwd_own_kernel, info[:2], (act, slope), [(tall, F32)] + [(tall_t, BF16)] * 3)
    attn, kv, far_kt, *sums = call(
        fwd_far_kernel,
        info,
        (act, *far_kv, near, *d_gated),
        [(tall, BF16), (wide, BF16), (tall_t, BF16)] + [((count + 8 * TILES, HD), BF16)] * HEADS,
        [(sums_shape, F32), (tall, F32), (tall, BF16)],
    )
    sums = trade(sums)

    g, u_cols = call(
        cotangent_kernel,
        info[1:],
        (act, slope, attn, *sums, *d_gated),
        [(tall, BF16), (tall_t, BF16)],
        [(tall, BF16)],
        (q_next,),
    )
    g_next = backward(g)
    q_cols, d_q, dkv = call(
        queries_kernel,
        info[:1],
        (act, slope_qt, qt, kt, g, kv, far_kt),
        [(tall_t, BF16), (tall, BF16), (wide, F32)],
        [(tall_t, BF16)],
    )
    rows, cols = 4 * HD // groups, 3 * HD
    half_rows = rows * groups // 2
    mine, other, *pairs, keep, send = call(
        functools.partial(keys_kernel, groups),
        (info[0], info[2]),
        (dkv, act, slope, q_next, g_next, u_cols, q_cols, d_q, normed),
        [((count, cols), BF16), ((4 * count, cols), BF16)]
        + [((2 * count, cols), BF16)] * 3
        + [((half_rows, width), F32), ((half_rows, width), BF16)],
        [((2 * HD, SPAN), BF16), ((4 * HD, width), BF16), (wide, F32)],
    )
    other = swap(other, 1)
    pairs = call(
        merge_kernel, (), (other,), [((2 * count, cols), BF16)] * 3, after=pairs, aliases={1: 0, 2: 1, 3: 2}, limit=4
    )
    pairs = [swap(x, mask) for x, mask in zip(pairs, (2, 4, 6))]
    layer_out, d_normed = call(
        rows_kernel,
        (info[2],),
        (*sums, *dg_own, tokens, w_out, w_in),
        [(own, BF16), (own, F32)],
        [(own, BF16)],
    )
    mask = 1
    while mask < groups:
        send = lax.ppermute(send, "g", [(i, i ^ mask) for i in range(groups)])
        mask, half_rows = 2 * mask, half_rows // 2
        outs = [((half_rows, width), F32), ((half_rows, width), BF16)] if mask < groups else [((rows, width), F32)]
        keep, *send = call(half_kernel, (), (keep, send), outs)
        send = send[0] if send else None
    grad_w_in = keep
    grad_tokens = call(
        last_kernel,
        (info[2],),
        (mine, other, *pairs, d_normed, tokens, grad_out, w_in),
        [(own, BF16)],
        [(own, BF16)],
        (grad_w_in,),
    )[0]
    parts = groups // 4
    if parts > 1:
        perm = [
            (i * HEADS + j, ((i // parts) * HEADS + j) * parts + i % parts)
            for i in range(groups)
            for j in range(HEADS)
        ]
        grad_w_in = lax.ppermute(grad_w_in, ("g", "h"), perm)
    return (layer_out, grad_tokens, grad_w_in)


def solution(mesh):
    groups = mesh.shape["seq"] // HEADS
    split = Mesh(mesh.devices.reshape(groups, HEADS), ("g", "h"))
    rows = P(("g", "h"), None)
    return jax.shard_map(
        functools.partial(per_device, groups),
        mesh=split,
        in_specs=(rows, P(), P(), P(), P(), rows),
        out_specs=(rows, rows, rows),
        check_vma=False,
    )
```

time: 150 us -> 139 us (0.927)
  the two profiles are of different devices: /device:TPU:9 before, /device:TPU:0 now
where the time goes in v3:
time: 139 us; the launch traced here: 137 us
  starting transfers between devices  45.9 us (33%)
  Pallas kernels  44.4 us (32%)
  waiting for transfers between devices  41.6 us (30%)
  local copies, waits for them, and re-layouts  4.32 us (3%)
    pallas_call x17, Pallas kernels, call(): pl.pallas_call(kernel, out_shape=[jax.ShapeDtypeStruct(*out) for out in o...  44.4 us
    ppermute x27, starting transfers between devices, swap(): return lax.ppermute(x, 'h', [(i, i ^ mask) for i in range(HEADS)])  23.9 us
    ppermute x2, waiting for transfers between devices, per_device(): send = lax.ppermute(send, 'g', [(i, i ^ mask) for i in range(groups)])  16.5 us
    ppermute x27, waiting for transfers between devices, swap(): return lax.ppermute(x, 'h', [(i, i ^ mask) for i in range(HEADS)])  12.2 us
    ppermute x3, starting transfers between devices, onward(): return lax.ppermute(x, 'g', [(i, i + 1) for i in range(groups - 1)])  11.7 us
    ppermute x2, waiting for transfers between devices, backward(): return lax.ppermute(x, 'g', [(i + 1, i) for i in range(groups - 1)])  9.03 us
    ppermute x2, starting transfers between devices, per_device(): send = lax.ppermute(send, 'g', [(i, i ^ mask) for i in range(groups)])  7.74 us
    unnamed x20, local copies, waits for them, and re-layouts  4.32 us
  transfers between devices with their start and end apart: 34, of which 15 were waited for; matrix products, arithmetic and copies ran while one was open for 0% of the time, Pallas kernels for 23%

profile of v3, /device:TPU:0, one launch (start us, length us, event | category | flops | bytes accessed | tf_op | source)
XLA Modules:
  0.0 137.2 jit_solution(5009712064207792673)
XLA Ops:
  1.2 2.6 %collective-permute-start = (bf16[256,1024]{1,0:T(8,128)(2,1)}, bf16[256,1024]{1,0:T(8,128)(2,1)S(1)}, u32[]{:S(2)}, u32[]{:S(2)}) collective-permute-start(bf16[256,1024]{1,0:T(8,128)(2,1)} %refs_4_.1), channel_id=1, source_target_pairs={{0,2},{1,3},{2,0},{3,1},{4,6},{5,7},{6,4},{7,5},{8,10},{9,11},{10,... | collective-permute-start | bytes 1572872 | tf_op jit(solution)/shard_map/ppermute | solution.py:475
  3.7 1.5 %collective-permute-start.1 = (bf16[256,1024]{1,0:T(8,128)(2,1)}, bf16[256,1024]{1,0:T(8,128)(2,1)S(1)}, u32[]{:S(2)}, u32[]{:S(2)}) collective-permute-start(bf16[256,1024]{1,0:T(8,128)(2,1)} %refs_4_.1), channel_id=1, source_target_pairs={{0,4},{1,5},{2,6},{3,7},{4,0},{5,1},{6,2},{7,3},{8,12},{9,13},{10,... | collective-permute-start | bytes 1572872 | tf_op jit(solution)/shard_map/ppermute | solution.py:475
  6.3 4.8 %shard_map.86 = (bf16[2048,1024]{1,0:T(8,128)(2,1)}, bf16[2048,512]{1,0:T(8,128)(2,1)S(1)}, bf16[2048,512]{1,0:T(8,128)(2,1)}, bf16[512,256]{1,0:T(8,128)(2,1)S(1)}, bf16[1024,512]{1,0:T(8,128)(2,1)S(1)}) custom-call(bf16[256,1024]{1,0:T(8,128)(2,1)S(1)} %collective-permute-done.2.other_ref, bf16[256,1024]{1,0:T(8,128)(2,1)S(1)} %copy-done.3, ...), custom_call_target="tpu_custom_call" | custom-call | tf_op jit(solution)/shard_map/pallas_call | solution.py:457
  11.1 3.6 %collective-permute-start.3 = (bf16[512,256]{1,0:T(8,128)(2,1)S(1)}, bf16[512,256]{1,0:T(8,128)(2,1)S(1)}, u32[]{:S(2)}, u32[]{:S(2)}) collective-permute-start(bf16[512,256]{1,0:T(8,128)(2,1)S(1)} %get-tuple-element.71.after_ref), channel_id=1, source_target_pairs={{0,8},{8,16},{16,24},{1,9},{9,17},{17,25},{2,10},{10,18},{18,26},{... | collective-permute-start | bytes 786440 | tf_op jit(solution)/shard_map/ppermute | solution.py:481
  17.9 1.5 %collective-permute-start.7 = (bf16[256,128]{1,0:T(8,128)(2,1)S(1)}, bf16[256,128]{1,0:T(8,128)(2,1)S(1)}, u32[]{:S(2)}, u32[]{:S(2)}) collective-permute-start(bf16[256,128]{1,0:T(8,128)(2,1)S(1)} %get-tuple-element.75.refs_12_), channel_id=1, source_target_pairs={{0,4},{1,5},{2,6},{3,7},{4,0},{5,1},{6,2},{7,3},{8,12},{9,13},{10,... | collective-permute-start | bytes 196616 | tf_op jit(solution)/shard_map/ppermute | solution.py:475
  23.0 1.5 %collective-permute-start.8 = (bf16[128,1024]{1,0:T(8,128)(2,1)S(1)}, bf16[128,1024]{1,0:T(8,128)(2,1)S(1)}, u32[]{:S(2)}, u32[]{:S(2)}) collective-permute-start(bf16[128,1024]{1,0:T(8,128)(2,1)S(1)} %get-tuple-element.76), channel_id=1, source_target_pairs={{0,4},{1,5},{2,6},{3,7},{4,0},{5,1},{6,2},{7,3},{8,12},{9,13},{10,... | collective-permute-start | bytes 786440 | tf_op jit(solution)/shard_map/ppermute | solution.py:475
  25.0 2.1 %collective-permute-start.13 = (bf16[256,128]{1,0:T(8,128)(2,1)S(1)}, bf16[256,128]{1,0:T(8,128)(2,1)S(1)}, u32[]{:S(2)}, u32[]{:S(2)}) collective-permute-start(bf16[256,128]{1,0:T(8,128)(2,1)S(1)} %get-tuple-element.86.refs_14_), channel_id=1, source_target_pairs={{0,6},{1,7},{2,4},{3,5},{4,2},{5,3},{6,0},{7,1},{8,14},{9,15},{10,... | collective-permute-start | bytes 196616 | tf_op jit(solution)/shard_map/ppermute | solution.py:475
  27.8 1.7 %shard_map.85 = (s32[32]{0:T(128)S(1)}, s32[32]{0:T(128)S(1)}, s32[2]{0:T(128)S(1)}) custom-call(s32[16]{0:T(128)S(1)} %copy-done.6, s32[16]{0:T(128)S(1)} %copy-done.7), custom_call_target="tpu_custom_call" | custom-call | tf_op jit(solution)/shard_map/pallas_call | solution.py:457
  29.5 2.2 %copy-done.1 = bf16[2048,1024]{1,0:T(8,128)(2,1)S(1)} copy-done((bf16[2048,1024]{1,0:T(8,128)(2,1)S(1)}, bf16[2048,1024]{1,0:T(8,128)(2,1)}, u32[]{:S(2)}) %copy-start.1) | copy-done | bytes 4194328
  31.7 2.5 %shard_map.89 = (bf16[2048,1024]{1,0:T(8,128)(2,1)S(1)}, bf16[2048,512]{1,0:T(8,128)(2,1)S(1)}, bf16[2048,512]{1,0:T(8,128)(2,1)S(1)}, bf16[1024,256]{1,0:T(8,128)(2,1)S(1)}) custom-call(s32[2]{0:T(128)S(1)} %get-tuple-element.68.at_ref, bf16[256,1024]{1,0:T(8,128)(2,1)S(1)} %get-tuple-element.78.refs_0_, ...), custom_call_target="tpu_custom_call", output_to_operand_aliasing={{0}: (6, {}), {1}: (7, {}), {2}: (8, {})} | custom-call | tf_op jit(solution)/shard_map/pallas_call | solution.py:457
  35.5 3.5 %collective-permute-start.17 = (bf16[1024,256]{1,0:T(8,128)(2,1)S(1)}, bf16[1024,256]{1,0:T(8,128)(2,1)S(1)}, u32[]{:S(2)}, u32[]{:S(2)}) collective-permute-start(bf16[1024,256]{1,0:T(8,128)(2,1)S(1)} %get-tuple-element.84.refs_2_), channel_id=1, source_target_pairs={{0,8},{8,16},{16,24},{1,9},{9,17},{17,25},{2,10},{10,18},{18,26},{... | collective-permute-start | bytes 1572872 | tf_op jit(solution)/shard_map/ppermute | solution.py:481
  39.0 1.8 %shard_map.91 = (bf16[2048,1024]{1,0:T(8,128)(2,1)S(1)}, bf16[2048,512]{1,0:T(8,128)(2,1)S(1)}, bf16[2048,512]{1,0:T(8,128)(2,1)S(1)}, bf16[512,256]{1,0:T(8,128)(2,1)S(1)}, bf16[2048,128]{1,0:T(8,128)(2,1)S(1)}) custom-call(s32[2]{0:T(128)S(1)} %get-tuple-element.68.at_ref, ...), custom_call_target="tpu_custom_call", output_to_operand_aliasing={{0}: (6, {}), {1}: (7, {}), {2}: (8, {})} | custom-call | tf_op jit(solution)/shard_map/pallas_call | solution.py:457
  42.1 4.6 %collective-permute-start.18 = (bf16[512,256]{1,0:T(8,128)(2,1)S(1)}, bf16[512,256]{1,0:T(8,128)(2,1)S(1)}, u32[]{:S(2)}, u32[]{:S(2)}) collective-permute-start(bf16[512,256]{1,0:T(8,128)(2,1)S(1)} %get-tuple-element.94), channel_id=1, source_target_pairs={{0,8},{8,16},{16,24},{1,9},{9,17},{17,25},{2,10},{10,18},{18,26},{... | collective-permute-start | bytes 786440 | tf_op jit(solution)/shard_map/ppermute | solution.py:481
  46.6 5.8 %shard_map.92 = (f32[2048,128]{1,0:T(8,128)S(1)}, bf16[128,2048]{1,0:T(8,128)(2,1)S(1)}, bf16[128,2048]{1,0:T(8,128)(2,1)S(1)}, bf16[128,2048]{1,0:T(8,128)(2,1)S(1)}) custom-call(s32[32]{0:T(128)S(1)} %get-tuple-element.69.lo_ref, s32[32]{0:T(128)S(1)} %get-tuple-element.70.nv_ref, bf16[2048,512]{1,0:T(8,128)(2,1)S(1)} %get-tuple-element.93.act_ref, ...), custom_call_target="tpu_custom_call" | custom-call | tf_op jit(solution)/shard_map/pallas_call | solution.py:457
  52.5 3.8 %collective-permute-done.18.kvc_ref = bf16[512,256]{1,0:T(8,128)(2,1)S(1)} collective-permute-done((bf16[512,256]{1,0:T(8,128)(2,1)S(1)}, bf16[512,256]{1,0:T(8,128)(2,1)S(1)}, u32[]{:S(2)}, u32[]{:S(2)}) %collective-permute-start.18) | collective-permute-done | bytes 262176 | tf_op jit(solution)/shard_map/ppermute | solution.py:481
  59.5 1.5 %collective-permute-start.22 = (bf16[320,128]{1,0:T(8,128)(2,1)S(1)}, bf16[320,128]{1,0:T(8,128)(2,1)S(1)}, u32[]{:S(2)}, u32[]{:S(2)}) collective-permute-start(bf16[320,128]{1,0:T(8,128)(2,1)S(1)} %get-tuple-element.102), channel_id=1, source_target_pairs={{0,4},{1,5},{2,6},{3,7},{4,0},{5,1},{6,2},{7,3},{8,12},{9,13},{10,... | collective-permute-start | bytes 245768 | tf_op jit(solution)/shard_map/ppermute | solution.py:475
  61.2 1.7 %collective-permute-done.20.refs_2_ = bf16[320,128]{1,0:T(8,128)(2,1)S(1)} collective-permute-done((bf16[320,128]{1,0:T(8,128)(2,1)S(1)}, bf16[320,128]{1,0:T(8,128)(2,1)S(1)}, u32[]{:S(2)}, u32[]{:S(2)}) %collective-permute-start.20) | collective-permute-done | bytes 81952 | tf_op jit(solution)/shard_map/ppermute | solution.py:475
  62.9 1.5 %collective-permute-start.24 = (bf16[320,128]{1,0:T(8,128)(2,1)S(1)}, bf16[320,128]{1,0:T(8,128)(2,1)S(1)}, u32[]{:S(2)}, u32[]{:S(2)}) collective-permute-start(bf16[320,128]{1,0:T(8,128)(2,1)S(1)} %get-tuple-element.104), channel_id=1, source_target_pairs={{0,6},{1,7},{2,4},{3,5},{4,2},{5,3},{6,0},{7,1},{8,14},{9,15},{10,... | collective-permute-start | bytes 245768 | tf_op jit(solution)/shard_map/ppermute | solution.py:475
  65.8 2.4 %collective-permute-done.24.refs_6_ = bf16[320,128]{1,0:T(8,128)(2,1)S(1)} collective-permute-done((bf16[320,128]{1,0:T(8,128)(2,1)S(1)}, bf16[320,128]{1,0:T(8,128)(2,1)S(1)}, u32[]{:S(2)}, u32[]{:S(2)}) %collective-permute-start.24) | collective-permute-done | bytes 81952 | tf_op jit(solution)/shard_map/ppermute | solution.py:475
  68.2 1.7 %collective-permute-done.25.refs_7_ = bf16[320,128]{1,0:T(8,128)(2,1)S(1)} collective-permute-done((bf16[320,128]{1,0:T(8,128)(2,1)S(1)}, bf16[320,128]{1,0:T(8,128)(2,1)S(1)}, u32[]{:S(2)}, u32[]{:S(2)}) %collective-permute-start.25) | collective-permute-done | bytes 81952 | tf_op jit(solution)/shard_map/ppermute | solution.py:475
  69.9 1.8 %shard_map.95 = (bf16[2048,128]{1,0:T(8,128)(2,1)S(1)}, bf16[128,2048]{1,0:T(8,128)(2,1)S(1)}) custom-call(s32[32]{0:T(128)S(1)} %get-tuple-element.70.nv_ref, s32[2]{0:T(128)S(1)} %get-tuple-element.68.at_ref, bf16[2048,512]{1,0:T(8,128)(2,1)S(1)} %get-tuple-element.93.act_ref, bf16[2048,512]{1,0:T(8,128)(2,1)S(1)} %get-tuple-element.95.slope_ref, ...), custom_call_target="tpu_custom_call" | custom-call | tf_op jit(solution)/shard_map/pallas_call | solution.py:457
  73.0 8.7 %shard_map.96 = (bf16[128,2048]{1,0:T(8,128)(2,1)S(1)}, bf16[2048,128]{1,0:T(8,128)(2,1)S(1)}, f32[2048,256]{1,0:T(8,128)S(1)}) custom-call(s32[32]{0:T(128)S(1)} %get-tuple-element.69.lo_ref, bf16[2048,512]{1,0:T(8,128)(2,1)S(1)} %get-tuple-element.93.act_ref, bf16[128,2048]{1,0:T(8,128)(2,1)S(1)} %get-tuple-element.107.slope_qt_ref, ...), custom_call_target="tpu_custom_call" | custom-call | tf_op jit(solution)/shard_map/pallas_call | solution.py:457
  81.7 9.0 %collective-permute-done.27.g_ref = bf16[2048,128]{1,0:T(8,128)(2,1)S(1)} collective-permute-done((bf16[2048,128]{1,0:T(8,128)(2,1)S(1)}, bf16[2048,128]{1,0:T(8,128)(2,1)S(1)}, u32[]{:S(2)}, u32[]{:S(2)}) %collective-permute-start.27) | collective-permute-done | bytes 524320 | tf_op jit(solution)/shard_map/ppermute | solution.py:484
  90.7 7.1 %shard_map.97 = (bf16[256,384]{1,0:T(8,128)(2,1)S(1)}, bf16[1024,384]{1,0:T(8,128)(2,1)S(1)}, bf16[512,384]{1,0:T(8,128)(2,1)S(1)}, bf16[512,384]{1,0:T(8,128)(2...) custom-call(s32[32]{0:T(128)S(1)} %get-tuple-element.69.lo_ref, ...), custom_call_target="tpu_custom_call" | custom-call | tf_op jit(solution)/shard_map/pallas_call | solution.py:457
  97.9 2.2 %collective-permute-done.28.other_ref = bf16[1024,384]{1,0:T(8,128)(2,1)S(1)} collective-permute-done((bf16[1024,384]{1,0:T(8,128)(2,1)S(1)}, bf16[1024,384]{1,0:T(8,128)(2,1)S(1)}, u32[]{:S(2)}, u32[]{:S(2)}) %collective-permute-start.28) | collective-permute-done | bytes 786464 | tf_op jit(solution)/shard_map/ppermute | solution.py:475
  100.5 1.7 %collective-permute-start.30 = (bf16[512,384]{1,0:T(8,128)(2,1)S(1)}, bf16[512,384]{1,0:T(8,128)(2,1)S(1)}, u32[]{:S(2)}, u32[]{:S(2)}) collective-permute-start(bf16[512,384]{1,0:T(8,128)(2,1)S(1)} %get-tuple-element.126), channel_id=1, source_target_pairs={{0,4},{1,5},{2,6},{3,7},{4,0},{5,1},{6,2},{7,3},{8,12},{9,13},{10,... | collective-permute-start | bytes 1179656 | tf_op jit(solution)/shard_map/ppermute | solution.py:475
  102.2 1.6 %collective-permute-start.31 = (bf16[512,384]{1,0:T(8,128)(2,1)S(1)}, bf16[512,384]{1,0:T(8,128)(2,1)S(1)}, u32[]{:S(2)}, u32[]{:S(2)}) collective-permute-start(bf16[512,384]{1,0:T(8,128)(2,1)S(1)} %get-tuple-element.127), channel_id=1, source_target_pairs={{0,6},{1,7},{2,4},{3,5},{4,2},{5,3},{6,0},{7,1},{8,14},{9,15},{10,... | collective-permute-start | bytes 1179656 | tf_op jit(solution)/shard_map/ppermute | solution.py:475
  103.8 8.5 %collective-permute-done.32.got_ref = bf16[256,1024]{1,0:T(8,128)(2,1)S(1)} collective-permute-done((bf16[256,1024]{1,0:T(8,128)(2,1)S(1)}, bf16[256,1024]{1,0:T(8,128)(2,1)S(1)}, u32[]{:S(2)}, u32[]{:S(2)}) %collective-permute-start.32) | collective-permute-done | bytes 524320 | tf_op jit(solution)/shard_map/ppermute | solution.py:571
  112.3 7.7 %collective-permute-start.33 = (bf16[128,1024]{1,0:T(8,128)(2,1)S(1)}, bf16[128,1024]{1,0:T(8,128)(2,1)S(1)}, u32[]{:S(2)}, u32[]{:S(2)}) collective-permute-start(bf16[128,1024]{1,0:T(8,128)(2,1)S(1)} %get-tuple-element.132), channel_id=1, source_target_pairs={{0,16},{8,24},{16,0},{24,8},{1,17},{9,25},{17,1},{25,9},{2,18},{10... | collective-permute-start | bytes 786440 | tf_op jit(solution)/shard_map/ppermute | solution.py:571
  120.0 3.6 %shard_map.94 = (bf16[256,1024]{1,0:T(8,128)(2,1)}, f32[256,1024]{1,0:T(8,128)S(1)}) custom-call(s32[2]{0:T(128)S(1)} %get-tuple-element.68.at_ref, bf16[320,128]{1,0:T(8,128)(2,1)S(1)} %get-tuple-element.98.refs_0_, bf16[320,128]{1,0:T(8,128)(2,1)S(1)} %collective-permute-done.19.refs_1_, bf16[320,128]{1,0:T(8,128)(2,1)S(1)} %collective-permute-done.20.refs_2_, ...), custom_call_target="tpu_custom_call" | custom-call | tf_op jit(solution)/shard_map/pallas_call | solution.py:457
  123.5 8.1 %collective-permute-done.33.got_ref = bf16[128,1024]{1,0:T(8,128)(2,1)S(1)} collective-permute-done((bf16[128,1024]{1,0:T(8,128)(2,1)S(1)}, bf16[128,1024]{1,0:T(8,128)(2,1)S(1)}, u32[]{:S(2)}, u32[]{:S(2)}) %collective-permute-start.33) | collective-permute-done | bytes 262176 | tf_op jit(solution)/shard_map/ppermute | solution.py:571
  133.5 3.7 %shard_map.101 = bf16[256,1024]{1,0:T(8,128)(2,1)} custom-call(s32[2]{0:T(128)S(1)} %get-tuple-element.68.at_ref, bf16[256,384]{1,0:T(8,128)(2,1)S(1)} %get-tuple-element.120.own_ref, bf16[1024,384]{1,0:T(8,128)(2,1)S(1)} %collective-permute-done.28.other_ref, bf16[512,384]{1,0:T(8,128)(2,1)S(1)} %collective-permute-done.29.refs_0_, ...), custom_call_target="tpu_custom_call" | custom-call | tf_op jit(solution)/shard_map/pallas_call | solution.py:457
  (74 shorter events, 20.6 us)
Async XLA Ops:
  0.6 4.6 %collective-permute-start.2 = (bf16[256,1024]{1,0:T(8,128)(2,1)}, bf16[256,1024]{1,0:T(8,128)(2,1)S(1)}, u32[]{:S(2)}, u32[]{:S(2)}) collective-permute-start(bf16[256,1024]{1,0:T(8,128)(2,1)} %refs_4_.1), channel_id=1, source_target_pairs={{0,1},{1,0},{2,3},{3,2},{4,5},{5,4},{6,7},{7,6},{8,9},{9,8},{10,11... | collective-permute-start | bytes 1572872 | tf_op jit(solution)/shard_map/ppermute | solution.py:475
  1.2 15.3 %collective-permute-start = (bf16[256,1024]{1,0:T(8,128)(2,1)}, bf16[256,1024]{1,0:T(8,128)(2,1)S(1)}, u32[]{:S(2)}, u32[]{:S(2)}) collective-permute-start(bf16[256,1024]{1,0:T(8,128)(2,1)} %refs_4_.1), channel_id=1, source_target_pairs={{0,2},{1,3},{2,0},{3,1},{4,6},{5,7},{6,4},{7,5},{8,10},{9,11},{10,... | collective-permute-start | bytes 1572872 | tf_op jit(solution)/shard_map/ppermute | solution.py:475
  3.7 14.2 %collective-permute-start.1 = (bf16[256,1024]{1,0:T(8,128)(2,1)}, bf16[256,1024]{1,0:T(8,128)(2,1)S(1)}, u32[]{:S(2)}, u32[]{:S(2)}) collective-permute-start(bf16[256,1024]{1,0:T(8,128)(2,1)} %refs_4_.1), channel_id=1, source_target_pairs={{0,4},{1,5},{2,6},{3,7},{4,0},{5,1},{6,2},{7,3},{8,12},{9,13},{10,... | collective-permute-start | bytes 1572872 | tf_op jit(solution)/shard_map/ppermute | solution.py:475
  11.1 11.2 %collective-permute-start.3 = (bf16[512,256]{1,0:T(8,128)(2,1)S(1)}, bf16[512,256]{1,0:T(8,128)(2,1)S(1)}, u32[]{:S(2)}, u32[]{:S(2)}) collective-permute-start(bf16[512,256]{1,0:T(8,128)(2,1)S(1)} %get-tuple-element.71.after_ref), channel_id=1, source_target_pairs={{0,8},{8,16},{16,24},{1,9},{9,17},{17,25},{2,10},{10,18},{18,26},{... | collective-permute-start | bytes 786440 | tf_op jit(solution)/shard_map/ppermute | solution.py:481
  15.7 3.8 %collective-permute-start.4 = (bf16[256,128]{1,0:T(8,128)(2,1)S(1)}, bf16[256,128]{1,0:T(8,128)(2,1)S(1)}, u32[]{:S(2)}, u32[]{:S(2)}) collective-permute-start(bf16[256,128]{1,0:T(8,128)(2,1)S(1)} %get-tuple-element.72.refs_9_), channel_id=1, source_target_pairs={{0,1},{1,0},{2,3},{3,2},{4,5},{5,4},{6,7},{7,6},{8,9},{9,8},{10,11... | collective-permute-start | bytes 196616 | tf_op jit(solution)/shard_map/ppermute | solution.py:475
  15.7 5.0 %collective-permute-start.5 = (bf16[256,128]{1,0:T(8,128)(2,1)S(1)}, bf16[256,128]{1,0:T(8,128)(2,1)S(1)}, u32[]{:S(2)}, u32[]{:S(2)}) collective-permute-start(bf16[256,128]{1,0:T(8,128)(2,1)S(1)} %get-tuple-element.73.refs_10_), channel_id=1, source_target_pairs={{0,2},{1,3},{2,0},{3,1},{4,6},{5,7},{6,4},{7,5},{8,10},{9,11},{10,... | collective-permute-start | bytes 196616 | tf_op jit(solution)/shard_map/ppermute | solution.py:475
  16.5 4.7 %collective-permute-start.6 = (bf16[256,128]{1,0:T(8,128)(2,1)S(1)}, bf16[256,128]{1,0:T(8,128)(2,1)S(1)}, u32[]{:S(2)}, u32[]{:S(2)}) collective-permute-start(bf16[256,128]{1,0:T(8,128)(2,1)S(1)} %get-tuple-element.74.refs_11_), channel_id=1, source_target_pairs={{0,3},{1,2},{2,1},{3,0},{4,7},{5,6},{6,5},{7,4},{8,11},{9,10},{10,... | collective-permute-start | bytes 196616 | tf_op jit(solution)/shard_map/ppermute | solution.py:475
  17.9 4.4 %collective-permute-start.7 = (bf16[256,128]{1,0:T(8,128)(2,1)S(1)}, bf16[256,128]{1,0:T(8,128)(2,1)S(1)}, u32[]{:S(2)}, u32[]{:S(2)}) collective-permute-start(bf16[256,128]{1,0:T(8,128)(2,1)S(1)} %get-tuple-element.75.refs_12_), channel_id=1, source_target_pairs={{0,4},{1,5},{2,6},{3,7},{4,0},{5,1},{6,2},{7,3},{8,12},{9,13},{10,... | collective-permute-start | bytes 196616 | tf_op jit(solution)/shard_map/ppermute | solution.py:475
  22.5 4.6 %collective-permute-start.11 = (bf16[256,1024]{1,0:T(8,128)(2,1)S(1)}, bf16[256,1024]{1,0:T(8,128)(2,1)S(1)}, u32[]{:S(2)}, u32[]{:S(2)}) collective-permute-start(bf16[256,1024]{1,0:T(8,128)(2,1)S(1)} %get-tuple-element.79.refs_2_), channel_id=1, source_target_pairs={{0,1},{1,0},{2,3},{3,2},{4,5},{5,4},{6,7},{7,6},{8,9},{9,8},{10,11... | collective-permute-start | bytes 1572872 | tf_op jit(solution)/shard_map/ppermute | solution.py:475
  23.0 11.7 %collective-permute-start.8 = (bf16[128,1024]{1,0:T(8,128)(2,1)S(1)}, bf16[128,1024]{1,0:T(8,128)(2,1)S(1)}, u32[]{:S(2)}, u32[]{:S(2)}) collective-permute-start(bf16[128,1024]{1,0:T(8,128)(2,1)S(1)} %get-tuple-element.76), channel_id=1, source_target_pairs={{0,4},{1,5},{2,6},{3,7},{4,0},{5,1},{6,2},{7,3},{8,12},{9,13},{10,... | collective-permute-start | bytes 786440 | tf_op jit(solution)/shard_map/ppermute | solution.py:475
  24.5 10.2 %collective-permute-start.9 = (bf16[128,1024]{1,0:T(8,128)(2,1)S(1)}, bf16[128,1024]{1,0:T(8,128)(2,1)S(1)}, u32[]{:S(2)}, u32[]{:S(2)}) collective-permute-start(bf16[128,1024]{1,0:T(8,128)(2,1)S(1)} %get-tuple-element.77), channel_id=1, source_target_pairs={{0,2},{1,3},{2,0},{3,1},{4,6},{5,7},{6,4},{7,5},{8,10},{9,11},{10,... | collective-permute-start | bytes 786440 | tf_op jit(solution)/shard_map/ppermute | solution.py:475
  25.0 9.1 %collective-permute-start.12 = (bf16[256,128]{1,0:T(8,128)(2,1)S(1)}, bf16[256,128]{1,0:T(8,128)(2,1)S(1)}, u32[]{:S(2)}, u32[]{:S(2)}) collective-permute-start(bf16[256,128]{1,0:T(8,128)(2,1)S(1)} %get-tuple-element.85.refs_13_), channel_id=1, source_target_pairs={{0,5},{1,4},{2,7},{3,6},{4,1},{5,0},{6,3},{7,2},{8,13},{9,12},{10,... | collective-permute-start | bytes 196616 | tf_op jit(solution)/shard_map/ppermute | solution.py:475
  25.0 9.6 %collective-permute-start.13 = (bf16[256,128]{1,0:T(8,128)(2,1)S(1)}, bf16[256,128]{1,0:T(8,128)(2,1)S(1)}, u32[]{:S(2)}, u32[]{:S(2)}) collective-permute-start(bf16[256,128]{1,0:T(8,128)(2,1)S(1)} %get-tuple-element.86.refs_14_), channel_id=1, source_target_pairs={{0,6},{1,7},{2,4},{3,5},{4,2},{5,3},{6,0},{7,1},{8,14},{9,15},{10,... | collective-permute-start | bytes 196616 | tf_op jit(solution)/shard_map/ppermute | solution.py:475
  27.1 7.5 %collective-permute-start.14 = (bf16[256,128]{1,0:T(8,128)(2,1)S(1)}, bf16[256,128]{1,0:T(8,128)(2,1)S(1)}, u32[]{:S(2)}, u32[]{:S(2)}) collective-permute-start(bf16[256,128]{1,0:T(8,128)(2,1)S(1)} %get-tuple-element.87.refs_15_), channel_id=1, source_target_pairs={{0,7},{1,6},{2,5},{3,4},{4,3},{5,2},{6,1},{7,0},{8,15},{9,14},{10,... | collective-permute-start | bytes 196616 | tf_op jit(solution)/shard_map/ppermute | solution.py:475
  34.7 4.3 %collective-permute-start.15 = (bf16[128,1024]{1,0:T(8,128)(2,1)S(1)}, bf16[128,1024]{1,0:T(8,128)(2,1)S(1)}, u32[]{:S(2)}, u32[]{:S(2)}) collective-permute-start(bf16[128,1024]{1,0:T(8,128)(2,1)S(1)} %get-tuple-element.88.refs_0_), channel_id=1, source_target_pairs={{0,1},{1,0},{2,3},{3,2},{4,5},{5,4},{6,7},{7,6},{8,9},{9,8},{10,11... | collective-permute-start | bytes 786440 | tf_op jit(solution)/shard_map/ppermute | solution.py:475
  35.4 3.6 %collective-permute-start.16 = (bf16[128,1024]{1,0:T(8,128)(2,1)S(1)}, bf16[128,1024]{1,0:T(8,128)(2,1)S(1)}, u32[]{:S(2)}, u32[]{:S(2)}) collective-permute-start(bf16[128,1024]{1,0:T(8,128)(2,1)S(1)} %get-tuple-element.89.refs_1_), channel_id=1, source_target_pairs={{0,1},{1,0},{2,3},{3,2},{4,5},{5,4},{6,7},{7,6},{8,9},{9,8},{10,11... | collective-permute-start | bytes 786440 | tf_op jit(solution)/shard_map/ppermute | solution.py:475
  35.5 17.0 %collective-permute-start.17 = (bf16[1024,256]{1,0:T(8,128)(2,1)S(1)}, bf16[1024,256]{1,0:T(8,128)(2,1)S(1)}, u32[]{:S(2)}, u32[]{:S(2)}) collective-permute-start(bf16[1024,256]{1,0:T(8,128)(2,1)S(1)} %get-tuple-element.84.refs_2_), channel_id=1, source_target_pairs={{0,8},{8,16},{16,24},{1,9},{9,17},{17,25},{2,10},{10,18},{18,26},{... | collective-permute-start | bytes 1572872 | tf_op jit(solution)/shard_map/ppermute | solution.py:481
  40.8 29.1 %collective-permute-start.26 = (bf16[2048,128]{1,0:T(8,128)(2,1)S(1)}, bf16[2048,128]{1,0:T(8,128)(2,1)S(1)}, u32[]{:S(2)}, u32[]{:S(2)}) collective-permute-start(bf16[2048,128]{1,0:T(8,128)(2,1)S(1)} %get-tuple-element.111), channel_id=1, source_target_pairs={{8,0},{16,8},{24,16},{9,1},{17,9},{25,17},{10,2},{18,10},{26,18},{... | collective-permute-start | bytes 1572872 | tf_op jit(solution)/shard_map/ppermute | solution.py:484
  42.1 14.3 %collective-permute-start.18 = (bf16[512,256]{1,0:T(8,128)(2,1)S(1)}, bf16[512,256]{1,0:T(8,128)(2,1)S(1)}, u32[]{:S(2)}, u32[]{:S(2)}) collective-permute-start(bf16[512,256]{1,0:T(8,128)(2,1)S(1)} %get-tuple-element.94), channel_id=1, source_target_pairs={{0,8},{8,16},{16,24},{1,9},{9,17},{17,25},{2,10},{10,18},{18,26},{... | collective-permute-start | bytes 786440 | tf_op jit(solution)/shard_map/ppermute | solution.py:481
  57.5 3.5 %collective-permute-start.19 = (bf16[320,128]{1,0:T(8,128)(2,1)S(1)}, bf16[320,128]{1,0:T(8,128)(2,1)S(1)}, u32[]{:S(2)}, u32[]{:S(2)}) collective-permute-start(bf16[320,128]{1,0:T(8,128)(2,1)S(1)} %get-tuple-element.99), channel_id=1, source_target_pairs={{0,1},{1,0},{2,3},{3,2},{4,5},{5,4},{6,7},{7,6},{8,9},{9,8},{10,11... | collective-permute-start | bytes 245768 | tf_op jit(solution)/shard_map/ppermute | solution.py:475
  57.6 5.3 %collective-permute-start.20 = (bf16[320,128]{1,0:T(8,128)(2,1)S(1)}, bf16[320,128]{1,0:T(8,128)(2,1)S(1)}, u32[]{:S(2)}, u32[]{:S(2)}) collective-permute-start(bf16[320,128]{1,0:T(8,128)(2,1)S(1)} %get-tuple-element.100), channel_id=1, source_target_pairs={{0,2},{1,3},{2,0},{3,1},{4,6},{5,7},{6,4},{7,5},{8,10},{9,11},{10,... | collective-permute-start | bytes 245768 | tf_op jit(solution)/shard_map/ppermute | solution.py:475
  58.3 6.1 %collective-permute-start.21 = (bf16[320,128]{1,0:T(8,128)(2,1)S(1)}, bf16[320,128]{1,0:T(8,128)(2,1)S(1)}, u32[]{:S(2)}, u32[]{:S(2)}) collective-permute-start(bf16[320,128]{1,0:T(8,128)(2,1)S(1)} %get-tuple-element.101), channel_id=1, source_target_pairs={{0,3},{1,2},{2,1},{3,0},{4,7},{5,6},{6,5},{7,4},{8,11},{9,10},{10,... | collective-permute-start | bytes 245768 | tf_op jit(solution)/shard_map/ppermute | solution.py:475
  59.5 6.0 %collective-permute-start.22 = (bf16[320,128]{1,0:T(8,128)(2,1)S(1)}, bf16[320,128]{1,0:T(8,128)(2,1)S(1)}, u32[]{:S(2)}, u32[]{:S(2)}) collective-permute-start(bf16[320,128]{1,0:T(8,128)(2,1)S(1)} %get-tuple-element.102), channel_id=1, source_target_pairs={{0,4},{1,5},{2,6},{3,7},{4,0},{5,1},{6,2},{7,3},{8,12},{9,13},{10,... | collective-permute-start | bytes 245768 | tf_op jit(solution)/shard_map/ppermute | solution.py:475
  61.0 4.9 %collective-permute-start.23 = (bf16[320,128]{1,0:T(8,128)(2,1)S(1)}, bf16[320,128]{1,0:T(8,128)(2,1)S(1)}, u32[]{:S(2)}, u32[]{:S(2)}) collective-permute-start(bf16[320,128]{1,0:T(8,128)(2,1)S(1)} %get-tuple-element.103), channel_id=1, source_target_pairs={{0,5},{1,4},{2,7},{3,6},{4,1},{5,0},{6,3},{7,2},{8,13},{9,12},{10,... | collective-permute-start | bytes 245768 | tf_op jit(solution)/shard_map/ppermute | solution.py:475
  62.9 5.3 %collective-permute-start.24 = (bf16[320,128]{1,0:T(8,128)(2,1)S(1)}, bf16[320,128]{1,0:T(8,128)(2,1)S(1)}, u32[]{:S(2)}, u32[]{:S(2)}) collective-permute-start(bf16[320,128]{1,0:T(8,128)(2,1)S(1)} %get-tuple-element.104), channel_id=1, source_target_pairs={{0,6},{1,7},{2,4},{3,5},{4,2},{5,3},{6,0},{7,1},{8,14},{9,15},{10,... | collective-permute-start | bytes 245768 | tf_op jit(solution)/shard_map/ppermute | solution.py:475
  64.4 5.5 %collective-permute-start.25 = (bf16[320,128]{1,0:T(8,128)(2,1)S(1)}, bf16[320,128]{1,0:T(8,128)(2,1)S(1)}, u32[]{:S(2)}, u32[]{:S(2)}) collective-permute-start(bf16[320,128]{1,0:T(8,128)(2,1)S(1)} %get-tuple-element.105), channel_id=1, source_target_pairs={{0,7},{1,6},{2,5},{3,4},{4,3},{5,2},{6,1},{7,0},{8,15},{9,14},{10,... | collective-permute-start | bytes 245768 | tf_op jit(solution)/shard_map/ppermute | solution.py:475
  71.7 19.0 %collective-permute-start.27 = (bf16[2048,128]{1,0:T(8,128)(2,1)S(1)}, bf16[2048,128]{1,0:T(8,128)(2,1)S(1)}, u32[]{:S(2)}, u32[]{:S(2)}) collective-permute-start(bf16[2048,128]{1,0:T(8,128)(2,1)S(1)} %get-tuple-element.112.g_ref), channel_id=1, source_target_pairs={{8,0},{16,8},{24,16},{9,1},{17,9},{25,17},{10,2},{18,10},{26,18},{... | collective-permute-start | bytes 1572872 | tf_op jit(solution)/shard_map/ppermute | solution.py:484
  97.9 14.3 %collective-permute-start.32 = (bf16[256,1024]{1,0:T(8,128)(2,1)S(1)}, bf16[256,1024]{1,0:T(8,128)(2,1)S(1)}, u32[]{:S(2)}, u32[]{:S(2)}) collective-permute-start(bf16[256,1024]{1,0:T(8,128)(2,1)S(1)} %get-tuple-element.130), channel_id=1, source_target_pairs={{0,8},{8,0},{16,24},{24,16},{1,9},{9,1},{17,25},{25,17},{2,10},{10... | collective-permute-start | bytes 1572872 | tf_op jit(solution)/shard_map/ppermute | solution.py:571
  100.2 32.3 %collective-permute-start.29 = (bf16[512,384]{1,0:T(8,128)(2,1)S(1)}, bf16[512,384]{1,0:T(8,128)(2,1)S(1)}, u32[]{:S(2)}, u32[]{:S(2)}) collective-permute-start(bf16[512,384]{1,0:T(8,128)(2,1)S(1)} %get-tuple-element.125), channel_id=1, source_target_pairs={{0,2},{1,3},{2,0},{3,1},{4,6},{5,7},{6,4},{7,5},{8,10},{9,11},{10,... | collective-permute-start | bytes 1179656 | tf_op jit(solution)/shard_map/ppermute | solution.py:475
  100.5 32.0 %collective-permute-start.30 = (bf16[512,384]{1,0:T(8,128)(2,1)S(1)}, bf16[512,384]{1,0:T(8,128)(2,1)S(1)}, u32[]{:S(2)}, u32[]{:S(2)}) collective-permute-start(bf16[512,384]{1,0:T(8,128)(2,1)S(1)} %get-tuple-element.126), channel_id=1, source_target_pairs={{0,4},{1,5},{2,6},{3,7},{4,0},{5,1},{6,2},{7,3},{8,12},{9,13},{10,... | collective-permute-start | bytes 1179656 | tf_op jit(solution)/shard_map/ppermute | solution.py:475
  102.2 30.3 %collective-permute-start.31 = (bf16[512,384]{1,0:T(8,128)(2,1)S(1)}, bf16[512,384]{1,0:T(8,128)(2,1)S(1)}, u32[]{:S(2)}, u32[]{:S(2)}) collective-permute-start(bf16[512,384]{1,0:T(8,128)(2,1)S(1)} %get-tuple-element.127), channel_id=1, source_target_pairs={{0,6},{1,7},{2,4},{3,5},{4,2},{5,3},{6,0},{7,1},{8,14},{9,15},{10,... | collective-permute-start | bytes 1179656 | tf_op jit(solution)/shard_map/ppermute | solution.py:475
  112.3 19.3 %collective-permute-start.33 = (bf16[128,1024]{1,0:T(8,128)(2,1)S(1)}, bf16[128,1024]{1,0:T(8,128)(2,1)S(1)}, u32[]{:S(2)}, u32[]{:S(2)}) collective-permute-start(bf16[128,1024]{1,0:T(8,128)(2,1)S(1)} %get-tuple-element.132), channel_id=1, source_target_pairs={{0,16},{8,24},{16,0},{24,8},{1,17},{9,25},{17,1},{25,9},{2,18},{10... | collective-permute-start | bytes 786440 | tf_op jit(solution)/shard_map/ppermute | solution.py:571
  (12 other events, 142.1 us)

commit v4 on v3

--- a/solution.py
+++ b/solution.py
@@ -29,10 +29,16 @@
 UQ, VK = slice(0, 2 * HD), slice(2 * HD, 4 * HD)
 
 
-def info_kernel(counts_ref, tails_ref, lo_ref, nv_ref, at_ref):
+def start_kernel(counts_ref, tails_ref, w_ref, lo_ref, nv_ref, at_ref, wh_ref, sems):
     group = lax.axis_index("g").astype(jnp.int32)
     at_ref[0] = group
-    at_ref[1] = lax.axis_index("h").astype(jnp.int32)
+    head = lax.axis_index("h").astype(jnp.int32)
+    at_ref[1] = head
+    copies = []
+    for i in range(4):
+        source = w_ref.at[:, lanes_at(PLACE[i] * (w_ref.shape[0] // HD) + head)]
+        copies.append(pltpu.make_async_copy(source, wh_ref.at[:, i * HD : (i + 1) * HD], sems.at[i]))
+        copies[i].start()
     base = group * MAXB
     for j in range(2 * MAXB):
         lo_ref[j] = j * BLK
@@ -50,6 +56,8 @@
         return end
 
     lax.fori_loop(0, counts_ref.shape[0], user, jnp.int32(0))
+    for copy in copies:
+        copy.wait()
 
 
 def by_half(t, ref, shape, dim):
@@ -96,21 +104,6 @@
     act_ref[rows, :] = act
     slope_ref[rows, :] = slope
     kv_ref[i * TILE : (i + 1) * TILE, :] = act[:, VK]
-
-
-def first_kernel(other_ref, tokens_ref, w_ref, normed_ref, act_ref, slope_ref, kv_ref, wh_ref, x_s, sems):
-    head, width = lax.axis_index("h").astype(jnp.int32), w_ref.shape[0]
-    copies = [pltpu.make_async_copy(tokens_ref, x_s, sems.at[4])]
-    for i in range(4):
-        source = w_ref.at[:, lanes_at(PLACE[i] * (width // HD) + head)]
-        copies.append(pltpu.make_async_copy(source, wh_ref.at[:, i * HD : (i + 1) * HD], sems.at[i]))
-    for copy in copies:
-        copy.start()
-    for copy in copies:
-        copy.wait()
-    outs = wh_ref, normed_ref, act_ref, slope_ref, kv_ref
-    store_rows(x_s[...], head, *outs, 0)
-    store_rows(other_ref[...], head ^ 1, *outs, 1)
 
 
 def proj_kernel(masks, pieces, last, at_ref, *refs):
@@ -152,11 +145,35 @@
     pass
 
 
-def d_gated_kernel(g_ref, w_ref, after_ref, *refs):
-    outs, d_s = refs[:-1], refs[-1]
-    d_s[...] = lax.dot_general(g_ref[...], w_ref[...], NT, preferred_element_type=F32).astype(BF16)
-    for mask in range(HEADS):
-        outs[mask][...] = d_s[:, lanes_at(lax.axis_index("h").astype(jnp.int32) ^ mask)]
+def merge_kernel(other_ref, *refs):
+    for i, ref in enumerate(refs[-3:]):
+        ref[TILE:, :] = other_ref[(i + 1) * TILE : (i + 2) * TILE, :]
+
+
+def places(refs):
+    mine, other, *pairs = refs
+    return [(mine, 0), (other, 0)] + [(ref, at) for ref in pairs for at in (0, TILE)]
+
+
+def outgoing(refs):
+    mine, other, *pairs = refs
+    found = [(mine, 0)] * HEADS
+    for i in range(4):
+        found[2 * i + 1] = other, i * TILE
+    for i in range(3):
+        found[2 * i + 2] = pairs[i], 0
+    return found
+
+
+def trade_outs(cols):
+    return [((TILE, cols), BF16), ((4 * TILE, cols), BF16)] + [((2 * TILE, cols), BF16)] * 3
+
+
+def d_gated_kernel(at_ref, g_ref, w_ref, *refs):
+    pieces, d_ref = refs[-6:-1], refs[-1]
+    d_ref[...] = lax.dot_general(g_ref[...], w_ref[...], NT, preferred_element_type=F32).astype(BF16)
+    for mask, (ref, at) in enumerate(outgoing(pieces)):
+        ref[at : at + TILE, :] = d_ref[:, lanes_at(at_ref[1] ^ mask)]
 
 
 def sigmoid(s):
@@ -198,15 +215,15 @@
 def fwd_far_kernel(
     lo_ref, nv_ref, at_ref, act_ref, kva_ref, kvb_ref, kvc_ref, near_ref, *refs,
 ):
-    dg_refs, (out_ref, kv_ref, kt_ref), pieces, (sum_s, attn_s, dg_s) = refs[:HEADS], refs[HEADS : HEADS + 3], refs[HEADS + 3 : -3], refs[-3:]
+    dg_refs, (out_ref, kv_ref, kt_ref, sum_ref), pieces, (attn_s, dg_s) = refs[:5], refs[5:9], refs[9:14], refs[14:]
     head = at_ref[1]
     slot = 0
     for ref in (kva_ref, kvb_ref, kvc_ref):
         for at in range(0, ref.shape[0], TILE):
             kv_ref[rows_at(slot ^ head), :] = ref[at : at + TILE, :]
             slot += 1
-    for mask in range(HEADS):
-        dg_s[rows_at(head ^ mask), :] = dg_refs[mask][...]
+    for mask, (ref, at) in enumerate(places(dg_refs)):
+        dg_s[rows_at(head ^ mask), :] = ref[at : at + TILE, :]
     first = jnp.minimum(lo_ref[0] + SPAN, SPAN) // CHUNK
     for t in range(TILES):
         rows = slice(t * TILE, (t + 1) * TILE)
@@ -239,15 +256,14 @@
         d_n = dg_s[rows, :].astype(F32) * act_ref[rows, U].astype(F32)
         square = lax.dot_general(ones, (attn * attn).astype(BF16), NT, preferred_element_type=F32)
         cross = lax.dot_general(ones, (attn * d_n).astype(BF16), NT, preferred_element_type=F32)
-        sum_s[t : t + 1, :] = square[:1]
-        sum_s[TILES + t : TILES + t + 1, :] = cross[:1]
-    sums = sum_s[...]
-    high = sums.astype(BF16)
-    low = (sums - high.astype(F32)).astype(BF16)
-    sums = jnp.concatenate([high[:, :HD], high[:, HD:], low[:, :HD], low[:, HD:]], axis=0)
-    for mask in range(HEADS):
-        pieces[mask][:TILE, :] = out_ref[rows_at(head ^ mask), :]
-        pieces[mask][TILE:, :] = sums
+        sum_ref[t : t + 1, :] = square[:1]
+        sum_ref[TILES + t : TILES + t + 1, :] = cross[:1]
+    for mask, (ref, at) in enumerate(outgoing(pieces)):
+        ref[at : at + TILE, :] = out_ref[rows_at(head ^ mask), :]
+
+
+def add_kernel(a_ref, b_ref, out_ref):
+    out_ref[...] = a_ref[...] + b_ref[...]
 
 
 def far_tiles(lo_ref):
@@ -256,11 +272,9 @@
 
 def row_scales(sum_refs):
     width = HEADS * HD
-    total = 0.0
-    for ref in sum_refs:
-        total += ref[TILE:, :].astype(F32)
-    n = 2 * TILES
-    total = jnp.concatenate([total[:n] + total[2 * n : 3 * n], total[n : 2 * n] + total[3 * n :]], axis=1)
+    total = sum_refs[0][...]
+    for ref in sum_refs[1:]:
+        total += ref[...]
     r = lax.rsqrt(total[:TILES] * (1.0 / width) + eps)
     c = total[TILES:] * (1.0 / width) * r
     return jnp.concatenate([r, c], axis=0).T
@@ -282,9 +296,9 @@
 
 
 def cotangent_kernel(nv_ref, at_ref, act_ref, slope_ref, attn_ref, *refs):
-    sum_refs, dg_refs, (g_ref, cols_ref, dg_s) = refs[:HEADS], refs[HEADS : 2 * HEADS], refs[-3:]
-    for mask in range(HEADS):
-        dg_s[rows_at(at_ref[1] ^ mask), :] = dg_refs[mask][...]
+    sum_refs, dg_refs, (g_ref, cols_ref, dg_s) = refs[:4], refs[4:9], refs[-3:]
+    for mask, (ref, at) in enumerate(places(dg_refs)):
+        dg_s[rows_at(at_ref[1] ^ mask), :] = ref[at : at + TILE, :]
     scales = row_scales(sum_refs)
     for t in range(TILES):
         rows = slice(t * TILE, (t + 1) * TILE)
@@ -342,7 +356,7 @@
 def keys_kernel(
     groups, lo_ref, at_ref, own_ref, act_ref, slope_ref, q_ref, g_ref, u_cols_ref, q_cols_ref, dq_ref, normed_ref, *refs
 ):
-    own_piece, other, pairs, (keep, send, cols_s, all_s, acc_s) = refs[0], refs[1], refs[2:5], refs[5:]
+    pieces, (keep, send, cols_s, all_s, acc_s) = refs[:5], refs[5:]
     first = jnp.minimum(lo_ref[2 * TILES], SPAN) // CHUNK
     key = lax.broadcasted_iota(jnp.int32, (CHUNK, TILE), 0)
 
@@ -368,18 +382,12 @@
 
     count = sum((lo_ref[2 * (TILES + t)] < SPAN).astype(jnp.int32) for t in range(TILES))
     lax.fori_loop(0, count, q_tile, 0)
-    places = {0: (own_piece, 0)}
-    for i in range(4):
-        places[2 * i + 1] = other, i * TILE
-    for i in range(3):
-        places[2 * i + 2] = pairs[i], 0
-    for mask in range(HEADS):
+    for mask, (ref, at) in enumerate(outgoing(pieces)):
         t = at_ref[1] ^ mask
         rows = rows_at(t)
         d = own_ref[rows, :] + jnp.where(t // 2 >= first, acc_s[rows, :], 0.0)
         d = (d * (SCALE / SPAN)).astype(BF16).astype(F32)
         d = (d * slope_ref[rows, VK].astype(F32)).astype(BF16)
-        ref, at = places[mask]
         ref[at : at + TILE, :HD] = dq_ref[rows, :]
         ref[at : at + TILE, HD:] = d
         cols_s[:, rows] = d.T
@@ -397,14 +405,9 @@
             send[(i - groups // 2) * size : (i + 1 - groups // 2) * size, :] = part
 
 
-def merge_kernel(other_ref, *refs):
-    for i, ref in enumerate(refs[-3:]):
-        ref[TILE:, :] = other_ref[(i + 1) * TILE : (i + 2) * TILE, :]
-
-
-def assemble(at_ref, refs, cols, out_s):
-    for mask in range(HEADS):
-        out_s[:, lanes_at(at_ref[1] ^ mask)] = refs[mask][:TILE, cols]
+def assemble(at_ref, refs, part, out_s):
+    for mask, (ref, at) in enumerate(places(refs)):
+        out_s[:, lanes_at(at_ref[1] ^ mask)] = ref[at : at + TILE, part * HD : (part + 1) * HD]
     return out_s[...]
 
 
@@ -414,35 +417,33 @@
 
 
 def rows_kernel(at_ref, *refs):
-    attn_refs, dg_refs = refs[:HEADS], refs[HEADS : 2 * HEADS]
-    tokens_ref, w_out_ref, w_in_ref, out_ref, dn_ref, row_s = refs[2 * HEADS :]
+    attn_refs, (dg_ref, tokens_ref, w_out_ref, w_in_ref, out_ref, dn_ref, row_s) = refs[:5], refs[5:]
     width = w_out_ref.shape[0]
     x = tokens_ref[...].astype(F32)
     u, slope = silu_and_slope(jnp.dot(norm_rows(x).astype(BF16), w_in_ref[:, :width], preferred_element_type=F32))
-    n = norm_rows(assemble(at_ref, attn_refs, slice(None), row_s).astype(F32))
+    n = norm_rows(assemble(at_ref, attn_refs, 0, row_s).astype(F32))
     gated = (n * u.astype(F32)).astype(BF16)
     y = jnp.dot(gated, w_out_ref[...], preferred_element_type=F32)
     out_ref[...] = (x + y).astype(BF16)
-    du = (assemble(at_ref, dg_refs, slice(None), row_s).astype(F32) * n).astype(BF16).astype(F32)
+    du = (dg_ref[...].astype(F32) * n).astype(BF16).astype(F32)
     du = (du * slope.astype(F32)).astype(BF16)
     dn_ref[...] = through(du, w_in_ref, 0)
 
 
-def half_kernel(keep_ref, got_ref, *refs):
+def half_kernel(later, keep_ref, got_ref, *refs):
+    refs = refs[later:]
     half = keep_ref.shape[0] // len(refs)
     refs[0][...] = keep_ref[:half, :] + got_ref[:half, :].astype(F32)
     if len(refs) > 1:
         refs[1][...] = (keep_ref[half:, :] + got_ref[half:, :].astype(F32)).astype(BF16)
 
 
-def last_kernel(at_ref, own_ref, other_ref, *refs):
-    pairs, (dn_ref, tokens_ref, grad_ref, w_in_ref, after_ref, out_ref, row_s) = refs[:3], refs[3:]
-    pieces = [(own_ref, 0), (other_ref, 0)] + [(ref, at) for ref in pairs for at in (0, TILE)]
+def last_kernel(at_ref, *refs):
+    pieces, (dn_ref, tokens_ref, grad_ref, w_in_ref, out_ref, end_ref, row_s) = refs[:5], refs[5:]
+    end_ref[...] = jnp.zeros(end_ref.shape, F32)
     dn = dn_ref[...]
     for i, branch in enumerate((2, 1, 3)):
-        for mask, (ref, at) in enumerate(pieces):
-            row_s[:, lanes_at(at_ref[1] ^ mask)] = ref[at : at + TILE, i * HD : (i + 1) * HD]
-        dn += through(row_s[...], w_in_ref, branch)
+        dn += through(assemble(at_ref, pieces, i, row_s), w_in_ref, branch)
     x = tokens_ref[...].astype(F32)
     r = lax.rsqrt(jnp.mean(x * x, axis=-1, keepdims=True) + eps)
     n = x * r
@@ -474,36 +475,52 @@
     def swap(x, mask):
         return lax.ppermute(x, "h", [(i, i ^ mask) for i in range(HEADS)])
 
-    def trade(pieces):
-        return [pieces[0]] + [swap(pieces[mask], mask) for mask in range(1, HEADS)]
-
     def onward(x):
         return lax.ppermute(x, "g", [(i, i + 1) for i in range(groups - 1)])
 
     def backward(x):
         return lax.ppermute(x, "g", [(i + 1, i) for i in range(groups - 1)])
 
+    def trade(pieces, after=(), merged=None):
+        mine, other, *pairs = pieces
+        other = swap(other, 1)
+        pairs = call(
+            merge_kernel,
+            (),
+            (other,),
+            [(x.shape, BF16) for x in pairs],
+            after=(*pairs, *after),
+            aliases={1: 0, 2: 1, 3: 2},
+            limit=4,
+        )
+        if merged is not None:
+            merged.extend(pairs)
+        return [mine, other] + [swap(x, mask) for x, mask in zip(pairs, (2, 4, 6))]
+
     x_rows, y_rows = swap(tokens, 2), swap(tokens, 4)
-    *kept, kv, w_head = call(
-        first_kernel,
+    other = swap(tokens, 1)
+    *info, w_head = call(
+        start_kernel,
+        (block_counts, tails),
         (),
-        (swap(tokens, 1),),
-        proj_outs(width, 2) + [((width, 4 * HD), BF16)],
-        [(own, BF16)],
-        (tokens, w_in),
-        limit=48,
-        sems=5,
-    )
+        [((2 * MAXB,), jnp.int32)] * 2 + [((2,), jnp.int32), ((width, 4 * HD), BF16)],
+        after=(w_in,),
+        limit=51,
+        sems=4,
+    )
+    *kept, kv = project(info, (0, 1), ((tokens,), (other,)), w_head, ())
     far_kv = [onward(kv)]
-    dg_own = call(d_gated_kernel, (), (grad_out, w_out), [(piece, BF16)] * HEADS, [(own, BF16)], (kv,))
-    d_gated = trade(dg_own)
-    info = call(info_kernel, (block_counts, tails), (), [((2 * MAXB,), jnp.int32)] * 2 + [((2,), jnp.int32)])
+    *dg_pieces, dg_own = call(
+        d_gated_kernel, info[2:], (grad_out, w_out), trade_outs(HD) + [(own, BF16)], after=(kv,)
+    )
+    merged = []
+    d_gated = trade(dg_pieces, merged=merged)
     x_rows, y_rows, x_half, y_half = call(
         cut_kernel,
         (),
         (x_rows, y_rows),
         [(own, BF16), (own, BF16), (half, BF16), (half, BF16)],
-        after=(far_kv[0], *d_gated[1:5]),
+        after=(far_kv[0], merged[0]),
         aliases={0: 0, 1: 1},
         limit=4,
     )
@@ -511,21 +528,22 @@
     chunks = ((x_rows,), (swap(x_rows, 1),), (y_rows,), (swap(y_rows, 1),))
     *kept, kv = project(info, (2, 3, 4, 5), chunks, w_head, kept)
     far_kv.append(onward(kv))
-    corner = call(gate_kernel, (), (), [(half, BF16), (half, BF16)], after=(*corner, kv, *d_gated[5:]), aliases={0: 0, 1: 1}, limit=4)
+    corner = call(gate_kernel, (), (), [(half, BF16), (half, BF16)], after=(*corner, kv, *d_gated[2:]), aliases={0: 0, 1: 1}, limit=4)
     *kept, kv, q = project(info, (6, 7), (corner, [swap(x, 1) for x in corner]), w_head, kept, True)
     far_kv.append(onward(kv))
     q_next = backward(q)
     normed, act, slope = kept
 
     near, kt, qt, slope_qt = call(fwd_own_kernel, info[:2], (act, slope), [(tall, F32)] + [(tall_t, BF16)] * 3)
-    attn, kv, far_kt, *sums = call(
+    attn, kv, far_kt, sums, *attn_pieces = call(
         fwd_far_kernel,
         info,
         (act, *far_kv, near, *d_gated),
-        [(tall, BF16), (wide, BF16), (tall_t, BF16)] + [((count + 8 * TILES, HD), BF16)] * HEADS,
-        [(sums_shape, F32), (tall, F32), (tall, BF16)],
-    )
-    sums = trade(sums)
+        [(tall, BF16), (wide, BF16), (tall_t, BF16), (sums_shape, F32)] + trade_outs(HD),
+        [(tall, F32), (tall, BF16)],
+    )
+    sums = call(add_kernel, (), (sums, swap(sums, 1)), [(sums_shape, F32)], limit=4)[0]
+    sums = [sums] + [swap(sums, mask) for mask in (2, 4, 6)]
 
     g, u_cols = call(
         cotangent_kernel,
@@ -545,43 +563,40 @@
     )
     rows, cols = 4 * HD // groups, 3 * HD
     half_rows = rows * groups // 2
-    mine, other, *pairs, keep, send = call(
+    attn_rows = trade(attn_pieces, (d_q,))
+    *pieces, keep, send = call(
         functools.partial(keys_kernel, groups),
         (info[0], info[2]),
         (dkv, act, slope, q_next, g_next, u_cols, q_cols, d_q, normed),
-        [((count, cols), BF16), ((4 * count, cols), BF16)]
-        + [((2 * count, cols), BF16)] * 3
-        + [((half_rows, width), F32), ((half_rows, width), BF16)],
+        trade_outs(cols) + [((half_rows, width), F32), ((half_rows, width), BF16)],
         [((2 * HD, SPAN), BF16), ((4 * HD, width), BF16), (wide, F32)],
     )
-    other = swap(other, 1)
-    pairs = call(
-        merge_kernel, (), (other,), [((2 * count, cols), BF16)] * 3, after=pairs, aliases={1: 0, 2: 1, 3: 2}, limit=4
-    )
-    pairs = [swap(x, mask) for x, mask in zip(pairs, (2, 4, 6))]
+    pieces = trade(pieces)
     layer_out, d_normed = call(
         rows_kernel,
-        (info[2],),
-        (*sums, *dg_own, tokens, w_out, w_in),
+        info[2:],
+        (*attn_rows, dg_own, tokens, w_out, w_in),
         [(own, BF16), (own, F32)],
+        [(own, BF16)],
+    )
+    grad_tokens, end = call(
+        last_kernel,
+        info[2:],
+        (*pieces, d_normed, tokens, grad_out, w_in),
+        [(own, BF16), ((8, HD), F32)],
         [(own, BF16)],
     )
     mask = 1
     while mask < groups:
         send = lax.ppermute(send, "g", [(i, i ^ mask) for i in range(groups)])
         mask, half_rows = 2 * mask, half_rows // 2
-        outs = [((half_rows, width), F32), ((half_rows, width), BF16)] if mask < groups else [((rows, width), F32)]
-        keep, *send = call(half_kernel, (), (keep, send), outs)
+        more = mask < groups
+        outs = [((half_rows, width), F32), ((half_rows, width), BF16)] if more else [((rows, width), F32)]
+        keep, *send = call(
+            functools.partial(half_kernel, 0 if more else 1), (), (keep, send), outs, after=() if more else (end,)
+        )
         send = send[0] if send else None
     grad_w_in = keep
-    grad_tokens = call(
-        last_kernel,
-        (info[2],),
-        (mine, other, *pairs, d_normed, tokens, grad_out, w_in),
-        [(own, BF16)],
-        [(own, BF16)],
-        (grad_w_in,),
-    )[0]
     parts = groups // 4
     if parts > 1:
         perm = [

time: 139 us -> 135 us (0.971)
  Pallas kernels: 44.4 us -> 41.4 us
  local copies, waits for them, and re-layouts: 4.32 us -> 1.33 us
  waiting for transfers between devices: 41.6 us -> 44.2 us
    ppermute x27 -> x25, waiting for transfers between devices: 12.2 us -> 25 us  [swap(): return lax.ppermute(x, 'h', [(i, i ^ mask) for i in range(HEADS)])]
    ppermute x2, waiting for transfers between devices: 16.5 us -> 7.16 us  [per_device(): send = lax.ppermute(send, 'g', [(i, i ^ mask) for i in range(groups)])]
    ppermute x2, waiting for transfers between devices: 9.03 us -> 5.08 us  [backward(): return lax.ppermute(x, 'g', [(i + 1, i) for i in range(groups - 1)])]
    ppermute x3, waiting for transfers between devices: 3.85 us -> 6.97 us  [onward(): return lax.ppermute(x, 'g', [(i, i + 1) for i in range(groups - 1)])]
    pallas_call x17 -> x20, Pallas kernels: 44.4 us -> 41.4 us  [call(): pl.pallas_call(kernel, out_shape=[jax.ShapeDtypeStruct(*out) for out in o...]
    unnamed x20 -> x14, local copies, waits for them, and re-layouts: 4.32 us -> 1.33 us
    ppermute x27 -> x25, starting transfers between devices: 23.9 us -> 23 us  [swap(): return lax.ppermute(x, 'h', [(i, i ^ mask) for i in range(HEADS)])]
  transfers between devices with their start and end apart: 34 -> 32, of which waited for: 15 -> 15; matrix products, arithmetic and copies ran while one was open for 0% -> 0% of each run, Pallas kernels for 23% -> 26%
where the time goes in v4:
time: 135 us; the launch traced here: 133 us
  starting transfers between devices  45.3 us (34%)
  waiting for transfers between devices  44.2 us (33%)
  Pallas kernels  41.4 us (31%)
    pallas_call x20, Pallas kernels, call(): pl.pallas_call(kernel, out_shape=[jax.ShapeDtypeStruct(*out) for out in o...  41.4 us
    ppermute x25, waiting for transfers between devices, swap(): return lax.ppermute(x, 'h', [(i, i ^ mask) for i in range(HEADS)])  25 us
    ppermute x25, starting transfers between devices, swap(): return lax.ppermute(x, 'h', [(i, i ^ mask) for i in range(HEADS)])  23 us
    ppermute x3, starting transfers between devices, onward(): return lax.ppermute(x, 'g', [(i, i + 1) for i in range(groups - 1)])  12.5 us
    ppermute x2, starting transfers between devices, per_device(): send = lax.ppermute(send, 'g', [(i, i ^ mask) for i in range(groups)])  7.24 us
    ppermute x2, waiting for transfers between devices, per_device(): send = lax.ppermute(send, 'g', [(i, i ^ mask) for i in range(groups)])  7.16 us
    ppermute x3, waiting for transfers between devices, onward(): return lax.ppermute(x, 'g', [(i, i + 1) for i in range(groups - 1)])  6.97 us
    ppermute x2, waiting for transfers between devices, backward(): return lax.ppermute(x, 'g', [(i + 1, i) for i in range(groups - 1)])  5.08 us
  transfers between devices with their start and end apart: 32, of which 15 were waited for; matrix products, arithmetic and copies ran while one was open for 0% of the time, Pallas kernels for 26%

profile of v4, /device:TPU:0, one launch (start us, length us, event | category | flops | bytes accessed | tf_op | source)
XLA Modules:
  0.0 133.2 jit_solution(14605614354931487573)
XLA Ops:
  1.2 2.6 %collective-permute-start.1 = (bf16[256,1024]{1,0:T(8,128)(2,1)}, bf16[256,1024]{1,0:T(8,128)(2,1)S(1)}, u32[]{:S(2)}, u32[]{:S(2)}) collective-permute-start(bf16[256,1024]{1,0:T(8,128)(2,1)} %refs_6_.3), channel_id=1, source_target_pairs={{0,4},{1,5},{2,6},{3,7},{4,0},{5,1},{6,2},{7,3},{8,12},{9,13},{10,... | collective-permute-start | bytes 1572872 | tf_op jit(solution)/shard_map/ppermute | solution.py:476
  3.8 1.5 %collective-permute-start = (bf16[256,1024]{1,0:T(8,128)(2,1)}, bf16[256,1024]{1,0:T(8,128)(2,1)S(1)}, u32[]{:S(2)}, u32[]{:S(2)}) collective-permute-start(bf16[256,1024]{1,0:T(8,128)(2,1)} %refs_6_.3), channel_id=1, source_target_pairs={{0,2},{1,3},{2,0},{3,1},{4,6},{5,7},{6,4},{7,5},{8,10},{9,11},{10,... | collective-permute-start | bytes 1572872 | tf_op jit(solution)/shard_map/ppermute | solution.py:476
  6.6 2.4 %shard_map.85 = (s32[32]{0:T(128)S(1)}, s32[32]{0:T(128)S(1)}, s32[2]{0:T(128)S(1)}, bf16[1024,512]{1,0:T(8,128)(2,1)S(1)}) custom-call(s32[16]{0:T(128)S(1)} %copy-done.3, s32[16]{0:T(128)S(1)} %copy-done.4, bf16[1024,4096]{1,0:T(8,128)(2,1)} %refs_8_.3), custom_call_target="tpu_custom_call" | custom-call | tf_op jit(solution)/shard_map/pallas_call | solution.py:458
  9.0 1.7 %shard_map.86 = (bf16[2048,1024]{1,0:T(8,128)(2,1)S(1)}, bf16[2048,512]{1,0:T(8,128)(2,1)S(1)}, bf16[2048,512]{1,0:T(8,128)(2,1)S(1)}, bf16[512,256]{1,0:T(8,128)(2,1)S(1)}) custom-call(s32[2]{0:T(128)S(1)} %get-tuple-element.72.at_ref, bf16[256,1024]{1,0:T(8,128)(2,1)S(1)} %copy-done.1, bf16[256,1024]{1,0:T(8,128)(2,1)S(1)} %collective-permute-done.2.refs_1_, ...), custom_call_target="tpu_custom_call" | custom-call | tf_op jit(solution)/shard_map/pallas_call | solution.py:458
  12.2 3.5 %collective-permute-start.3 = (bf16[512,256]{1,0:T(8,128)(2,1)S(1)}, bf16[512,256]{1,0:T(8,128)(2,1)S(1)}, u32[]{:S(2)}, u32[]{:S(2)}) collective-permute-start(bf16[512,256]{1,0:T(8,128)(2,1)S(1)} %get-tuple-element.76.refs_0_), channel_id=1, source_target_pairs={{0,8},{8,16},{16,24},{1,9},{9,17},{17,25},{2,10},{10,18},{18,26},{... | collective-permute-start | bytes 786440 | tf_op jit(solution)/shard_map/ppermute | solution.py:479
  16.5 1.5 %collective-permute-done.x_ref = bf16[256,1024]{1,0:T(8,128)(2,1)S(1)} collective-permute-done((bf16[256,1024]{1,0:T(8,128)(2,1)}, bf16[256,1024]{1,0:T(8,128)(2,1)S(1)}, u32[]{:S(2)}, u32[]{:S(2)}) %collective-permute-start) | collective-permute-done | bytes 524320 | tf_op jit(solution)/shard_map/ppermute | solution.py:476
  18.0 3.9 %collective-permute-done.3.refs_0_.kva_ref = bf16[512,256]{1,0:T(8,128)(2,1)S(1)} collective-permute-done((bf16[512,256]{1,0:T(8,128)(2,1)S(1)}, bf16[512,256]{1,0:T(8,128)(2,1)S(1)}, u32[]{:S(2)}, u32[]{:S(2)}) %collective-permute-start.3) | collective-permute-done | bytes 262176 | tf_op jit(solution)/shard_map/ppermute | solution.py:479
  23.5 1.5 %collective-permute-start.10 = (bf16[512,128]{1,0:T(8,128)(2,1)S(1)}, bf16[512,128]{1,0:T(8,128)(2,1)S(1)}, u32[]{:S(2)}, u32[]{:S(2)}) collective-permute-start(bf16[512,128]{1,0:T(8,128)(2,1)S(1)} %get-tuple-element.90), channel_id=1, source_target_pairs={{0,4},{1,5},{2,6},{3,7},{4,0},{5,1},{6,2},{7,3},{8,12},{9,13},{10,... | collective-permute-start | bytes 393224 | tf_op jit(solution)/shard_map/ppermute | solution.py:476
  27.0 2.6 %shard_map.90 = (bf16[2048,1024]{1,0:T(8,128)(2,1)S(1)}, bf16[2048,512]{1,0:T(8,128)(2,1)S(1)}, bf16[2048,512]{1,0:T(8,128)(2,1)S(1)}, bf16[1024,256]{1,0:T(8,128)(2,1)S(1)}) custom-call(s32[2]{0:T(128)S(1)} %get-tuple-element.72.at_ref, bf16[256,1024]{1,0:T(8,128)(2,1)S(1)} %get-tuple-element.84.refs_0_, ...), custom_call_target="tpu_custom_call", output_to_operand_aliasing={{0}: (6, {}), {1}: (7, {}), {2}: (8, {})} | custom-call | tf_op jit(solution)/shard_map/pallas_call | solution.py:458
  29.6 6.8 %collective-permute-done.10.refs_4_.refs_3_.refs_7_ = bf16[512,128]{1,0:T(8,128)(2,1)S(1)} collective-permute-done((bf16[512,128]{1,0:T(8,128)(2,1)S(1)}, bf16[512,128]{1,0:T(8,128)(2,1)S(1)}, u32[]{:S(2)}, u32[]{:S(2)}) %collective-permute-start.10) | collective-permute-done | bytes 131104 | tf_op jit(solution)/shard_map/ppermute | solution.py:476
  37.2 4.4 %collective-permute-start.14 = (bf16[1024,256]{1,0:T(8,128)(2,1)S(1)}, bf16[1024,256]{1,0:T(8,128)(2,1)S(1)}, u32[]{:S(2)}, u32[]{:S(2)}) collective-permute-start(bf16[1024,256]{1,0:T(8,128)(2,1)S(1)} %get-tuple-element.89.refs_2_), channel_id=1, source_target_pairs={{0,8},{8,16},{16,24},{1,9},{9,17},{17,25},{2,10},{10,18},{18,26},{... | collective-permute-start | bytes 1572872 | tf_op jit(solution)/shard_map/ppermute | solution.py:479
  41.6 1.8 %shard_map.92 = (bf16[2048,1024]{1,0:T(8,128)(2,1)S(1)}, bf16[2048,512]{1,0:T(8,128)(2,1)S(1)}, bf16[2048,512]{1,0:T(8,128)(2,1)S(1)}, bf16[512,256]{1,0:T(8,128)(2,1)S(1)}, bf16[2048,128]{1,0:T(8,128)(2,1)S(1)}) custom-call(s32[2]{0:T(128)S(1)} %get-tuple-element.72.at_ref, ...), custom_call_target="tpu_custom_call", output_to_operand_aliasing={{0}: (6, {}), {1}: (7, {}), {2}: (8, {})} | custom-call | tf_op jit(solution)/shard_map/pallas_call | solution.py:458
  44.7 4.6 %collective-permute-start.15 = (bf16[512,256]{1,0:T(8,128)(2,1)S(1)}, bf16[512,256]{1,0:T(8,128)(2,1)S(1)}, u32[]{:S(2)}, u32[]{:S(2)}) collective-permute-start(bf16[512,256]{1,0:T(8,128)(2,1)S(1)} %get-tuple-element.98), channel_id=1, source_target_pairs={{0,8},{8,16},{16,24},{1,9},{9,17},{17,25},{2,10},{10,18},{18,26},{... | collective-permute-start | bytes 786440 | tf_op jit(solution)/shard_map/ppermute | solution.py:479
  49.3 6.3 %shard_map.93 = (f32[2048,128]{1,0:T(8,128)S(1)}, bf16[128,2048]{1,0:T(8,128)(2,1)S(1)}, bf16[128,2048]{1,0:T(8,128)(2,1)S(1)}, bf16[128,2048]{1,0:T(8,128)(2,1)S(1)}) custom-call(s32[32]{0:T(128)S(1)} %get-tuple-element.73.lo_ref, s32[32]{0:T(128)S(1)} %get-tuple-element.74.nv_ref, bf16[2048,512]{1,0:T(8,128)(2,1)S(1)} %get-tuple-element.97.act_ref, ...), custom_call_target="tpu_custom_call" | custom-call | tf_op jit(solution)/shard_map/pallas_call | solution.py:458
  55.6 3.0 %collective-permute-done.15.kvc_ref = bf16[512,256]{1,0:T(8,128)(2,1)S(1)} collective-permute-done((bf16[512,256]{1,0:T(8,128)(2,1)S(1)}, bf16[512,256]{1,0:T(8,128)(2,1)S(1)}, u32[]{:S(2)}, u32[]{:S(2)}) %collective-permute-start.15) | collective-permute-done | bytes 262176 | tf_op jit(solution)/shard_map/ppermute | solution.py:479
  61.0 1.5 %collective-permute-start.20 = (f32[16,256]{1,0:T(8,128)S(1)}, f32[16,256]{1,0:T(8,128)S(1)}, u32[]{:S(2)}, u32[]{:S(2)}) collective-permute-start(f32[16,256]{1,0:T(8,128)S(1)} %shard_map.95.refs_0_), channel_id=1, source_target_pairs={{0,6},{1,7},{2,4},{3,5},{4,2},{5,3},{6,0},{7,1},{8,14},{9,15},{10,... | collective-permute-start | bytes 49160 | tf_op jit(solution)/shard_map/ppermute | solution.py:476
  63.0 1.5 %collective-permute-start.18 = (f32[16,256]{1,0:T(8,128)S(1)}, f32[16,256]{1,0:T(8,128)S(1)}, u32[]{:S(2)}, u32[]{:S(2)}) collective-permute-start(f32[16,256]{1,0:T(8,128)S(1)} %shard_map.95.refs_0_), channel_id=1, source_target_pairs={{0,2},{1,3},{2,0},{3,1},{4,6},{5,7},{6,4},{7,5},{8,10},{9,11},{10,... | collective-permute-start | bytes 49160 | tf_op jit(solution)/shard_map/ppermute | solution.py:476
  66.7 1.8 %shard_map.96 = (bf16[2048,128]{1,0:T(8,128)(2,1)S(1)}, bf16[128,2048]{1,0:T(8,128)(2,1)S(1)}) custom-call(s32[32]{0:T(128)S(1)} %get-tuple-element.74.nv_ref, s32[2]{0:T(128)S(1)} %get-tuple-element.72.at_ref, bf16[2048,512]{1,0:T(8,128)(2,1)S(1)} %get-tuple-element.97.act_ref, bf16[2048,512]{1,0:T(8,128)(2,1)S(1)} %get-tuple-element.99.slope_ref, ...), custom_call_target="tpu_custom_call" | custom-call | tf_op jit(solution)/shard_map/pallas_call | solution.py:458
  69.9 9.4 %shard_map.97 = (bf16[128,2048]{1,0:T(8,128)(2,1)S(1)}, bf16[2048,128]{1,0:T(8,128)(2,1)S(1)}, f32[2048,256]{1,0:T(8,128)S(1)}) custom-call(s32[32]{0:T(128)S(1)} %get-tuple-element.73.lo_ref, bf16[2048,512]{1,0:T(8,128)(2,1)S(1)} %get-tuple-element.97.act_ref, bf16[128,2048]{1,0:T(8,128)(2,1)S(1)} %get-tuple-element.107.slope_qt_ref, ...), custom_call_target="tpu_custom_call" | custom-call | tf_op jit(solution)/shard_map/pallas_call | solution.py:458
  79.2 5.1 %collective-permute-done.25.g_ref = bf16[2048,128]{1,0:T(8,128)(2,1)S(1)} collective-permute-done((bf16[2048,128]{1,0:T(8,128)(2,1)S(1)}, bf16[2048,128]{1,0:T(8,128)(2,1)S(1)}, u32[]{:S(2)}, u32[]{:S(2)}) %collective-permute-start.25) | collective-permute-done | bytes 524320 | tf_op jit(solution)/shard_map/ppermute | solution.py:482
  84.3 4.5 %shard_map.100 = (bf16[256,384]{1,0:T(8,128)(2,1)S(1)}, bf16[1024,384]{1,0:T(8,128)(2,1)S(1)}, bf16[512,384]{1,0:T(8,128)(2,1)S(1)}, bf16[512,384]{1,0:T(8,128)(...) custom-call(s32[32]{0:T(128)S(1)} %get-tuple-element.73.lo_ref, ...), custom_call_target="tpu_custom_call" | custom-call | tf_op jit(solution)/shard_map/pallas_call | solution.py:458
  88.9 2.0 %collective-permute-start.30 = (bf16[256,1024]{1,0:T(8,128)(2,1)S(1)}, bf16[256,1024]{1,0:T(8,128)(2,1)S(1)}, u32[]{:S(2)}, u32[]{:S(2)}) collective-permute-start(bf16[256,1024]{1,0:T(8,128)(2,1)S(1)} %get-tuple-element.137), channel_id=1, source_target_pairs={{0,8},{8,0},{16,24},{24,16},{1,9},{9,1},{17,25},{25,17},{2,10},{10... | collective-permute-start | bytes 1572872 | tf_op jit(solution)/shard_map/ppermute | solution.py:591
  92.7 1.5 %collective-permute-start.28 = (bf16[512,384]{1,0:T(8,128)(2,1)S(1)}, bf16[512,384]{1,0:T(8,128)(2,1)S(1)}, u32[]{:S(2)}, u32[]{:S(2)}) collective-permute-start(bf16[512,384]{1,0:T(8,128)(2,1)S(1)} %get-tuple-element.132), channel_id=1, source_target_pairs={{0,4},{1,5},{2,6},{3,7},{4,0},{5,1},{6,2},{7,3},{8,12},{9,13},{10,... | collective-permute-start | bytes 1179656 | tf_op jit(solution)/shard_map/ppermute | solution.py:476
  94.8 1.4 %collective-permute-start.22 = (bf16[512,128]{1,0:T(8,128)(2,1)S(1)}, bf16[512,128]{1,0:T(8,128)(2,1)S(1)}, u32[]{:S(2)}, u32[]{:S(2)}) collective-permute-start(bf16[512,128]{1,0:T(8,128)(2,1)S(1)} %get-tuple-element.117), channel_id=1, source_target_pairs={{0,2},{1,3},{2,0},{3,1},{4,6},{5,7},{6,4},{7,5},{8,10},{9,11},{10,... | collective-permute-start | bytes 393224 | tf_op jit(solution)/shard_map/ppermute | solution.py:476
  96.3 7.2 %collective-permute-done.30.got_ref = bf16[256,1024]{1,0:T(8,128)(2,1)S(1)} collective-permute-done((bf16[256,1024]{1,0:T(8,128)(2,1)S(1)}, bf16[256,1024]{1,0:T(8,128)(2,1)S(1)}, u32[]{:S(2)}, u32[]{:S(2)}) %collective-permute-start.30) | collective-permute-done | bytes 524320 | tf_op jit(solution)/shard_map/ppermute | solution.py:591
  103.4 1.5 %collective-permute-start.23 = (bf16[512,128]{1,0:T(8,128)(2,1)S(1)}, bf16[512,128]{1,0:T(8,128)(2,1)S(1)}, u32[]{:S(2)}, u32[]{:S(2)}) collective-permute-start(bf16[512,128]{1,0:T(8,128)(2,1)S(1)} %get-tuple-element.118), channel_id=1, source_target_pairs={{0,4},{1,5},{2,6},{3,7},{4,0},{5,1},{6,2},{7,3},{8,12},{9,13},{10,... | collective-permute-start | bytes 393224 | tf_op jit(solution)/shard_map/ppermute | solution.py:476
  105.1 8.8 %collective-permute-done.22.refs_2_ = bf16[512,128]{1,0:T(8,128)(2,1)S(1)} collective-permute-done((bf16[512,128]{1,0:T(8,128)(2,1)S(1)}, bf16[512,128]{1,0:T(8,128)(2,1)S(1)}, u32[]{:S(2)}, u32[]{:S(2)}) %collective-permute-start.22) | collective-permute-done | bytes 131104 | tf_op jit(solution)/shard_map/ppermute | solution.py:476
  113.9 5.3 %collective-permute-start.31 = (bf16[128,1024]{1,0:T(8,128)(2,1)S(1)}, bf16[128,1024]{1,0:T(8,128)(2,1)S(1)}, u32[]{:S(2)}, u32[]{:S(2)}) collective-permute-start(bf16[128,1024]{1,0:T(8,128)(2,1)S(1)} %get-tuple-element.139), channel_id=1, source_target_pairs={{0,16},{8,24},{16,0},{24,8},{1,17},{9,25},{17,1},{25,9},{2,18},{10... | collective-permute-start | bytes 786440 | tf_op jit(solution)/shard_map/ppermute | solution.py:591
  119.1 2.4 %collective-permute-start.24 = (bf16[512,128]{1,0:T(8,128)(2,1)S(1)}, bf16[512,128]{1,0:T(8,128)(2,1)S(1)}, u32[]{:S(2)}, u32[]{:S(2)}) collective-permute-start(bf16[512,128]{1,0:T(8,128)(2,1)S(1)} %get-tuple-element.119), channel_id=1, source_target_pairs={{0,6},{1,7},{2,4},{3,5},{4,2},{5,3},{6,0},{7,1},{8,14},{9,15},{10,... | collective-permute-start | bytes 393224 | tf_op jit(solution)/shard_map/ppermute | solution.py:476
  121.5 3.5 %collective-permute-done.24.refs_4_ = bf16[512,128]{1,0:T(8,128)(2,1)S(1)} collective-permute-done((bf16[512,128]{1,0:T(8,128)(2,1)S(1)}, bf16[512,128]{1,0:T(8,128)(2,1)S(1)}, u32[]{:S(2)}, u32[]{:S(2)}) %collective-permute-start.24) | collective-permute-done | bytes 131104 | tf_op jit(solution)/shard_map/ppermute | solution.py:476
  125.0 3.6 %shard_map.99 = (bf16[256,1024]{1,0:T(8,128)(2,1)}, f32[256,1024]{1,0:T(8,128)S(1)}) custom-call(s32[2]{0:T(128)S(1)} %get-tuple-element.72.at_ref, bf16[256,128]{1,0:T(8,128)(2,1)S(1)} %get-tuple-element.102.refs_0_, bf16[1024,128]{1,0:T(8,128)(2,1)S(1)} %collective-permute-done.16.other_ref.refs_1_, bf16[512,128]{1,0:T(8,128)(2,1)S(1)} %collective-permute-done.22.refs_2_, ...), custom_call_target="tpu_custom_call" | custom-call | tf_op jit(solution)/shard_map/pallas_call | solution.py:458
  128.6 3.7 %shard_map.102 = (bf16[256,1024]{1,0:T(8,128)(2,1)}, f32[8,128]{1,0:T(8,128)S(1)}) custom-call(s32[2]{0:T(128)S(1)} %get-tuple-element.72.at_ref, bf16[256,384]{1,0:T(8,128)(2,1)S(1)} %get-tuple-element.126.refs_0_, bf16[1024,384]{1,0:T(8,128)(2,1)S(1)} %collective-permute-done.26.other_ref.refs_1_, bf16[512,384]{1,0:T(8,128)(2,1)S(1)} %collective-permute-done.27.refs_2_, ...), custom_call_target="tpu_custom_call" | custom-call | tf_op jit(solution)/shard_map/pallas_call | solution.py:458
  (67 shorter events, 19.7 us)
Async XLA Ops:
  0.6 8.3 %collective-permute-start.2 = (bf16[256,1024]{1,0:T(8,128)(2,1)}, bf16[256,1024]{1,0:T(8,128)(2,1)S(1)}, u32[]{:S(2)}, u32[]{:S(2)}) collective-permute-start(bf16[256,1024]{1,0:T(8,128)(2,1)} %refs_6_.3), channel_id=1, source_target_pairs={{0,1},{1,0},{2,3},{3,2},{4,5},{5,4},{6,7},{7,6},{8,9},{9,8},{10,11... | collective-permute-start | bytes 1572872 | tf_op jit(solution)/shard_map/ppermute | solution.py:476
  1.2 15.3 %collective-permute-start.1 = (bf16[256,1024]{1,0:T(8,128)(2,1)}, bf16[256,1024]{1,0:T(8,128)(2,1)S(1)}, u32[]{:S(2)}, u32[]{:S(2)}) collective-permute-start(bf16[256,1024]{1,0:T(8,128)(2,1)} %refs_6_.3), channel_id=1, source_target_pairs={{0,4},{1,5},{2,6},{3,7},{4,0},{5,1},{6,2},{7,3},{8,12},{9,13},{10,... | collective-permute-start | bytes 1572872 | tf_op jit(solution)/shard_map/ppermute | solution.py:476
  3.8 14.2 %collective-permute-start = (bf16[256,1024]{1,0:T(8,128)(2,1)}, bf16[256,1024]{1,0:T(8,128)(2,1)S(1)}, u32[]{:S(2)}, u32[]{:S(2)}) collective-permute-start(bf16[256,1024]{1,0:T(8,128)(2,1)} %refs_6_.3), channel_id=1, source_target_pairs={{0,2},{1,3},{2,0},{3,1},{4,6},{5,7},{6,4},{7,5},{8,10},{9,11},{10,... | collective-permute-start | bytes 1572872 | tf_op jit(solution)/shard_map/ppermute | solution.py:476
  12.1 3.6 %collective-permute-start.4 = (bf16[1024,128]{1,0:T(8,128)(2,1)S(1)}, bf16[1024,128]{1,0:T(8,128)(2,1)S(1)}, u32[]{:S(2)}, u32[]{:S(2)}) collective-permute-start(bf16[1024,128]{1,0:T(8,128)(2,1)S(1)} %get-tuple-element.77), channel_id=1, source_target_pairs={{0,1},{1,0},{2,3},{3,2},{4,5},{5,4},{6,7},{7,6},{8,9},{9,8},{10,11... | collective-permute-start | bytes 786440 | tf_op jit(solution)/shard_map/ppermute | solution.py:476
  12.2 9.7 %collective-permute-start.3 = (bf16[512,256]{1,0:T(8,128)(2,1)S(1)}, bf16[512,256]{1,0:T(8,128)(2,1)S(1)}, u32[]{:S(2)}, u32[]{:S(2)}) collective-permute-start(bf16[512,256]{1,0:T(8,128)(2,1)S(1)} %get-tuple-element.76.refs_0_), channel_id=1, source_target_pairs={{0,8},{8,16},{16,24},{1,9},{9,17},{17,25},{2,10},{10,18},{18,26},{... | collective-permute-start | bytes 786440 | tf_op jit(solution)/shard_map/ppermute | solution.py:479
  21.9 3.2 %collective-permute-start.7 = (bf16[256,1024]{1,0:T(8,128)(2,1)S(1)}, bf16[256,1024]{1,0:T(8,128)(2,1)S(1)}, u32[]{:S(2)}, u32[]{:S(2)}) collective-permute-start(bf16[256,1024]{1,0:T(8,128)(2,1)S(1)} %get-tuple-element.84.refs_0_), channel_id=1, source_target_pairs={{0,1},{1,0},{2,3},{3,2},{4,5},{5,4},{6,7},{7,6},{8,9},{9,8},{10,11... | collective-permute-start | bytes 1572872 | tf_op jit(solution)/shard_map/ppermute | solution.py:476
  22.0 4.5 %collective-permute-start.8 = (bf16[256,1024]{1,0:T(8,128)(2,1)S(1)}, bf16[256,1024]{1,0:T(8,128)(2,1)S(1)}, u32[]{:S(2)}, u32[]{:S(2)}) collective-permute-start(bf16[256,1024]{1,0:T(8,128)(2,1)S(1)} %get-tuple-element.85.refs_2_), channel_id=1, source_target_pairs={{0,1},{1,0},{2,3},{3,2},{4,5},{5,4},{6,7},{7,6},{8,9},{9,8},{10,11... | collective-permute-start | bytes 1572872 | tf_op jit(solution)/shard_map/ppermute | solution.py:476
  22.5 14.1 %collective-permute-start.5 = (bf16[128,1024]{1,0:T(8,128)(2,1)S(1)}, bf16[128,1024]{1,0:T(8,128)(2,1)S(1)}, u32[]{:S(2)}, u32[]{:S(2)}) collective-permute-start(bf16[128,1024]{1,0:T(8,128)(2,1)S(1)} %get-tuple-element.82), channel_id=1, source_target_pairs={{0,4},{1,5},{2,6},{3,7},{4,0},{5,1},{6,2},{7,3},{8,12},{9,13},{10,... | collective-permute-start | bytes 786440 | tf_op jit(solution)/shard_map/ppermute | solution.py:476
  23.0 13.6 %collective-permute-start.6 = (bf16[128,1024]{1,0:T(8,128)(2,1)S(1)}, bf16[128,1024]{1,0:T(8,128)(2,1)S(1)}, u32[]{:S(2)}, u32[]{:S(2)}) collective-permute-start(bf16[128,1024]{1,0:T(8,128)(2,1)S(1)} %get-tuple-element.83), channel_id=1, source_target_pairs={{0,2},{1,3},{2,0},{3,1},{4,6},{5,7},{6,4},{7,5},{8,10},{9,11},{10,... | collective-permute-start | bytes 786440 | tf_op jit(solution)/shard_map/ppermute | solution.py:476
  23.5 12.9 %collective-permute-start.10 = (bf16[512,128]{1,0:T(8,128)(2,1)S(1)}, bf16[512,128]{1,0:T(8,128)(2,1)S(1)}, u32[]{:S(2)}, u32[]{:S(2)}) collective-permute-start(bf16[512,128]{1,0:T(8,128)(2,1)S(1)} %get-tuple-element.90), channel_id=1, source_target_pairs={{0,4},{1,5},{2,6},{3,7},{4,0},{5,1},{6,2},{7,3},{8,12},{9,13},{10,... | collective-permute-start | bytes 393224 | tf_op jit(solution)/shard_map/ppermute | solution.py:476
  25.1 11.3 %collective-permute-start.11 = (bf16[512,128]{1,0:T(8,128)(2,1)S(1)}, bf16[512,128]{1,0:T(8,128)(2,1)S(1)}, u32[]{:S(2)}, u32[]{:S(2)}) collective-permute-start(bf16[512,128]{1,0:T(8,128)(2,1)S(1)} %get-tuple-element.91), channel_id=1, source_target_pairs={{0,6},{1,7},{2,4},{3,5},{4,2},{5,3},{6,0},{7,1},{8,14},{9,15},{10,... | collective-permute-start | bytes 393224 | tf_op jit(solution)/shard_map/ppermute | solution.py:476
  26.5 10.1 %collective-permute-start.9 = (bf16[512,128]{1,0:T(8,128)(2,1)S(1)}, bf16[512,128]{1,0:T(8,128)(2,1)S(1)}, u32[]{:S(2)}, u32[]{:S(2)}) collective-permute-start(bf16[512,128]{1,0:T(8,128)(2,1)S(1)} %get-tuple-element.81.refs_1_), channel_id=1, source_target_pairs={{0,2},{1,3},{2,0},{3,1},{4,6},{5,7},{6,4},{7,5},{8,10},{9,11},{10,... | collective-permute-start | bytes 393224 | tf_op jit(solution)/shard_map/ppermute | solution.py:476
  36.6 5.0 %collective-permute-start.12 = (bf16[128,1024]{1,0:T(8,128)(2,1)S(1)}, bf16[128,1024]{1,0:T(8,128)(2,1)S(1)}, u32[]{:S(2)}, u32[]{:S(2)}) collective-permute-start(bf16[128,1024]{1,0:T(8,128)(2,1)S(1)} %get-tuple-element.92.refs_0_), channel_id=1, source_target_pairs={{0,1},{1,0},{2,3},{3,2},{4,5},{5,4},{6,7},{7,6},{8,9},{9,8},{10,11... | collective-permute-start | bytes 786440 | tf_op jit(solution)/shard_map/ppermute | solution.py:476
  36.7 4.9 %collective-permute-start.13 = (bf16[128,1024]{1,0:T(8,128)(2,1)S(1)}, bf16[128,1024]{1,0:T(8,128)(2,1)S(1)}, u32[]{:S(2)}, u32[]{:S(2)}) collective-permute-start(bf16[128,1024]{1,0:T(8,128)(2,1)S(1)} %get-tuple-element.93.refs_1_), channel_id=1, source_target_pairs={{0,1},{1,0},{2,3},{3,2},{4,5},{5,4},{6,7},{7,6},{8,9},{9,8},{10,11... | collective-permute-start | bytes 786440 | tf_op jit(solution)/shard_map/ppermute | solution.py:476
  37.2 21.4 %collective-permute-start.14 = (bf16[1024,256]{1,0:T(8,128)(2,1)S(1)}, bf16[1024,256]{1,0:T(8,128)(2,1)S(1)}, u32[]{:S(2)}, u32[]{:S(2)}) collective-permute-start(bf16[1024,256]{1,0:T(8,128)(2,1)S(1)} %get-tuple-element.89.refs_2_), channel_id=1, source_target_pairs={{0,8},{8,16},{16,24},{1,9},{9,17},{17,25},{2,10},{10,18},{18,26},{... | collective-permute-start | bytes 1572872 | tf_op jit(solution)/shard_map/ppermute | solution.py:479
  43.4 23.3 %collective-permute-start.21 = (bf16[2048,128]{1,0:T(8,128)(2,1)S(1)}, bf16[2048,128]{1,0:T(8,128)(2,1)S(1)}, u32[]{:S(2)}, u32[]{:S(2)}) collective-permute-start(bf16[2048,128]{1,0:T(8,128)(2,1)S(1)} %get-tuple-element.112), channel_id=1, source_target_pairs={{8,0},{16,8},{24,16},{9,1},{17,9},{25,17},{10,2},{18,10},{26,18},{... | collective-permute-start | bytes 1572872 | tf_op jit(solution)/shard_map/ppermute | solution.py:482
  44.7 13.9 %collective-permute-start.15 = (bf16[512,256]{1,0:T(8,128)(2,1)S(1)}, bf16[512,256]{1,0:T(8,128)(2,1)S(1)}, u32[]{:S(2)}, u32[]{:S(2)}) collective-permute-start(bf16[512,256]{1,0:T(8,128)(2,1)S(1)} %get-tuple-element.98), channel_id=1, source_target_pairs={{0,8},{8,16},{16,24},{1,9},{9,17},{17,25},{2,10},{10,18},{18,26},{... | collective-permute-start | bytes 786440 | tf_op jit(solution)/shard_map/ppermute | solution.py:479
  59.8 1.2 collective-permute-start.17
  61.0 4.6 %collective-permute-start.20 = (f32[16,256]{1,0:T(8,128)S(1)}, f32[16,256]{1,0:T(8,128)S(1)}, u32[]{:S(2)}, u32[]{:S(2)}) collective-permute-start(f32[16,256]{1,0:T(8,128)S(1)} %shard_map.95.refs_0_), channel_id=1, source_target_pairs={{0,6},{1,7},{2,4},{3,5},{4,2},{5,3},{6,0},{7,1},{8,14},{9,15},{10,... | collective-permute-start | bytes 49160 | tf_op jit(solution)/shard_map/ppermute | solution.py:476
  62.5 3.7 %collective-permute-start.19 = (f32[16,256]{1,0:T(8,128)S(1)}, f32[16,256]{1,0:T(8,128)S(1)}, u32[]{:S(2)}, u32[]{:S(2)}) collective-permute-start(f32[16,256]{1,0:T(8,128)S(1)} %shard_map.95.refs_0_), channel_id=1, source_target_pairs={{0,4},{1,5},{2,6},{3,7},{4,0},{5,1},{6,2},{7,3},{8,12},{9,13},{10,... | collective-permute-start | bytes 49160 | tf_op jit(solution)/shard_map/ppermute | solution.py:476
  63.0 3.7 %collective-permute-start.18 = (f32[16,256]{1,0:T(8,128)S(1)}, f32[16,256]{1,0:T(8,128)S(1)}, u32[]{:S(2)}, u32[]{:S(2)}) collective-permute-start(f32[16,256]{1,0:T(8,128)S(1)} %shard_map.95.refs_0_), channel_id=1, source_target_pairs={{0,2},{1,3},{2,0},{3,1},{4,6},{5,7},{6,4},{7,5},{8,10},{9,11},{10,... | collective-permute-start | bytes 49160 | tf_op jit(solution)/shard_map/ppermute | solution.py:476
  68.6 15.8 %collective-permute-start.25 = (bf16[2048,128]{1,0:T(8,128)(2,1)S(1)}, bf16[2048,128]{1,0:T(8,128)(2,1)S(1)}, u32[]{:S(2)}, u32[]{:S(2)}) collective-permute-start(bf16[2048,128]{1,0:T(8,128)(2,1)S(1)} %get-tuple-element.113.g_ref), channel_id=1, source_target_pairs={{8,0},{16,8},{24,16},{9,1},{17,9},{25,17},{10,2},{18,10},{26,18},{... | collective-permute-start | bytes 1572872 | tf_op jit(solution)/shard_map/ppermute | solution.py:482
  88.9 2.4 %collective-permute-start.26 = (bf16[1024,384]{1,0:T(8,128)(2,1)S(1)}, bf16[1024,384]{1,0:T(8,128)(2,1)S(1)}, u32[]{:S(2)}, u32[]{:S(2)}) collective-permute-start(bf16[1024,384]{1,0:T(8,128)(2,1)S(1)} %get-tuple-element.127), channel_id=1, source_target_pairs={{0,1},{1,0},{2,3},{3,2},{4,5},{5,4},{6,7},{7,6},{8,9},{9,8},{10,11... | collective-permute-start | bytes 2359304 | tf_op jit(solution)/shard_map/ppermute | solution.py:476
  88.9 14.5 %collective-permute-start.30 = (bf16[256,1024]{1,0:T(8,128)(2,1)S(1)}, bf16[256,1024]{1,0:T(8,128)(2,1)S(1)}, u32[]{:S(2)}, u32[]{:S(2)}) collective-permute-start(bf16[256,1024]{1,0:T(8,128)(2,1)S(1)} %get-tuple-element.137), channel_id=1, source_target_pairs={{0,8},{8,0},{16,24},{24,16},{1,9},{9,1},{17,25},{25,17},{2,10},{10... | collective-permute-start | bytes 1572872 | tf_op jit(solution)/shard_map/ppermute | solution.py:591
  90.9 3.9 %collective-permute-start.16 = (bf16[1024,128]{1,0:T(8,128)(2,1)S(1)}, bf16[1024,128]{1,0:T(8,128)(2,1)S(1)}, u32[]{:S(2)}, u32[]{:S(2)}) collective-permute-start(bf16[1024,128]{1,0:T(8,128)(2,1)S(1)} %get-tuple-element.103), channel_id=1, source_target_pairs={{0,1},{1,0},{2,3},{3,2},{4,5},{5,4},{6,7},{7,6},{8,9},{9,8},{10,11... | collective-permute-start | bytes 786440 | tf_op jit(solution)/shard_map/ppermute | solution.py:476
  91.3 37.3 %collective-permute-start.27 = (bf16[512,384]{1,0:T(8,128)(2,1)S(1)}, bf16[512,384]{1,0:T(8,128)(2,1)S(1)}, u32[]{:S(2)}, u32[]{:S(2)}) collective-permute-start(bf16[512,384]{1,0:T(8,128)(2,1)S(1)} %get-tuple-element.131), channel_id=1, source_target_pairs={{0,2},{1,3},{2,0},{3,1},{4,6},{5,7},{6,4},{7,5},{8,10},{9,11},{10,... | collective-permute-start | bytes 1179656 | tf_op jit(solution)/shard_map/ppermute | solution.py:476
  92.7 35.9 %collective-permute-start.28 = (bf16[512,384]{1,0:T(8,128)(2,1)S(1)}, bf16[512,384]{1,0:T(8,128)(2,1)S(1)}, u32[]{:S(2)}, u32[]{:S(2)}) collective-permute-start(bf16[512,384]{1,0:T(8,128)(2,1)S(1)} %get-tuple-element.132), channel_id=1, source_target_pairs={{0,4},{1,5},{2,6},{3,7},{4,0},{5,1},{6,2},{7,3},{8,12},{9,13},{10,... | collective-permute-start | bytes 1179656 | tf_op jit(solution)/shard_map/ppermute | solution.py:476
  94.2 34.4 %collective-permute-start.29 = (bf16[512,384]{1,0:T(8,128)(2,1)S(1)}, bf16[512,384]{1,0:T(8,128)(2,1)S(1)}, u32[]{:S(2)}, u32[]{:S(2)}) collective-permute-start(bf16[512,384]{1,0:T(8,128)(2,1)S(1)} %get-tuple-element.133), channel_id=1, source_target_pairs={{0,6},{1,7},{2,4},{3,5},{4,2},{5,3},{6,0},{7,1},{8,14},{9,15},{10,... | collective-permute-start | bytes 1179656 | tf_op jit(solution)/shard_map/ppermute | solution.py:476
  94.8 19.0 %collective-permute-start.22 = (bf16[512,128]{1,0:T(8,128)(2,1)S(1)}, bf16[512,128]{1,0:T(8,128)(2,1)S(1)}, u32[]{:S(2)}, u32[]{:S(2)}) collective-permute-start(bf16[512,128]{1,0:T(8,128)(2,1)S(1)} %get-tuple-element.117), channel_id=1, source_target_pairs={{0,2},{1,3},{2,0},{3,1},{4,6},{5,7},{6,4},{7,5},{8,10},{9,11},{10,... | collective-permute-start | bytes 393224 | tf_op jit(solution)/shard_map/ppermute | solution.py:476
  103.4 15.7 %collective-permute-start.23 = (bf16[512,128]{1,0:T(8,128)(2,1)S(1)}, bf16[512,128]{1,0:T(8,128)(2,1)S(1)}, u32[]{:S(2)}, u32[]{:S(2)}) collective-permute-start(bf16[512,128]{1,0:T(8,128)(2,1)S(1)} %get-tuple-element.118), channel_id=1, source_target_pairs={{0,4},{1,5},{2,6},{3,7},{4,0},{5,1},{6,2},{7,3},{8,12},{9,13},{10,... | collective-permute-start | bytes 393224 | tf_op jit(solution)/shard_map/ppermute | solution.py:476
  113.9 18.5 %collective-permute-start.31 = (bf16[128,1024]{1,0:T(8,128)(2,1)S(1)}, bf16[128,1024]{1,0:T(8,128)(2,1)S(1)}, u32[]{:S(2)}, u32[]{:S(2)}) collective-permute-start(bf16[128,1024]{1,0:T(8,128)(2,1)S(1)} %get-tuple-element.139), channel_id=1, source_target_pairs={{0,16},{8,24},{16,0},{24,8},{1,17},{9,25},{17,1},{25,9},{2,18},{10... | collective-permute-start | bytes 786440 | tf_op jit(solution)/shard_map/ppermute | solution.py:591
  119.1 5.9 %collective-permute-start.24 = (bf16[512,128]{1,0:T(8,128)(2,1)S(1)}, bf16[512,128]{1,0:T(8,128)(2,1)S(1)}, u32[]{:S(2)}, u32[]{:S(2)}) collective-permute-start(bf16[512,128]{1,0:T(8,128)(2,1)S(1)} %get-tuple-element.119), channel_id=1, source_target_pairs={{0,6},{1,7},{2,4},{3,5},{4,2},{5,3},{6,0},{7,1},{8,14},{9,15},{10,... | collective-permute-start | bytes 393224 | tf_op jit(solution)/shard_map/ppermute | solution.py:476
  (7 other events, 96.8 us)

commit v5 on v4

--- a/solution.py
+++ b/solution.py
@@ -106,13 +106,15 @@
     kv_ref[i * TILE : (i + 1) * TILE, :] = act[:, VK]
 
 
-def proj_kernel(masks, pieces, last, at_ref, *refs):
+def proj_kernel(masks, pieces, last, ahead, at_ref, *refs):
     x_refs, wh_ref = refs[: sum(pieces)], refs[sum(pieces)]
     outs = refs[-5:-1] if last else refs[-4:]
+    if ahead:
+        outs[3][: ahead * TILE, :] = refs[sum(pieces) + 1][...]
     for i, mask in enumerate(masks):
         parts = [ref[...] for ref in x_refs[sum(pieces[:i]) : sum(pieces[: i + 1])]]
         x = parts[0] if len(parts) == 1 else jnp.concatenate(parts, axis=0)
-        store_rows(x, at_ref[1] ^ mask, wh_ref, *outs, i)
+        store_rows(x, at_ref[1] ^ mask, wh_ref, *outs, ahead + i)
     if last:
         refs[-1][...] = outs[1][:, Q]
 
@@ -121,15 +123,17 @@
     return [((SPAN, width), BF16), ((SPAN, 4 * HD), BF16), ((SPAN, 4 * HD), BF16), ((n * TILE, 2 * HD), BF16)]
 
 
-def project(info, masks, chunks, w, kept, last=False):
+def project(info, masks, chunks, w, kept, last=False, kv=None):
     pieces = tuple(len(chunk) for chunk in chunks)
     flat = [piece for chunk in chunks for piece in chunk]
-    start = 2 + len(flat)
+    lead = () if kv is None else (kv,)
+    ahead = 0 if kv is None else kv.shape[0] // TILE
+    start = 2 + len(flat) + len(lead)
     return call(
-        functools.partial(proj_kernel, masks, pieces, last),
+        functools.partial(proj_kernel, masks, pieces, last, ahead),
         (info[2],),
-        (*flat, w),
-        proj_outs(w.shape[0], len(masks)) + ([((SPAN, HD), BF16)] if last else []),
+        (*flat, w, *lead),
+        proj_outs(w.shape[0], ahead + len(masks)) + ([((SPAN, HD), BF16)] if last else []),
         after=kept,
         aliases={start + i: i for i in range(len(kept))},
     )
@@ -213,12 +217,12 @@
 
 
 def fwd_far_kernel(
-    lo_ref, nv_ref, at_ref, act_ref, kva_ref, kvb_ref, kvc_ref, near_ref, *refs,
+    lo_ref, nv_ref, at_ref, act_ref, kva_ref, kvb_ref, near_ref, *refs,
 ):
     dg_refs, (out_ref, kv_ref, kt_ref, sum_ref), pieces, (attn_s, dg_s) = refs[:5], refs[5:9], refs[9:14], refs[14:]
     head = at_ref[1]
     slot = 0
-    for ref in (kva_ref, kvb_ref, kvc_ref):
+    for ref in (kva_ref, kvb_ref):
         for at in range(0, ref.shape[0], TILE):
             kv_ref[rows_at(slot ^ head), :] = ref[at : at + TILE, :]
             slot += 1
@@ -416,23 +420,42 @@
     return lax.dot_general(x, w_ref[:, branch * width : (branch + 1) * width], NT, preferred_element_type=F32)
 
 
+def branches_kernel(at_ref, *refs):
+    pieces, (w_in_ref, dn_ref, row_s) = refs[:5], refs[5:]
+    dn = through(assemble(at_ref, pieces, 0, row_s), w_in_ref, 2)
+    for i, branch in ((1, 1), (2, 3)):
+        dn += through(assemble(at_ref, pieces, i, row_s), w_in_ref, branch)
+    dn_ref[...] = dn
+
+
+def own_u_kernel(tokens_ref, w_in_ref, after_ref, u_ref, slope_ref):
+    xn = norm_rows(tokens_ref[...].astype(F32)).astype(BF16)
+    pre = jnp.dot(xn, w_in_ref[:, : tokens_ref.shape[1]], preferred_element_type=F32)
+    u_ref[...], slope_ref[...] = silu_and_slope(pre)
+
+
 def rows_kernel(at_ref, *refs):
-    attn_refs, (dg_ref, tokens_ref, w_out_ref, w_in_ref, out_ref, dn_ref, row_s) = refs[:5], refs[5:]
-    width = w_out_ref.shape[0]
+    attn_refs, (dn_ref, dg_ref, u_ref, slope_ref, tokens_ref, grad_ref, w_out_ref, w_in_ref) = refs[:5], refs[5:-4]
+    out_ref, dx_ref, end_ref, row_s = refs[-4:]
+    end_ref[...] = jnp.zeros(end_ref.shape, F32)
     x = tokens_ref[...].astype(F32)
-    u, slope = silu_and_slope(jnp.dot(norm_rows(x).astype(BF16), w_in_ref[:, :width], preferred_element_type=F32))
-    n = norm_rows(assemble(at_ref, attn_refs, 0, row_s).astype(F32))
-    gated = (n * u.astype(F32)).astype(BF16)
+    attn_n = norm_rows(assemble(at_ref, attn_refs, 0, row_s).astype(F32))
+    gated = (attn_n * u_ref[...].astype(F32)).astype(BF16)
     y = jnp.dot(gated, w_out_ref[...], preferred_element_type=F32)
     out_ref[...] = (x + y).astype(BF16)
-    du = (dg_ref[...].astype(F32) * n).astype(BF16).astype(F32)
-    du = (du * slope.astype(F32)).astype(BF16)
-    dn_ref[...] = through(du, w_in_ref, 0)
-
-
-def half_kernel(later, keep_ref, got_ref, *refs):
-    refs = refs[later:]
-    half = keep_ref.shape[0] // len(refs)
+    du = (dg_ref[...].astype(F32) * attn_n).astype(BF16).astype(F32)
+    du = (du * slope_ref[...].astype(F32)).astype(BF16)
+    dn = dn_ref[...] + through(du, w_in_ref, 0)
+    r = lax.rsqrt(jnp.mean(x * x, axis=-1, keepdims=True) + eps)
+    n = x * r
+    dx = r * (dn - n * jnp.mean(dn * n, axis=-1, keepdims=True))
+    dx_ref[...] = (grad_ref[...].astype(F32) + dx).astype(BF16)
+
+
+def half_kernel(keep_ref, got_ref, *refs):
+    half = refs[-1].shape[0]
+    if half == keep_ref.shape[0]:
+        refs = refs[-1:]
     refs[0][...] = keep_ref[:half, :] + got_ref[:half, :].astype(F32)
     if len(refs) > 1:
         refs[1][...] = (keep_ref[half:, :] + got_ref[half:, :].astype(F32)).astype(BF16)
@@ -481,7 +504,7 @@
     def backward(x):
         return lax.ppermute(x, "g", [(i + 1, i) for i in range(groups - 1)])
 
-    def trade(pieces, after=(), merged=None):
+    def trade(pieces, after=()):
         mine, other, *pairs = pieces
         other = swap(other, 1)
         pairs = call(
@@ -493,8 +516,6 @@
             aliases={1: 0, 2: 1, 3: 2},
             limit=4,
         )
-        if merged is not None:
-            merged.extend(pairs)
         return [mine, other] + [swap(x, mask) for x, mask in zip(pairs, (2, 4, 6))]
 
     x_rows, y_rows = swap(tokens, 2), swap(tokens, 4)
@@ -509,32 +530,30 @@
         sems=4,
     )
     *kept, kv = project(info, (0, 1), ((tokens,), (other,)), w_head, ())
-    far_kv = [onward(kv)]
     *dg_pieces, dg_own = call(
         d_gated_kernel, info[2:], (grad_out, w_out), trade_outs(HD) + [(own, BF16)], after=(kv,)
     )
-    merged = []
-    d_gated = trade(dg_pieces, merged=merged)
     x_rows, y_rows, x_half, y_half = call(
         cut_kernel,
         (),
         (x_rows, y_rows),
         [(own, BF16), (own, BF16), (half, BF16), (half, BF16)],
-        after=(far_kv[0], merged[0]),
+        after=(kv, dg_own),
         aliases={0: 0, 1: 1},
         limit=4,
     )
     corner = swap(x_half, 4), swap(y_half, 2)
     chunks = ((x_rows,), (swap(x_rows, 1),), (y_rows,), (swap(y_rows, 1),))
-    *kept, kv = project(info, (2, 3, 4, 5), chunks, w_head, kept)
-    far_kv.append(onward(kv))
-    corner = call(gate_kernel, (), (), [(half, BF16), (half, BF16)], after=(*corner, kv, *d_gated[2:]), aliases={0: 0, 1: 1}, limit=4)
+    *kept, kv = project(info, (2, 3, 4, 5), chunks, w_head, kept, kv=kv)
+    far_kv = [onward(kv)]
+    corner = call(gate_kernel, (), (), [(half, BF16), (half, BF16)], after=(*corner, kv), aliases={0: 0, 1: 1}, limit=4)
     *kept, kv, q = project(info, (6, 7), (corner, [swap(x, 1) for x in corner]), w_head, kept, True)
     far_kv.append(onward(kv))
     q_next = backward(q)
     normed, act, slope = kept
 
     near, kt, qt, slope_qt = call(fwd_own_kernel, info[:2], (act, slope), [(tall, F32)] + [(tall_t, BF16)] * 3)
+    d_gated = trade(dg_pieces, (near,))
     attn, kv, far_kt, sums, *attn_pieces = call(
         fwd_far_kernel,
         info,
@@ -563,7 +582,6 @@
     )
     rows, cols = 4 * HD // groups, 3 * HD
     half_rows = rows * groups // 2
-    attn_rows = trade(attn_pieces, (d_q,))
     *pieces, keep, send = call(
         functools.partial(keys_kernel, groups),
         (info[0], info[2]),
@@ -572,31 +590,24 @@
         [((2 * HD, SPAN), BF16), ((4 * HD, width), BF16), (wide, F32)],
     )
     pieces = trade(pieces)
-    layer_out, d_normed = call(
-        rows_kernel,
-        info[2:],
-        (*attn_rows, dg_own, tokens, w_out, w_in),
-        [(own, BF16), (own, F32)],
-        [(own, BF16)],
-    )
-    grad_tokens, end = call(
-        last_kernel,
-        info[2:],
-        (*pieces, d_normed, tokens, grad_out, w_in),
-        [(own, BF16), ((8, HD), F32)],
-        [(own, BF16)],
-    )
-    mask = 1
+    u, slope_u = call(own_u_kernel, (), (tokens, w_in), [(own, BF16), (own, BF16)], after=(pieces[0],))
+    mask, attn_rows = 1, None
     while mask < groups:
         send = lax.ppermute(send, "g", [(i, i ^ mask) for i in range(groups)])
         mask, half_rows = 2 * mask, half_rows // 2
-        more = mask < groups
-        outs = [((half_rows, width), F32), ((half_rows, width), BF16)] if more else [((rows, width), F32)]
-        keep, *send = call(
-            functools.partial(half_kernel, 0 if more else 1), (), (keep, send), outs, after=() if more else (end,)
-        )
-        send = send[0] if send else None
-    grad_w_in = keep
+        if mask < groups:
+            keep, send = call(half_kernel, (), (keep, send), [((half_rows, width), F32), ((half_rows, width), BF16)])
+        if attn_rows is None:
+            attn_rows = trade(attn_pieces, (send,))
+    d_normed = call(branches_kernel, info[2:], (*pieces, w_in), [(own, F32)], [(own, BF16)])[0]
+    layer_out, grad_tokens, end = call(
+        rows_kernel,
+        info[2:],
+        (*attn_rows, d_normed, dg_own, u, slope_u, tokens, grad_out, w_out, w_in),
+        [(own, BF16), (own, BF16), ((8, HD), F32)],
+        [(own, BF16)],
+    )
+    grad_w_in = call(half_kernel, (), (keep, send), [((rows, width), F32)], after=(end,))[0]
     parts = groups // 4
     if parts > 1:
         perm = [

time: 135 us -> 126 us (0.933)
  waiting for transfers between devices: 44.2 us -> 30.6 us
  starting transfers between devices: 45.3 us -> 49.5 us
    ppermute x2, starting transfers between devices: 7.24 us -> 16.7 us  [per_device(): send = lax.ppermute(send, 'g', [(i, i ^ mask) for i in range(groups)])]
    ppermute x25, waiting for transfers between devices: 25 us -> 17.1 us  [swap(): return lax.ppermute(x, 'h', [(i, i ^ mask) for i in range(HEADS)])]
    ppermute x3 -> x2, waiting for transfers between devices: 6.97 us -> 0.01 us  [onward(): return lax.ppermute(x, 'g', [(i, i + 1) for i in range(groups - 1)])]
    ppermute x3 -> x2, starting transfers between devices: 12.5 us -> 7.18 us  [onward(): return lax.ppermute(x, 'g', [(i, i + 1) for i in range(groups - 1)])]
    ppermute x2, waiting for transfers between devices: 7.16 us -> 8.9 us  [per_device(): send = lax.ppermute(send, 'g', [(i, i ^ mask) for i in range(groups)])]
    pallas_call x20 -> x21, Pallas kernels: 41.4 us -> 42.3 us  [call(): pl.pallas_call(kernel, out_shape=[jax.ShapeDtypeStruct(*out) for out in o...]
  transfers between devices with their start and end apart: 32 -> 31, of which waited for: 15 -> 13; matrix products, arithmetic and copies ran while one was open for 0% -> 0% of each run, Pallas kernels for 26% -> 28%
where the time goes in v5:
time: 126 us; the launch traced here: 125 us
  starting transfers between devices  49.5 us (39%)
  Pallas kernels  42.3 us (34%)
  waiting for transfers between devices  30.6 us (24%)
  local copies, waits for them, and re-layouts  1.33 us (1%)
    pallas_call x21, Pallas kernels, call(): pl.pallas_call(kernel, out_shape=[jax.ShapeDtypeStruct(*out) for out in o...  42.3 us
    ppermute x25, starting transfers between devices, swap(): return lax.ppermute(x, 'h', [(i, i ^ mask) for i in range(HEADS)])  23 us
    ppermute x25, waiting for transfers between devices, swap(): return lax.ppermute(x, 'h', [(i, i ^ mask) for i in range(HEADS)])  17.1 us
    ppermute x2, starting transfers between devices, per_device(): send = lax.ppermute(send, 'g', [(i, i ^ mask) for i in range(groups)])  16.7 us
    ppermute x2, waiting for transfers between devices, per_device(): send = lax.ppermute(send, 'g', [(i, i ^ mask) for i in range(groups)])  8.9 us
    ppermute x2, starting transfers between devices, onward(): return lax.ppermute(x, 'g', [(i, i + 1) for i in range(groups - 1)])  7.18 us
    ppermute x2, waiting for transfers between devices, backward(): return lax.ppermute(x, 'g', [(i + 1, i) for i in range(groups - 1)])  4.63 us
    ppermute x2, starting transfers between devices, backward(): return lax.ppermute(x, 'g', [(i + 1, i) for i in range(groups - 1)])  2.58 us
  transfers between devices with their start and end apart: 31, of which 13 were waited for; matrix products, arithmetic and copies ran while one was open for 0% of the time, Pallas kernels for 28%

profile of v5, /device:TPU:0, one launch (start us, length us, event | category | flops | bytes accessed | tf_op | source)
XLA Modules:
  0.0 124.7 jit_solution(4391719899033182777)
XLA Ops:
  1.2 2.6 %collective-permute-start.1 = (bf16[256,1024]{1,0:T(8,128)(2,1)}, bf16[256,1024]{1,0:T(8,128)(2,1)S(1)}, u32[]{:S(2)}, u32[]{:S(2)}) collective-permute-start(bf16[256,1024]{1,0:T(8,128)(2,1)} %refs_9_.1), channel_id=1, source_target_pairs={{0,4},{1,5},{2,6},{3,7},{4,0},{5,1},{6,2},{7,3},{8,12},{9,13},{10,... | collective-permute-start | bytes 1572872 | tf_op jit(solution)/shard_map/ppermute | solution.py:499
  3.8 1.5 %collective-permute-start = (bf16[256,1024]{1,0:T(8,128)(2,1)}, bf16[256,1024]{1,0:T(8,128)(2,1)S(1)}, u32[]{:S(2)}, u32[]{:S(2)}) collective-permute-start(bf16[256,1024]{1,0:T(8,128)(2,1)} %refs_9_.1), channel_id=1, source_target_pairs={{0,2},{1,3},{2,0},{3,1},{4,6},{5,7},{6,4},{7,5},{8,10},{9,11},{10,... | collective-permute-start | bytes 1572872 | tf_op jit(solution)/shard_map/ppermute | solution.py:499
  6.6 2.4 %shard_map.85 = (s32[32]{0:T(128)S(1)}, s32[32]{0:T(128)S(1)}, s32[2]{0:T(128)S(1)}, bf16[1024,512]{1,0:T(8,128)(2,1)S(1)}) custom-call(s32[16]{0:T(128)S(1)} %copy-done.3, s32[16]{0:T(128)S(1)} %copy-done.4, bf16[1024,4096]{1,0:T(8,128)(2,1)} %refs_12_.1), custom_call_target="tpu_custom_call" | custom-call | tf_op jit(solution)/shard_map/pallas_call | solution.py:481
  9.0 1.7 %shard_map.86 = (bf16[2048,1024]{1,0:T(8,128)(2,1)S(1)}, bf16[2048,512]{1,0:T(8,128)(2,1)S(1)}, bf16[2048,512]{1,0:T(8,128)(2,1)S(1)}, bf16[512,256]{1,0:T(8,128)(2,1)S(1)}) custom-call(s32[2]{0:T(128)S(1)} %get-tuple-element.73.at_ref, bf16[256,1024]{1,0:T(8,128)(2,1)S(1)} %copy-done.1, bf16[256,1024]{1,0:T(8,128)(2,1)S(1)} %collective-permute-done.2.refs_1_, ...), custom_call_target="tpu_custom_call" | custom-call | tf_op jit(solution)/shard_map/pallas_call | solution.py:481
  10.7 1.4 %shard_map.87 = (bf16[256,128]{1,0:T(8,128)(2,1)S(1)}, bf16[1024,128]{1,0:T(8,128)(2,1)S(1)}, bf16[512,128]{1,0:T(8,128)(2,1)S(1)}, bf16[512,128]{1,0:T(8,128)(2...) custom-call(s32[2]{0:T(128)S(1)} %get-tuple-element.73.at_ref, bf16[256,1024]{1,0:T(8,128)(2,1)S(1)} %copy-done.2, ...), custom_call_target="tpu_custom_call" | custom-call | tf_op jit(solution)/shard_map/pallas_call | solution.py:481
  12.1 4.4 %collective-permute-done.1.y_ref = bf16[256,1024]{1,0:T(8,128)(2,1)S(1)} collective-permute-done((bf16[256,1024]{1,0:T(8,128)(2,1)}, bf16[256,1024]{1,0:T(8,128)(2,1)S(1)}, u32[]{:S(2)}, u32[]{:S(2)}) %collective-permute-start.1) | collective-permute-done | bytes 524320 | tf_op jit(solution)/shard_map/ppermute | solution.py:499
  16.5 1.5 %collective-permute-done.x_ref = bf16[256,1024]{1,0:T(8,128)(2,1)S(1)} collective-permute-done((bf16[256,1024]{1,0:T(8,128)(2,1)}, bf16[256,1024]{1,0:T(8,128)(2,1)S(1)}, u32[]{:S(2)}, u32[]{:S(2)}) %collective-permute-start) | collective-permute-done | bytes 524320 | tf_op jit(solution)/shard_map/ppermute | solution.py:499
  18.9 1.7 %collective-permute-start.4 = (bf16[128,1024]{1,0:T(8,128)(2,1)S(1)}, bf16[128,1024]{1,0:T(8,128)(2,1)S(1)}, u32[]{:S(2)}, u32[]{:S(2)}) collective-permute-start(bf16[128,1024]{1,0:T(8,128)(2,1)S(1)} %get-tuple-element.80), channel_id=1, source_target_pairs={{0,2},{1,3},{2,0},{3,1},{4,6},{5,7},{6,4},{7,5},{8,10},{9,11},{10,... | collective-permute-start | bytes 786440 | tf_op jit(solution)/shard_map/ppermute | solution.py:499
  20.7 2.6 %shard_map.89 = (bf16[2048,1024]{1,0:T(8,128)(2,1)S(1)}, bf16[2048,512]{1,0:T(8,128)(2,1)S(1)}, bf16[2048,512]{1,0:T(8,128)(2,1)S(1)}, bf16[1536,256]{1,0:T(8,128)(2,1)S(1)}) custom-call(s32[2]{0:T(128)S(1)} %get-tuple-element.73.at_ref, bf16[256,1024]{1,0:T(8,128)(2,1)S(1)} %get-tuple-element.81.refs_0_, ...), custom_call_target="tpu_custom_call", output_to_operand_aliasing={{0}: (7, {}), {1}: (8, {}), {2}: (9, {})} | custom-call | tf_op jit(solution)/shard_map/pallas_call | solution.py:481
  23.3 3.5 %collective-permute-start.9 = (bf16[1536,256]{1,0:T(8,128)(2,1)S(1)}, bf16[1536,256]{1,0:T(8,128)(2,1)S(1)}, u32[]{:S(2)}, u32[]{:S(2)}) collective-permute-start(bf16[1536,256]{1,0:T(8,128)(2,1)S(1)} %get-tuple-element.86.refs_2_), channel_id=1, source_target_pairs={{0,8},{8,16},{16,24},{1,9},{9,17},{17,25},{2,10},{10,18},{18,26},{... | collective-permute-start | bytes 2359304 | tf_op jit(solution)/shard_map/ppermute | solution.py:502
  28.9 1.8 %shard_map.91 = (bf16[2048,1024]{1,0:T(8,128)(2,1)S(1)}, bf16[2048,512]{1,0:T(8,128)(2,1)S(1)}, bf16[2048,512]{1,0:T(8,128)(2,1)S(1)}, bf16[512,256]{1,0:T(8,128)(2,1)S(1)}, bf16[2048,128]{1,0:T(8,128)(2,1)S(1)}) custom-call(s32[2]{0:T(128)S(1)} %get-tuple-element.73.at_ref, ...), custom_call_target="tpu_custom_call", output_to_operand_aliasing={{0}: (6, {}), {1}: (7, {}), {2}: (8, {})} | custom-call | tf_op jit(solution)/shard_map/pallas_call | solution.py:481
  30.7 1.3 %collective-permute-start.20 = (bf16[2048,128]{1,0:T(8,128)(2,1)S(1)}, bf16[2048,128]{1,0:T(8,128)(2,1)S(1)}, u32[]{:S(2)}, u32[]{:S(2)}) collective-permute-start(bf16[2048,128]{1,0:T(8,128)(2,1)S(1)} %get-tuple-element.114), channel_id=1, source_target_pairs={{8,0},{16,8},{24,16},{9,1},{17,9},{25,17},{10,2},{18,10},{26,18},{... | collective-permute-start | bytes 1572872 | tf_op jit(solution)/shard_map/ppermute | solution.py:505
  32.0 6.7 %shard_map.92 = (f32[2048,128]{1,0:T(8,128)S(1)}, bf16[128,2048]{1,0:T(8,128)(2,1)S(1)}, bf16[128,2048]{1,0:T(8,128)(2,1)S(1)}, bf16[128,2048]{1,0:T(8,128)(2,1)S(1)}) custom-call(s32[32]{0:T(128)S(1)} %get-tuple-element.74.lo_ref, s32[32]{0:T(128)S(1)} %get-tuple-element.75.nv_ref, bf16[2048,512]{1,0:T(8,128)(2,1)S(1)} %get-tuple-element.92.act_ref, ...), custom_call_target="tpu_custom_call" | custom-call | tf_op jit(solution)/shard_map/pallas_call | solution.py:481
  38.7 1.7 %collective-permute-start.12 = (bf16[512,128]{1,0:T(8,128)(2,1)S(1)}, bf16[512,128]{1,0:T(8,128)(2,1)S(1)}, u32[]{:S(2)}, u32[]{:S(2)}) collective-permute-start(bf16[512,128]{1,0:T(8,128)(2,1)S(1)} %get-tuple-element.101), channel_id=1, source_target_pairs={{0,2},{1,3},{2,0},{3,1},{4,6},{5,7},{6,4},{7,5},{8,10},{9,11},{10,... | collective-permute-start | bytes 393224 | tf_op jit(solution)/shard_map/ppermute | solution.py:499
  40.4 3.7 %collective-permute-start.10 = (bf16[512,256]{1,0:T(8,128)(2,1)S(1)}, bf16[512,256]{1,0:T(8,128)(2,1)S(1)}, u32[]{:S(2)}, u32[]{:S(2)}) collective-permute-start(bf16[512,256]{1,0:T(8,128)(2,1)S(1)} %get-tuple-element.93), channel_id=1, source_target_pairs={{0,8},{8,16},{16,24},{1,9},{9,17},{17,25},{2,10},{10,18},{18,26},{... | collective-permute-start | bytes 786440 | tf_op jit(solution)/shard_map/ppermute | solution.py:502
  44.1 1.6 %collective-permute-start.13 = (bf16[512,128]{1,0:T(8,128)(2,1)S(1)}, bf16[512,128]{1,0:T(8,128)(2,1)S(1)}, u32[]{:S(2)}, u32[]{:S(2)}) collective-permute-start(bf16[512,128]{1,0:T(8,128)(2,1)S(1)} %get-tuple-element.102), channel_id=1, source_target_pairs={{0,4},{1,5},{2,6},{3,7},{4,0},{5,1},{6,2},{7,3},{8,12},{9,13},{10,... | collective-permute-start | bytes 393224 | tf_op jit(solution)/shard_map/ppermute | solution.py:499
  46.9 5.0 %collective-permute-done.13.refs_3_.refs_7_ = bf16[512,128]{1,0:T(8,128)(2,1)S(1)} collective-permute-done((bf16[512,128]{1,0:T(8,128)(2,1)S(1)}, bf16[512,128]{1,0:T(8,128)(2,1)S(1)}, u32[]{:S(2)}, u32[]{:S(2)}) %collective-permute-start.13) | collective-permute-done | bytes 131104 | tf_op jit(solution)/shard_map/ppermute | solution.py:499
  54.3 1.5 %collective-permute-start.19 = (f32[16,256]{1,0:T(8,128)S(1)}, f32[16,256]{1,0:T(8,128)S(1)}, u32[]{:S(2)}, u32[]{:S(2)}) collective-permute-start(f32[16,256]{1,0:T(8,128)S(1)} %shard_map.95.refs_0_), channel_id=1, source_target_pairs={{0,6},{1,7},{2,4},{3,5},{4,2},{5,3},{6,0},{7,1},{8,14},{9,15},{10,... | collective-permute-start | bytes 49160 | tf_op jit(solution)/shard_map/ppermute | solution.py:499
  56.2 1.6 %collective-permute-start.17 = (f32[16,256]{1,0:T(8,128)S(1)}, f32[16,256]{1,0:T(8,128)S(1)}, u32[]{:S(2)}, u32[]{:S(2)}) collective-permute-start(f32[16,256]{1,0:T(8,128)S(1)} %shard_map.95.refs_0_), channel_id=1, source_target_pairs={{0,2},{1,3},{2,0},{3,1},{4,6},{5,7},{6,4},{7,5},{8,10},{9,11},{10,... | collective-permute-start | bytes 49160 | tf_op jit(solution)/shard_map/ppermute | solution.py:499
  59.9 1.8 %shard_map.96 = (bf16[2048,128]{1,0:T(8,128)(2,1)S(1)}, bf16[128,2048]{1,0:T(8,128)(2,1)S(1)}) custom-call(s32[32]{0:T(128)S(1)} %get-tuple-element.75.nv_ref, s32[2]{0:T(128)S(1)} %get-tuple-element.73.at_ref, bf16[2048,512]{1,0:T(8,128)(2,1)S(1)} %get-tuple-element.92.act_ref, bf16[2048,512]{1,0:T(8,128)(2,1)S(1)} %get-tuple-element.94.slope_ref, ...), custom_call_target="tpu_custom_call" | custom-call | tf_op jit(solution)/shard_map/pallas_call | solution.py:481
  63.0 10.1 %shard_map.97 = (bf16[128,2048]{1,0:T(8,128)(2,1)S(1)}, bf16[2048,128]{1,0:T(8,128)(2,1)S(1)}, f32[2048,256]{1,0:T(8,128)S(1)}) custom-call(s32[32]{0:T(128)S(1)} %get-tuple-element.74.lo_ref, bf16[2048,512]{1,0:T(8,128)(2,1)S(1)} %get-tuple-element.92.act_ref, bf16[128,2048]{1,0:T(8,128)(2,1)S(1)} %get-tuple-element.109.slope_qt_ref, ...), custom_call_target="tpu_custom_call" | custom-call | tf_op jit(solution)/shard_map/pallas_call | solution.py:481
  73.1 4.6 %collective-permute-done.21.g_ref = bf16[2048,128]{1,0:T(8,128)(2,1)S(1)} collective-permute-done((bf16[2048,128]{1,0:T(8,128)(2,1)S(1)}, bf16[2048,128]{1,0:T(8,128)(2,1)S(1)}, u32[]{:S(2)}, u32[]{:S(2)}) %collective-permute-start.21) | collective-permute-done | bytes 524320 | tf_op jit(solution)/shard_map/ppermute | solution.py:505
  77.7 4.5 %shard_map.98 = (bf16[256,384]{1,0:T(8,128)(2,1)S(1)}, bf16[1024,384]{1,0:T(8,128)(2,1)S(1)}, bf16[512,384]{1,0:T(8,128)(2,1)S(1)}, bf16[512,384]{1,0:T(8,128)(2...) custom-call(s32[32]{0:T(128)S(1)} %get-tuple-element.74.lo_ref, ...), custom_call_target="tpu_custom_call" | custom-call | tf_op jit(solution)/shard_map/pallas_call | solution.py:481
  82.3 4.0 %collective-permute-start.22 = (bf16[256,1024]{1,0:T(8,128)(2,1)S(1)}, bf16[256,1024]{1,0:T(8,128)(2,1)S(1)}, u32[]{:S(2)}, u32[]{:S(2)}) collective-permute-start(bf16[256,1024]{1,0:T(8,128)(2,1)S(1)} %get-tuple-element.124), channel_id=1, source_target_pairs={{0,8},{8,0},{16,24},{24,16},{1,9},{9,1},{17,25},{25,17},{2,10},{10... | collective-permute-start | bytes 1572872 | tf_op jit(solution)/shard_map/ppermute | solution.py:596
  87.6 1.6 %collective-permute-start.28 = (bf16[512,384]{1,0:T(8,128)(2,1)S(1)}, bf16[512,384]{1,0:T(8,128)(2,1)S(1)}, u32[]{:S(2)}, u32[]{:S(2)}) collective-permute-start(bf16[512,384]{1,0:T(8,128)(2,1)S(1)} %get-tuple-element.135), channel_id=1, source_target_pairs={{0,4},{1,5},{2,6},{3,7},{4,0},{5,1},{6,2},{7,3},{8,12},{9,13},{10,... | collective-permute-start | bytes 1179656 | tf_op jit(solution)/shard_map/ppermute | solution.py:499
  90.0 8.9 %collective-permute-done.22.got_ref = bf16[256,1024]{1,0:T(8,128)(2,1)S(1)} collective-permute-done((bf16[256,1024]{1,0:T(8,128)(2,1)S(1)}, bf16[256,1024]{1,0:T(8,128)(2,1)S(1)}, u32[]{:S(2)}, u32[]{:S(2)}) %collective-permute-start.22) | collective-permute-done | bytes 524320 | tf_op jit(solution)/shard_map/ppermute | solution.py:596
  99.0 12.7 %collective-permute-start.30 = (bf16[128,1024]{1,0:T(8,128)(2,1)S(1)}, bf16[128,1024]{1,0:T(8,128)(2,1)S(1)}, u32[]{:S(2)}, u32[]{:S(2)}) collective-permute-start(bf16[128,1024]{1,0:T(8,128)(2,1)S(1)} %get-tuple-element.125.refs_3_), channel_id=1, source_target_pairs={{0,16},{8,24},{16,0},{24,8},{1,17},{9,25},{17,1},{25,9},{2,18},{10... | collective-permute-start | bytes 786440 | tf_op jit(solution)/shard_map/ppermute | solution.py:596
  112.3 1.5 %collective-permute-start.24 = (bf16[512,128]{1,0:T(8,128)(2,1)S(1)}, bf16[512,128]{1,0:T(8,128)(2,1)S(1)}, u32[]{:S(2)}, u32[]{:S(2)}) collective-permute-start(bf16[512,128]{1,0:T(8,128)(2,1)S(1)} %get-tuple-element.127), channel_id=1, source_target_pairs={{0,4},{1,5},{2,6},{3,7},{4,0},{5,1},{6,2},{7,3},{8,12},{9,13},{10,... | collective-permute-start | bytes 393224 | tf_op jit(solution)/shard_map/ppermute | solution.py:499
  113.9 1.4 %collective-permute-start.25 = (bf16[512,128]{1,0:T(8,128)(2,1)S(1)}, bf16[512,128]{1,0:T(8,128)(2,1)S(1)}, u32[]{:S(2)}, u32[]{:S(2)}) collective-permute-start(bf16[512,128]{1,0:T(8,128)(2,1)S(1)} %get-tuple-element.128), channel_id=1, source_target_pairs={{0,6},{1,7},{2,4},{3,5},{4,2},{5,3},{6,0},{7,1},{8,14},{9,15},{10,... | collective-permute-start | bytes 393224 | tf_op jit(solution)/shard_map/ppermute | solution.py:499
  116.4 2.7 %shard_map.102.refs_5_ = f32[256,1024]{1,0:T(8,128)S(1)} custom-call(s32[2]{0:T(128)S(1)} %get-tuple-element.73.at_ref, bf16[256,384]{1,0:T(8,128)(2,1)S(1)} %get-tuple-element.129.refs_0_.after_ref, bf16[1024,384]{1,0:T(8,128)(2,1)S(1)} %collective-permute-done.26.other_ref.refs_1_, bf16[512,384]{1,0:T(8,128)(2,1)S(1)} %collective-permute-done.27.refs_2_, ...), custom_call_target="tpu_custom_call" | custom-call | tf_op jit(solution)/shard_map/pallas_call | solution.py:481
  119.1 1.4 %collective-permute-done.25.refs_4_ = bf16[512,128]{1,0:T(8,128)(2,1)S(1)} collective-permute-done((bf16[512,128]{1,0:T(8,128)(2,1)S(1)}, bf16[512,128]{1,0:T(8,128)(2,1)S(1)}, u32[]{:S(2)}, u32[]{:S(2)}) %collective-permute-start.25) | collective-permute-done | bytes 131104 | tf_op jit(solution)/shard_map/ppermute | solution.py:499
  120.5 3.3 %shard_map.104 = (bf16[256,1024]{1,0:T(8,128)(2,1)}, bf16[256,1024]{1,0:T(8,128)(2,1)}, f32[8,128]{1,0:T(8,128)S(1)}) custom-call(s32[2]{0:T(128)S(1)} %get-tuple-element.73.at_ref, bf16[256,128]{1,0:T(8,128)(2,1)S(1)} %get-tuple-element.104.refs_0_, bf16[1024,128]{1,0:T(8,128)(2,1)S(1)} %collective-permute-done.15.other_ref.refs_1_, ...), custom_call_target="tpu_custom_call" | custom-call | tf_op jit(solution)/shard_map/pallas_call | solution.py:481
  (66 shorter events, 17.1 us)
Async XLA Ops:
  0.6 8.3 %collective-permute-start.2 = (bf16[256,1024]{1,0:T(8,128)(2,1)}, bf16[256,1024]{1,0:T(8,128)(2,1)S(1)}, u32[]{:S(2)}, u32[]{:S(2)}) collective-permute-start(bf16[256,1024]{1,0:T(8,128)(2,1)} %refs_9_.1), channel_id=1, source_target_pairs={{0,1},{1,0},{2,3},{3,2},{4,5},{5,4},{6,7},{7,6},{8,9},{9,8},{10,11... | collective-permute-start | bytes 1572872 | tf_op jit(solution)/shard_map/ppermute | solution.py:499
  1.2 15.3 %collective-permute-start.1 = (bf16[256,1024]{1,0:T(8,128)(2,1)}, bf16[256,1024]{1,0:T(8,128)(2,1)S(1)}, u32[]{:S(2)}, u32[]{:S(2)}) collective-permute-start(bf16[256,1024]{1,0:T(8,128)(2,1)} %refs_9_.1), channel_id=1, source_target_pairs={{0,4},{1,5},{2,6},{3,7},{4,0},{5,1},{6,2},{7,3},{8,12},{9,13},{10,... | collective-permute-start | bytes 1572872 | tf_op jit(solution)/shard_map/ppermute | solution.py:499
  3.8 14.2 %collective-permute-start = (bf16[256,1024]{1,0:T(8,128)(2,1)}, bf16[256,1024]{1,0:T(8,128)(2,1)S(1)}, u32[]{:S(2)}, u32[]{:S(2)}) collective-permute-start(bf16[256,1024]{1,0:T(8,128)(2,1)} %refs_9_.1), channel_id=1, source_target_pairs={{0,2},{1,3},{2,0},{3,1},{4,6},{5,7},{6,4},{7,5},{8,10},{9,11},{10,... | collective-permute-start | bytes 1572872 | tf_op jit(solution)/shard_map/ppermute | solution.py:499
  18.0 2.6 %collective-permute-start.5 = (bf16[256,1024]{1,0:T(8,128)(2,1)S(1)}, bf16[256,1024]{1,0:T(8,128)(2,1)S(1)}, u32[]{:S(2)}, u32[]{:S(2)}) collective-permute-start(bf16[256,1024]{1,0:T(8,128)(2,1)S(1)} %get-tuple-element.81.refs_0_), channel_id=1, source_target_pairs={{0,1},{1,0},{2,3},{3,2},{4,5},{5,4},{6,7},{7,6},{8,9},{9,8},{10,11... | collective-permute-start | bytes 1572872 | tf_op jit(solution)/shard_map/ppermute | solution.py:499
  18.1 2.6 %collective-permute-start.6 = (bf16[256,1024]{1,0:T(8,128)(2,1)S(1)}, bf16[256,1024]{1,0:T(8,128)(2,1)S(1)}, u32[]{:S(2)}, u32[]{:S(2)}) collective-permute-start(bf16[256,1024]{1,0:T(8,128)(2,1)S(1)} %get-tuple-element.82.refs_2_), channel_id=1, source_target_pairs={{0,1},{1,0},{2,3},{3,2},{4,5},{5,4},{6,7},{7,6},{8,9},{9,8},{10,11... | collective-permute-start | bytes 1572872 | tf_op jit(solution)/shard_map/ppermute | solution.py:499
  18.6 8.3 %collective-permute-start.3 = (bf16[128,1024]{1,0:T(8,128)(2,1)S(1)}, bf16[128,1024]{1,0:T(8,128)(2,1)S(1)}, u32[]{:S(2)}, u32[]{:S(2)}) collective-permute-start(bf16[128,1024]{1,0:T(8,128)(2,1)S(1)} %get-tuple-element.79), channel_id=1, source_target_pairs={{0,4},{1,5},{2,6},{3,7},{4,0},{5,1},{6,2},{7,3},{8,12},{9,13},{10,... | collective-permute-start | bytes 786440 | tf_op jit(solution)/shard_map/ppermute | solution.py:499
  18.9 8.0 %collective-permute-start.4 = (bf16[128,1024]{1,0:T(8,128)(2,1)S(1)}, bf16[128,1024]{1,0:T(8,128)(2,1)S(1)}, u32[]{:S(2)}, u32[]{:S(2)}) collective-permute-start(bf16[128,1024]{1,0:T(8,128)(2,1)S(1)} %get-tuple-element.80), channel_id=1, source_target_pairs={{0,2},{1,3},{2,0},{3,1},{4,6},{5,7},{6,4},{7,5},{8,10},{9,11},{10,... | collective-permute-start | bytes 786440 | tf_op jit(solution)/shard_map/ppermute | solution.py:499
  23.3 28.6 %collective-permute-start.9 = (bf16[1536,256]{1,0:T(8,128)(2,1)S(1)}, bf16[1536,256]{1,0:T(8,128)(2,1)S(1)}, u32[]{:S(2)}, u32[]{:S(2)}) collective-permute-start(bf16[1536,256]{1,0:T(8,128)(2,1)S(1)} %get-tuple-element.86.refs_2_), channel_id=1, source_target_pairs={{0,8},{8,16},{16,24},{1,9},{9,17},{17,25},{2,10},{10,18},{18,26},{... | collective-permute-start | bytes 2359304 | tf_op jit(solution)/shard_map/ppermute | solution.py:502
  26.9 1.6 %collective-permute-start.7 = (bf16[128,1024]{1,0:T(8,128)(2,1)S(1)}, bf16[128,1024]{1,0:T(8,128)(2,1)S(1)}, u32[]{:S(2)}, u32[]{:S(2)}) collective-permute-start(bf16[128,1024]{1,0:T(8,128)(2,1)S(1)} %get-tuple-element.87.refs_0_), channel_id=1, source_target_pairs={{0,1},{1,0},{2,3},{3,2},{4,5},{5,4},{6,7},{7,6},{8,9},{9,8},{10,11... | collective-permute-start | bytes 786440 | tf_op jit(solution)/shard_map/ppermute | solution.py:499
  27.0 1.9 %collective-permute-start.8 = (bf16[128,1024]{1,0:T(8,128)(2,1)S(1)}, bf16[128,1024]{1,0:T(8,128)(2,1)S(1)}, u32[]{:S(2)}, u32[]{:S(2)}) collective-permute-start(bf16[128,1024]{1,0:T(8,128)(2,1)S(1)} %get-tuple-element.88.refs_1_), channel_id=1, source_target_pairs={{0,1},{1,0},{2,3},{3,2},{4,5},{5,4},{6,7},{7,6},{8,9},{9,8},{10,11... | collective-permute-start | bytes 786440 | tf_op jit(solution)/shard_map/ppermute | solution.py:499
  27.5 11.2 %collective-permute-start.11 = (bf16[1024,128]{1,0:T(8,128)(2,1)S(1)}, bf16[1024,128]{1,0:T(8,128)(2,1)S(1)}, u32[]{:S(2)}, u32[]{:S(2)}) collective-permute-start(bf16[1024,128]{1,0:T(8,128)(2,1)S(1)} %get-tuple-element.97), channel_id=1, source_target_pairs={{0,1},{1,0},{2,3},{3,2},{4,5},{5,4},{6,7},{7,6},{8,9},{9,8},{10,11... | collective-permute-start | bytes 786440 | tf_op jit(solution)/shard_map/ppermute | solution.py:499
  30.7 27.1 %collective-permute-start.20 = (bf16[2048,128]{1,0:T(8,128)(2,1)S(1)}, bf16[2048,128]{1,0:T(8,128)(2,1)S(1)}, u32[]{:S(2)}, u32[]{:S(2)}) collective-permute-start(bf16[2048,128]{1,0:T(8,128)(2,1)S(1)} %get-tuple-element.114), channel_id=1, source_target_pairs={{8,0},{16,8},{24,16},{9,1},{17,9},{25,17},{10,2},{18,10},{26,18},{... | collective-permute-start | bytes 1572872 | tf_op jit(solution)/shard_map/ppermute | solution.py:505
  38.7 6.9 %collective-permute-start.12 = (bf16[512,128]{1,0:T(8,128)(2,1)S(1)}, bf16[512,128]{1,0:T(8,128)(2,1)S(1)}, u32[]{:S(2)}, u32[]{:S(2)}) collective-permute-start(bf16[512,128]{1,0:T(8,128)(2,1)S(1)} %get-tuple-element.101), channel_id=1, source_target_pairs={{0,2},{1,3},{2,0},{3,1},{4,6},{5,7},{6,4},{7,5},{8,10},{9,11},{10,... | collective-permute-start | bytes 393224 | tf_op jit(solution)/shard_map/ppermute | solution.py:499
  40.4 11.5 %collective-permute-start.10 = (bf16[512,256]{1,0:T(8,128)(2,1)S(1)}, bf16[512,256]{1,0:T(8,128)(2,1)S(1)}, u32[]{:S(2)}, u32[]{:S(2)}) collective-permute-start(bf16[512,256]{1,0:T(8,128)(2,1)S(1)} %get-tuple-element.93), channel_id=1, source_target_pairs={{0,8},{8,16},{16,24},{1,9},{9,17},{17,25},{2,10},{10,18},{18,26},{... | collective-permute-start | bytes 786440 | tf_op jit(solution)/shard_map/ppermute | solution.py:502
  44.1 7.8 %collective-permute-start.13 = (bf16[512,128]{1,0:T(8,128)(2,1)S(1)}, bf16[512,128]{1,0:T(8,128)(2,1)S(1)}, u32[]{:S(2)}, u32[]{:S(2)}) collective-permute-start(bf16[512,128]{1,0:T(8,128)(2,1)S(1)} %get-tuple-element.102), channel_id=1, source_target_pairs={{0,4},{1,5},{2,6},{3,7},{4,0},{5,1},{6,2},{7,3},{8,12},{9,13},{10,... | collective-permute-start | bytes 393224 | tf_op jit(solution)/shard_map/ppermute | solution.py:499
  45.6 6.3 %collective-permute-start.14 = (bf16[512,128]{1,0:T(8,128)(2,1)S(1)}, bf16[512,128]{1,0:T(8,128)(2,1)S(1)}, u32[]{:S(2)}, u32[]{:S(2)}) collective-permute-start(bf16[512,128]{1,0:T(8,128)(2,1)S(1)} %get-tuple-element.103), channel_id=1, source_target_pairs={{0,6},{1,7},{2,4},{3,5},{4,2},{5,3},{6,0},{7,1},{8,14},{9,15},{10,... | collective-permute-start | bytes 393224 | tf_op jit(solution)/shard_map/ppermute | solution.py:499
  53.1 1.2 collective-permute-start.16
  54.3 4.6 %collective-permute-start.19 = (f32[16,256]{1,0:T(8,128)S(1)}, f32[16,256]{1,0:T(8,128)S(1)}, u32[]{:S(2)}, u32[]{:S(2)}) collective-permute-start(f32[16,256]{1,0:T(8,128)S(1)} %shard_map.95.refs_0_), channel_id=1, source_target_pairs={{0,6},{1,7},{2,4},{3,5},{4,2},{5,3},{6,0},{7,1},{8,14},{9,15},{10,... | collective-permute-start | bytes 49160 | tf_op jit(solution)/shard_map/ppermute | solution.py:499
  55.8 3.7 %collective-permute-start.18 = (f32[16,256]{1,0:T(8,128)S(1)}, f32[16,256]{1,0:T(8,128)S(1)}, u32[]{:S(2)}, u32[]{:S(2)}) collective-permute-start(f32[16,256]{1,0:T(8,128)S(1)} %shard_map.95.refs_0_), channel_id=1, source_target_pairs={{0,4},{1,5},{2,6},{3,7},{4,0},{5,1},{6,2},{7,3},{8,12},{9,13},{10,... | collective-permute-start | bytes 49160 | tf_op jit(solution)/shard_map/ppermute | solution.py:499
  56.2 3.7 %collective-permute-start.17 = (f32[16,256]{1,0:T(8,128)S(1)}, f32[16,256]{1,0:T(8,128)S(1)}, u32[]{:S(2)}, u32[]{:S(2)}) collective-permute-start(f32[16,256]{1,0:T(8,128)S(1)} %shard_map.95.refs_0_), channel_id=1, source_target_pairs={{0,2},{1,3},{2,0},{3,1},{4,6},{5,7},{6,4},{7,5},{8,10},{9,11},{10,... | collective-permute-start | bytes 49160 | tf_op jit(solution)/shard_map/ppermute | solution.py:499
  61.7 16.0 %collective-permute-start.21 = (bf16[2048,128]{1,0:T(8,128)(2,1)S(1)}, bf16[2048,128]{1,0:T(8,128)(2,1)S(1)}, u32[]{:S(2)}, u32[]{:S(2)}) collective-permute-start(bf16[2048,128]{1,0:T(8,128)(2,1)S(1)} %get-tuple-element.115.g_ref), channel_id=1, source_target_pairs={{8,0},{16,8},{24,16},{9,1},{17,9},{25,17},{10,2},{18,10},{26,18},{... | collective-permute-start | bytes 1572872 | tf_op jit(solution)/shard_map/ppermute | solution.py:505
  77.7 37.5 %slice-start.1 = ((s8[8388608]{0:T(1024)(128)(4,1)}), s8[4194304]{0:T(1024)(128)(4,1)S(1)}, s32[]{:S(2)}) async-start(s8[8388608]{0:T(1024)(128)(4,1)} %bitcast), calls=%async_computation.1 | async-start | bytes 8388608
  82.3 4.1 %collective-permute-start.26 = (bf16[1024,384]{1,0:T(8,128)(2,1)S(1)}, bf16[1024,384]{1,0:T(8,128)(2,1)S(1)}, u32[]{:S(2)}, u32[]{:S(2)}) collective-permute-start(bf16[1024,384]{1,0:T(8,128)(2,1)S(1)} %get-tuple-element.130), channel_id=1, source_target_pairs={{0,1},{1,0},{2,3},{3,2},{4,5},{5,4},{6,7},{7,6},{8,9},{9,8},{10,11... | collective-permute-start | bytes 2359304 | tf_op jit(solution)/shard_map/ppermute | solution.py:499
  82.3 16.6 %collective-permute-start.22 = (bf16[256,1024]{1,0:T(8,128)(2,1)S(1)}, bf16[256,1024]{1,0:T(8,128)(2,1)S(1)}, u32[]{:S(2)}, u32[]{:S(2)}) collective-permute-start(bf16[256,1024]{1,0:T(8,128)(2,1)S(1)} %get-tuple-element.124), channel_id=1, source_target_pairs={{0,8},{8,0},{16,24},{24,16},{1,9},{9,1},{17,25},{25,17},{2,10},{10... | collective-permute-start | bytes 1572872 | tf_op jit(solution)/shard_map/ppermute | solution.py:596
  86.4 25.9 %collective-permute-start.27 = (bf16[512,384]{1,0:T(8,128)(2,1)S(1)}, bf16[512,384]{1,0:T(8,128)(2,1)S(1)}, u32[]{:S(2)}, u32[]{:S(2)}) collective-permute-start(bf16[512,384]{1,0:T(8,128)(2,1)S(1)} %get-tuple-element.134), channel_id=1, source_target_pairs={{0,2},{1,3},{2,0},{3,1},{4,6},{5,7},{6,4},{7,5},{8,10},{9,11},{10,... | collective-permute-start | bytes 1179656 | tf_op jit(solution)/shard_map/ppermute | solution.py:499
  87.6 26.3 %collective-permute-start.28 = (bf16[512,384]{1,0:T(8,128)(2,1)S(1)}, bf16[512,384]{1,0:T(8,128)(2,1)S(1)}, u32[]{:S(2)}, u32[]{:S(2)}) collective-permute-start(bf16[512,384]{1,0:T(8,128)(2,1)S(1)} %get-tuple-element.135), channel_id=1, source_target_pairs={{0,4},{1,5},{2,6},{3,7},{4,0},{5,1},{6,2},{7,3},{8,12},{9,13},{10,... | collective-permute-start | bytes 1179656 | tf_op jit(solution)/shard_map/ppermute | solution.py:499
  89.1 22.6 %collective-permute-start.15 = (bf16[1024,128]{1,0:T(8,128)(2,1)S(1)}, bf16[1024,128]{1,0:T(8,128)(2,1)S(1)}, u32[]{:S(2)}, u32[]{:S(2)}) collective-permute-start(bf16[1024,128]{1,0:T(8,128)(2,1)S(1)} %get-tuple-element.105), channel_id=1, source_target_pairs={{0,1},{1,0},{2,3},{3,2},{4,5},{5,4},{6,7},{7,6},{8,9},{9,8},{10,11... | collective-permute-start | bytes 786440 | tf_op jit(solution)/shard_map/ppermute | solution.py:499
  89.1 27.2 %collective-permute-start.29 = (bf16[512,384]{1,0:T(8,128)(2,1)S(1)}, bf16[512,384]{1,0:T(8,128)(2,1)S(1)}, u32[]{:S(2)}, u32[]{:S(2)}) collective-permute-start(bf16[512,384]{1,0:T(8,128)(2,1)S(1)} %get-tuple-element.136), channel_id=1, source_target_pairs={{0,6},{1,7},{2,4},{3,5},{4,2},{5,3},{6,0},{7,1},{8,14},{9,15},{10,... | collective-permute-start | bytes 1179656 | tf_op jit(solution)/shard_map/ppermute | solution.py:499
  99.0 24.9 %collective-permute-start.30 = (bf16[128,1024]{1,0:T(8,128)(2,1)S(1)}, bf16[128,1024]{1,0:T(8,128)(2,1)S(1)}, u32[]{:S(2)}, u32[]{:S(2)}) collective-permute-start(bf16[128,1024]{1,0:T(8,128)(2,1)S(1)} %get-tuple-element.125.refs_3_), channel_id=1, source_target_pairs={{0,16},{8,24},{16,0},{24,8},{1,17},{9,25},{17,1},{25,9},{2,18},{10... | collective-permute-start | bytes 786440 | tf_op jit(solution)/shard_map/ppermute | solution.py:596
  111.7 7.4 %collective-permute-start.23 = (bf16[512,128]{1,0:T(8,128)(2,1)S(1)}, bf16[512,128]{1,0:T(8,128)(2,1)S(1)}, u32[]{:S(2)}, u32[]{:S(2)}) collective-permute-start(bf16[512,128]{1,0:T(8,128)(2,1)S(1)} %get-tuple-element.126), channel_id=1, source_target_pairs={{0,2},{1,3},{2,0},{3,1},{4,6},{5,7},{6,4},{7,5},{8,10},{9,11},{10,... | collective-permute-start | bytes 393224 | tf_op jit(solution)/shard_map/ppermute | solution.py:499
  112.3 6.8 %collective-permute-start.24 = (bf16[512,128]{1,0:T(8,128)(2,1)S(1)}, bf16[512,128]{1,0:T(8,128)(2,1)S(1)}, u32[]{:S(2)}, u32[]{:S(2)}) collective-permute-start(bf16[512,128]{1,0:T(8,128)(2,1)S(1)} %get-tuple-element.127), channel_id=1, source_target_pairs={{0,4},{1,5},{2,6},{3,7},{4,0},{5,1},{6,2},{7,3},{8,12},{9,13},{10,... | collective-permute-start | bytes 393224 | tf_op jit(solution)/shard_map/ppermute | solution.py:499
  113.9 6.6 %collective-permute-start.25 = (bf16[512,128]{1,0:T(8,128)(2,1)S(1)}, bf16[512,128]{1,0:T(8,128)(2,1)S(1)}, u32[]{:S(2)}, u32[]{:S(2)}) collective-permute-start(bf16[512,128]{1,0:T(8,128)(2,1)S(1)} %get-tuple-element.128), channel_id=1, source_target_pairs={{0,6},{1,7},{2,4},{3,5},{4,2},{5,3},{6,0},{7,1},{8,14},{9,15},{10,... | collective-permute-start | bytes 393224 | tf_op jit(solution)/shard_map/ppermute | solution.py:499
  (6 other events, 53.0 us)
